TPU v7x, 32 devices: a whole 2x2x4 slice. The times are simulated.
32 devices in a mesh: dp: 8 (over z, y), mp: 4 (over x, core).
Axes of the slice: x: 2, y: 2, z: 4, core: 2. Of those that a mesh axis runs over, the one named last changes fastest.
Arguments:
- tokens_in: bfloat16 [1024, 1536], P('dp'), may hold values from -6 to 6
- text_feats: bfloat16 [8, 4, 32, 4096], P('dp'), may hold values from -6 to 6
- frame_counts: int32 [8, 4], P('dp'), may hold values from 0 to 16, as said below
- time_steps: int32 [8, 4], P('dp'), may hold values from 0 to 999
- attn_master: float32 [4, 7079424], P('mp', 'dp'), may hold values from -8 to 8
- attn_first: float32 [4, 7079424], P('mp', 'dp'), may hold values from -21.12 to 21.12
- attn_second: float32 [4, 7079424], P('mp', 'dp'), may hold values from 51.2 to 204.8
- ffn_master: float32 [4, 4718592], P('mp', 'dp'), may hold values from -0.15625 to 0.15625
- ffn_first: float32 [4, 4718592], P('mp', 'dp'), may hold values from -21.12 to 21.12
- ffn_second: float32 [4, 4718592], P('mp', 'dp'), may hold values from 51.2 to 204.8
- norm_master: float32 [6144], P('dp'), may hold values from 0.5 to 1.5
- norm_first: float32 [6144], P('dp'), may hold values from -21.12 to 21.12
- norm_second: float32 [6144], P('dp'), may hold values from 51.2 to 204.8
- step_count: int32 [1], replicated, may hold values from 1 to 3
- cotangent: bfloat16 [1024, 1536], P('dp'), may hold values from -6 to 6
Outputs:
- output: bfloat16 [1024, 1536], P('dp')
- input_grad: bfloat16 [1024, 1536], P('dp')
- attn_new: float32 [4, 7079424], P('mp', 'dp')
- attn_first_new: float32 [4, 7079424], P('mp', 'dp')
- attn_second_new: float32 [4, 7079424], P('mp', 'dp')
- attn_grad: float32 [4, 7079424], P('mp', 'dp')
- attn_copy: bfloat16 [4, 7079424], P('mp', 'dp')
- ffn_new: float32 [4, 4718592], P('mp', 'dp')
- ffn_first_new: float32 [4, 4718592], P('mp', 'dp')
- ffn_second_new: float32 [4, 4718592], P('mp', 'dp')
- ffn_grad: float32 [4, 4718592], P('mp', 'dp')
- ffn_copy: bfloat16 [4, 4718592], P('mp', 'dp')
- norm_new: float32 [6144], P('dp')
- norm_first_new: float32 [6144], P('dp')
- norm_second_new: float32 [6144], P('dp')
- norm_grad: float32 [6144], P('dp')
- norm_copy: bfloat16 [6144], P('dp')
- gate_grads: float32 [8, 1536], P('dp', 'mp')
Inputs may be any that keep to these rules, and one draw needn't show every extreme that they name: `frame_counts`: A slot holds 0 or 4 to 16 frames; a pack's frames add up to at most 16; empty slots come after the used ones, and slot 0 is used.
All inputs are finite; a program needn't handle non-finite values.
Results may differ from a plain program's by a relative error of at most 0.02.
Values may be sent and summed in bfloat16 or wider, within the bound.
No kernel may reach another device: no remote copies, remote signals or barrier semaphores. Data moves between devices by JAX's collectives and lax.ppermute only.
A program may use at most 384 MiB of HBM per device.

v0:
```python
import math

import jax
import jax.numpy as jnp
from jax import lax
from jax.sharding import PartitionSpec as P

HEAD_DIM = 64
COND = 1024
FRAME_TOK = 8


EPS = 1e-06
NEG = -1e30
BETA_ONE = 0.9
BETA_TWO = 0.95
RATE = 0.03
RATE_NORM = 0.3
DECAY = 0.1
ADAM_EPS = 1e-08


def rms_norm(values):
    return values * lax.rsqrt(jnp.mean(values * values, -1, keepdims=True) + EPS)


def rope_tables(positions, head_size):
    half_size = head_size // 2
    frequency = jnp.exp(
        -jnp.log(10000.0) * 2.0 * jnp.arange(half_size, dtype=jnp.float32) / head_size
    )
    angles = positions.astype(jnp.float32)[:, None] * frequency[None, :]
    cosine = jnp.cos(angles)
    sine_table = jnp.sin(angles)
    return (jnp.concatenate([cosine, cosine], -1), jnp.concatenate([sine_table, sine_table], -1))


def rotate(values, cosine, sine_table):
    half_size = values.shape[-1] // 2
    turned = jnp.concatenate([-values[..., half_size:], values[..., :half_size]], -1)
    return values * cosine[:, None, :] + turned * sine_table[:, None, :]


def clip_layout(frames_row, length, frame_tok, clip_slots):
    clip_len = frames_row * frame_tok
    clip_end = jnp.cumsum(clip_len)
    clip_start = clip_end - clip_len
    row_index = jnp.arange(length, dtype=jnp.int32)
    segment = jnp.sum(
        (row_index[:, None] >= clip_end[None, :]).astype(jnp.int32), 1, dtype=jnp.int32
    )
    member = segment[:, None] == jnp.arange(clip_slots, dtype=jnp.int32)[None, :]
    begin_row = jnp.sum(jnp.where(member, clip_start[None, :], 0), 1, dtype=jnp.int32)
    begin_row = begin_row + jnp.where(segment == clip_slots, clip_end[clip_slots - 1], 0)
    return (segment, member.astype(jnp.float32), row_index - begin_row)


def condition(steps_row, cond_width):
    half_size = cond_width // 2
    frequency = jnp.exp(-jnp.log(10000.0) * jnp.arange(half_size, dtype=jnp.float32) / half_size)
    angles = steps_row.astype(jnp.float32)[:, None] * frequency[None, :]
    return jax.nn.silu(jnp.concatenate([jnp.cos(angles), jnp.sin(angles)], -1))


def split_flat(flat_row, shapes):
    result = []
    offset = 0
    for piece_shape in shapes:
        piece_size = math.prod(piece_shape)
        result.append(lax.slice_in_dim(flat_row, offset, offset + piece_size).reshape(piece_shape))
        offset += piece_size
    return result


def modulate(values, gain, scale_tok):
    return rms_norm(values) * gain * (1.0 + scale_tok)


def branch_add(base, branch, gate_tok, gain):
    return base + jnp.tanh(gate_tok) * rms_norm(branch) * gain


def swiglu(gate_lin, up_lin):
    return jax.nn.silu(gate_lin) * up_lin


def attend(query, keys, values, mask):
    scores = jnp.dot(query, keys.T, preferred_element_type=jnp.float32) * HEAD_DIM ** (-0.5)
    scores = jnp.where(mask, scores, NEG)
    top_score = jnp.max(scores, -1, keepdims=True)
    raised = jnp.exp(scores - top_score)
    row_total = jnp.sum(raised, -1, keepdims=True)
    weights = (raised / row_total).astype(jnp.bfloat16)
    return (
        jnp.dot(weights, values, preferred_element_type=jnp.float32),
        top_score + jnp.log(row_total),
    )


def attend_back(query, keys, values, mask, log_total, grad_out):
    scores = jnp.dot(query, keys.T, preferred_element_type=jnp.float32) * HEAD_DIM ** (-0.5)
    scores = jnp.where(mask, scores, NEG)
    probabilities = jnp.exp(scores - log_total)
    grad_probs = jnp.dot(grad_out, values.T, preferred_element_type=jnp.float32)
    grad_values = jnp.dot(
        probabilities.astype(jnp.bfloat16).T, grad_out, preferred_element_type=jnp.float32
    )
    inner_sum = jnp.sum(probabilities * grad_probs, -1, keepdims=True)
    grad_scores = (probabilities * (grad_probs - inner_sum) * HEAD_DIM ** (-0.5)).astype(
        jnp.bfloat16
    )
    grad_query = jnp.dot(grad_scores, keys, preferred_element_type=jnp.float32)
    grad_keys = jnp.dot(grad_scores.T, query, preferred_element_type=jnp.float32)
    return (grad_query, grad_keys, grad_values)


def adamw(master, first, second, gradient, step_value, rate):
    first_new = BETA_ONE * first + (1.0 - BETA_ONE) * gradient
    second_new = BETA_TWO * second + (1.0 - BETA_TWO) * gradient * gradient
    first_fix = 1.0 - jnp.power(BETA_ONE, step_value)
    second_fix = 1.0 - jnp.power(BETA_TWO, step_value)
    update = rate * (
        first_new / first_fix / (jnp.sqrt(second_new / second_fix) + ADAM_EPS) + DECAY * master
    )
    master_new = master - update
    return (master_new, first_new, second_new, gradient, master_new.astype(jnp.bfloat16))


def local(
    tokens_in,
    text_feats,
    frame_counts,
    time_steps,
    attn_master,
    attn_first,
    attn_second,
    ffn_master,
    ffn_first,
    ffn_second,
    norm_master,
    norm_first,
    norm_second,
    step_count,
    cotangent,
):
    length, model_width = tokens_in.shape
    local_width = model_width // lax.axis_size("mp")
    heads_local = local_width // HEAD_DIM
    clip_slots = frame_counts.shape[1]
    text_len = text_feats.shape[2]
    text_width = text_feats.shape[3]
    key_count = clip_slots * text_len
    attn_flat, ffn_flat, norm_flat = (
        lax.all_gather(attn_master.astype(jnp.bfloat16), "dp", axis=1, tiled=True),
        lax.all_gather(ffn_master.astype(jnp.bfloat16), "dp", axis=1, tiled=True),
        lax.all_gather(norm_master.astype(jnp.bfloat16), "dp", axis=0, tiled=True),
    )
    hidden_local = ffn_flat.shape[1] // (3 * model_width)
    attn_pieces = split_flat(
        attn_flat[0],
        [
            (model_width, local_width),
            (model_width, local_width),
            (model_width, local_width),
            (local_width, model_width),
            (text_width, local_width),
            (text_width, local_width),
            (COND, 4 * local_width),
            (local_width,),
            (local_width,),
            (local_width,),
            (local_width,),
        ],
    )
    w_query, w_key, w_value, w_out, w_text_key, w_text_value, w_mod = attn_pieces[:7]
    query_gain, key_gain, text_gain, cross_gate = [
        gain_piece.astype(jnp.float32) for gain_piece in attn_pieces[7:]
    ]
    w_gate, w_up, w_down = split_flat(
        ffn_flat[0],
        [(model_width, hidden_local), (model_width, hidden_local), (hidden_local, model_width)],
    )
    norm_gains = norm_flat.astype(jnp.float32).reshape(4, model_width)
    segment, member, positions = clip_layout(frame_counts[0], length, FRAME_TOK, clip_slots)
    cosine, sine_table = rope_tables(positions, HEAD_DIM)
    cond_low = condition(time_steps[0], COND).astype(jnp.bfloat16)
    mod_local = jnp.dot(cond_low, w_mod, preferred_element_type=jnp.float32).reshape(
        clip_slots, 4, local_width
    )
    modulation = lax.all_gather(mod_local, "mp", axis=2, tiled=True)
    scale_attn, gate_attn, scale_ffn, gate_ffn = [
        jnp.dot(member, modulation[:, part_index], precision=lax.Precision.HIGHEST)
        for part_index in range(4)
    ]
    residual = tokens_in.astype(jnp.float32)
    normed_full, back_pre = jax.vjp(modulate, residual, norm_gains[0], scale_attn)
    normed = normed_full.astype(jnp.bfloat16)
    query_lin = jnp.dot(normed, w_query, preferred_element_type=jnp.float32)
    key_lin = jnp.dot(normed, w_key, preferred_element_type=jnp.float32)
    value_lin = jnp.dot(normed, w_value, preferred_element_type=jnp.float32)

    def head_rope(linear, gain):
        heads_view = linear.reshape(length, heads_local, HEAD_DIM)
        return rotate(
            rms_norm(heads_view) * gain.reshape(heads_local, HEAD_DIM), cosine, sine_table
        )

    def text_norm(linear, gain):
        return rms_norm(linear.reshape(key_count, heads_local, HEAD_DIM)) * gain.reshape(
            heads_local, HEAD_DIM
        )

    query_rot, back_query = jax.vjp(head_rope, query_lin, query_gain)
    key_rot, back_key = jax.vjp(head_rope, key_lin, key_gain)
    text_rows = text_feats[0].reshape(key_count, text_width)
    text_key_lin = jnp.dot(text_rows, w_text_key, preferred_element_type=jnp.float32)
    text_value_lin = jnp.dot(text_rows, w_text_value, preferred_element_type=jnp.float32)
    text_key_full, back_text = jax.vjp(text_norm, text_key_lin, text_gain)
    query_heads = query_rot.astype(jnp.bfloat16).transpose(1, 0, 2)
    key_heads = key_rot.astype(jnp.bfloat16).transpose(1, 0, 2)
    value_heads = (
        value_lin.astype(jnp.bfloat16).reshape(length, heads_local, HEAD_DIM).transpose(1, 0, 2)
    )
    text_key_heads = text_key_full.astype(jnp.bfloat16).transpose(1, 0, 2)
    text_value_heads = (
        text_value_lin.astype(jnp.bfloat16)
        .reshape(key_count, heads_local, HEAD_DIM)
        .transpose(1, 0, 2)
    )
    self_mask = segment[:, None] == segment[None, :]
    key_clip = jnp.arange(key_count, dtype=jnp.int32) // text_len
    cross_mask = (segment[:, None] == key_clip[None, :]) | (segment == clip_slots)[:, None]

    def forward_head(head_inputs):
        query_one, key_one, value_one, text_key_one, text_value_one = head_inputs
        own_out, own_total = attend(query_one, key_one, value_one, self_mask)
        cross_out, cross_total = attend(query_one, text_key_one, text_value_one, cross_mask)
        return (own_out, cross_out, own_total, cross_total)

    own_heads, cross_heads, own_log, cross_log = lax.map(
        forward_head, (query_heads, key_heads, value_heads, text_key_heads, text_value_heads)
    )

    def combine(own_part, cross_part, gate_vector):
        return own_part + jnp.tanh(gate_vector.reshape(heads_local, 1, HEAD_DIM)) * cross_part

    mixed_full, back_mix = jax.vjp(combine, own_heads, cross_heads, cross_gate)
    mixed_heads = mixed_full.transpose(1, 0, 2).reshape(length, local_width).astype(jnp.bfloat16)
    attn_part = jnp.dot(mixed_heads, w_out, preferred_element_type=jnp.float32)
    attn_out = lax.psum(attn_part.astype(jnp.bfloat16), "mp").astype(jnp.float32)
    middle, back_mid = jax.vjp(branch_add, residual, attn_out, gate_attn, norm_gains[1])
    ffn_in_full, back_ffn_in = jax.vjp(modulate, middle, norm_gains[2], scale_ffn)
    ffn_in = ffn_in_full.astype(jnp.bfloat16)
    gate_lin = jnp.dot(ffn_in, w_gate, preferred_element_type=jnp.float32)
    up_lin = jnp.dot(ffn_in, w_up, preferred_element_type=jnp.float32)
    hidden_full, back_swiglu = jax.vjp(swiglu, gate_lin, up_lin)
    hidden = hidden_full.astype(jnp.bfloat16)
    ffn_part = jnp.dot(hidden, w_down, preferred_element_type=jnp.float32)
    ffn_out = lax.psum(ffn_part.astype(jnp.bfloat16), "mp").astype(jnp.float32)
    result_full, back_last = jax.vjp(branch_add, middle, ffn_out, gate_ffn, norm_gains[3])
    output = result_full.astype(jnp.bfloat16)
    dmiddle_last, dffn_out, dgate_ffn, dgain_four = back_last(cotangent.astype(jnp.float32))
    dffn_low = dffn_out.astype(jnp.bfloat16)
    dhidden = jnp.dot(dffn_low, w_down.T, preferred_element_type=jnp.float32)
    grad_down = jnp.dot(hidden.T, dffn_low, preferred_element_type=jnp.float32)
    dgate_lin, dup_lin = back_swiglu(dhidden)
    dgate_low = dgate_lin.astype(jnp.bfloat16)
    dup_low = dup_lin.astype(jnp.bfloat16)
    grad_gate = jnp.dot(ffn_in.T, dgate_low, preferred_element_type=jnp.float32)
    grad_up = jnp.dot(ffn_in.T, dup_low, preferred_element_type=jnp.float32)
    dffn_in_part = jnp.dot(dgate_low, w_gate.T, preferred_element_type=jnp.float32) + jnp.dot(
        dup_low, w_up.T, preferred_element_type=jnp.float32
    )
    dffn_in = lax.psum(dffn_in_part.astype(jnp.bfloat16), "mp").astype(jnp.float32)
    dmiddle_pre, dgain_three, dscale_ffn = back_ffn_in(dffn_in)
    ffn_grad_flat = jnp.concatenate(
        [grad_gate.reshape(-1), grad_up.reshape(-1), grad_down.reshape(-1)]
    )[None, :]
    dresidual_mid, dattn_out, dgate_attn, dgain_two = back_mid(dmiddle_last + dmiddle_pre)
    dattn_low = dattn_out.astype(jnp.bfloat16)
    dmixed = jnp.dot(dattn_low, w_out.T, preferred_element_type=jnp.float32)
    grad_out = jnp.dot(mixed_heads.T, dattn_low, preferred_element_type=jnp.float32)
    dmixed_heads = (
        dmixed.astype(jnp.bfloat16)
        .astype(jnp.float32)
        .reshape(length, heads_local, HEAD_DIM)
        .transpose(1, 0, 2)
    )
    down_own, down_cross, grad_cross_gate = back_mix(dmixed_heads)

    def backward_head(head_inputs):
        (
            query_one,
            key_one,
            value_one,
            text_key_one,
            text_value_one,
            own_total,
            cross_total,
            down_own_one,
            down_cross_one,
        ) = head_inputs
        dquery_own, dkey_one, dvalue_one = attend_back(
            query_one, key_one, value_one, self_mask, own_total, down_own_one
        )
        dquery_cross, dtext_key_one, dtext_value_one = attend_back(
            query_one, text_key_one, text_value_one, cross_mask, cross_total, down_cross_one
        )
        return (dquery_own + dquery_cross, dkey_one, dvalue_one, dtext_key_one, dtext_value_one)

    dquery_heads, dkey_heads, dvalue_heads, dtext_key_heads, dtext_value_heads = lax.map(
        backward_head,
        (
            query_heads,
            key_heads,
            value_heads,
            text_key_heads,
            text_value_heads,
            own_log,
            cross_log,
            down_own.astype(jnp.bfloat16),
            down_cross.astype(jnp.bfloat16),
        ),
    )
    dquery_lin, grad_query_gain = back_query(dquery_heads.transpose(1, 0, 2))
    dkey_lin, grad_key_gain = back_key(dkey_heads.transpose(1, 0, 2))
    dtext_key_lin, grad_text_gain = back_text(dtext_key_heads.transpose(1, 0, 2))
    dquery_low = dquery_lin.astype(jnp.bfloat16)
    dkey_low = dkey_lin.astype(jnp.bfloat16)
    dvalue_low = dvalue_heads.transpose(1, 0, 2).reshape(length, local_width).astype(jnp.bfloat16)
    dtext_key_low = dtext_key_lin.astype(jnp.bfloat16)
    dtext_value_low = (
        dtext_value_heads.transpose(1, 0, 2).reshape(key_count, local_width).astype(jnp.bfloat16)
    )
    grad_query = jnp.dot(normed.T, dquery_low, preferred_element_type=jnp.float32)
    grad_key = jnp.dot(normed.T, dkey_low, preferred_element_type=jnp.float32)
    grad_value = jnp.dot(normed.T, dvalue_low, preferred_element_type=jnp.float32)
    grad_text_key = jnp.dot(text_rows.T, dtext_key_low, preferred_element_type=jnp.float32)
    grad_text_value = jnp.dot(text_rows.T, dtext_value_low, preferred_element_type=jnp.float32)
    dnormed_part = jnp.dot(dquery_low, w_query.T, preferred_element_type=jnp.float32)
    dnormed_part = dnormed_part + jnp.dot(dkey_low, w_key.T, preferred_element_type=jnp.float32)
    dnormed_part = dnormed_part + jnp.dot(dvalue_low, w_value.T, preferred_element_type=jnp.float32)
    dnormed = lax.psum(dnormed_part.astype(jnp.bfloat16), "mp").astype(jnp.float32)
    dresidual_pre, dgain_one, dscale_attn = back_pre(dnormed)
    input_grad = (dresidual_mid + dresidual_pre).astype(jnp.bfloat16)
    dmod_full = jnp.stack(
        [
            jnp.dot(member.T, term_rows, precision=lax.Precision.HIGHEST)
            for term_rows in (dscale_attn, dgate_attn, dscale_ffn, dgate_ffn)
        ],
        1,
    )
    rank_offset = lax.axis_index("mp") * local_width
    dmod_local = (
        lax.dynamic_slice_in_dim(dmod_full, rank_offset, local_width, 2)
        .reshape(clip_slots, 4 * local_width)
        .astype(jnp.bfloat16)
    )
    grad_mod = jnp.dot(cond_low.T, dmod_local, preferred_element_type=jnp.float32)
    attn_grad_flat = jnp.concatenate(
        [
            grad_query.reshape(-1),
            grad_key.reshape(-1),
            grad_value.reshape(-1),
            grad_out.reshape(-1),
            grad_text_key.reshape(-1),
            grad_text_value.reshape(-1),
            grad_mod.reshape(-1),
            grad_query_gain,
            grad_key_gain,
            grad_text_gain,
            grad_cross_gate,
        ]
    )[None, :]
    norm_grad_flat = jnp.concatenate([dgain_one, dgain_two, dgain_three, dgain_four])
    attn_shard, ffn_shard, norm_shard = (
        lax.psum_scatter(attn_grad_flat, "dp", scatter_dimension=1, tiled=True),
        lax.psum_scatter(ffn_grad_flat, "dp", scatter_dimension=1, tiled=True),
        lax.psum_scatter(norm_grad_flat, "dp", scatter_dimension=0, tiled=True),
    )
    step_value = step_count[0].astype(jnp.float32)
    attn_result = adamw(attn_master, attn_first, attn_second, attn_shard, step_value, RATE)
    ffn_result = adamw(ffn_master, ffn_first, ffn_second, ffn_shard, step_value, RATE)
    norm_result = adamw(norm_master, norm_first, norm_second, norm_shard, step_value, RATE_NORM)
    return (
        (output, input_grad) + attn_result + ffn_result + norm_result + (grad_cross_gate[None, :],)
    )


def solution(mesh):
    placed = (
        P("dp", None),
        P("dp", None, None, None),
        P("dp", None),
        P("dp", None),
        P("mp", "dp"),
        P("mp", "dp"),
        P("mp", "dp"),
        P("mp", "dp"),
        P("mp", "dp"),
        P("mp", "dp"),
        P("dp"),
        P("dp"),
        P("dp"),
        P(),
        P("dp", None),
    )
    return jax.shard_map(
        local,
        mesh=mesh,
        in_specs=placed,
        out_specs=(
            P("dp", None),
            P("dp", None),
            P("mp", "dp"),
            P("mp", "dp"),
            P("mp", "dp"),
            P("mp", "dp"),
            P("mp", "dp"),
            P("mp", "dp"),
            P("mp", "dp"),
            P("mp", "dp"),
            P("mp", "dp"),
            P("mp", "dp"),
            P("dp"),
            P("dp"),
            P("dp"),
            P("dp"),
            P("dp"),
            P("dp", "mp"),
        ),
        check_vma=False,
    )
```

profile of v0, /device:TPU:8, one launch (start us, length us, event | category | flops | bytes accessed | tf_op | source)
XLA Modules:
  0.0 3081.5 jit_solution(1140857020468914735)
XLA Ops:
  7.3 35.4 %convert_reduce_fusion = bf16[884928]{0:T(1024)(128)(2,1)S(1)} fusion(f32[1,884928]{1,0:T(1,128)} %param.23), kind=kLoop, calls=%fused_computation.123 | loop fusion | flops 884928 | bytes 5309568 | tf_op jit(solution)/shard_map/convert_element_type | solution.py:154
  44.0 5.1 broadcast.337
  49.1 27.7 dynamic-update-slice
  78.3 28.7 all-gather
  111.8 403.8 %all-reduce.24.cloned.1.call-done = bf16[7079424]{0:T(1024)(128)(2,1)} async-done(((bf16[7079424]{0:T(1024)(128)(2,1)}), bf16[7079424]{0:T(1024)(128)(2,1)}) %all-reduce.24.cloned.1.call-update) | async-done | bytes 14158864
  515.6 169.5 %while.38 = (u32[]{:T(128)}, bf16[7079424]{0:T(1024)(128)(2,1)}, bf16[1,1,7079424]{2,1,0:T(2,128)(2,1)}) while((u32[]{:T(128)}, bf16[7079424]{0:T(1024)(128)(2,1)}, bf16[1,1,7079424]{2,1,0:T(2,128)(2,1)}) %tuple.149), condition=%cond, body=%body | while | flops 9 | bytes 56635532
  515.6 7.2 dynamic-slice.9
  522.8 162.3 %reshape_dynamic-update-slice_fusion = bf16[1,1,7079424]{2,1,0:T(2,128)(2,1)} fusion(bf16[1,1,7079424]{2,1,0:T(2,128)(2,1)} %get-tuple-element.880, u32[]{:T(128)S(6)} %multiply.124, u32[]{:T(128)S(6)} %multiply.125, bf16[7079424]{0:T(1024)(128)(2,1)S(1)} %dynamic-slice.9), kind=kLoop, calls=%fused_computation.400 | loop fusion | bytes 28317704
  686.4 39.6 %slice_reduce_fusion.6 = (bf16[589824]{0:T(1024)(128)(2,1)S(1)}, bf16[589824]{0:T(1024)(128)(2,1)S(1)}, bf16[589824]{0:T(1024)(128)(2,1)}, bf16[589824]{0:T(1024)(128)(2,1)}) fusion(bf16[1,7079424]{1,0:T(2,128)(2,1)} %bitcast.389), kind=kLoop, calls=%fused_computation.139 | loop fusion | bytes 9437184 | tf_op jit(solution)/shard_map/slice | solution.py:70
  726.0 94.5 %slice_reduce_fusion.3 = (bf16[1572864]{0:T(1024)(128)(2,1)}, bf16[1572864]{0:T(1024)(128)(2,1)}, bf16[1572864]{0:T(1024)(128)(2,1)}) fusion(bf16[1,7079424]{1,0:T(2,128)(2,1)} %bitcast.390), kind=kLoop, calls=%fused_computation.114 | loop fusion | bytes 18874368 | tf_op jit(solution)/shard_map/slice | solution.py:70
  825.3 2.7 reshape.493
  828.0 3.5 reshape.491
  835.5 5.8 reshape.497
  841.3 2.9 convolution_convert_fusion.3
  845.1 5.8 reshape.496
  850.9 4.6 copy.91
  855.5 2.9 fusion.159
  860.0 6.8 reshape.490
  866.8 4.7 copy.87
  871.5 3.0 fusion.169
  874.4 5.3 all_gather.13
  887.8 26.0 while.40
  916.3 5.3 convert_element_type.276
  922.3 27.7 all-reduce.16.cloned.1.call-done
  956.3 358.4 %all-gather.3.cloned.1.call-done = bf16[1,4718592]{1,0:T(2,128)(2,1)} async-done(((bf16[1,589824]{1,0:T(2,128)(2,1)}), bf16[1,4718592]{1,0:T(2,128)(2,1)}) %all-gather.3.cloned.1.call-update) | async-done | bytes 9437200 | tf_op jit(solution)/shard_map/all_gather | solution.py:155
  1314.7 94.9 %slice_reduce_fusion = (bf16[1572864]{0:T(1024)(128)(2,1)}, bf16[1572864]{0:T(1024)(128)(2,1)}, bf16[1572864]{0:T(1024)(128)(2,1)}) fusion(bf16[1,4718592]{1,0:T(2,128)(2,1)} %all-gather.3.cloned.1.call-done), kind=kLoop, calls=%fused_computation.111 | loop fusion | bytes 18874368 | tf_op jit(solution)/shard_map/slice | solution.py:70
  1409.5 6.8 reshape.502
  1416.3 5.8 reshape.501
  1422.1 5.8 reshape.500
  1427.9 2.6 fusion.215
  1438.0 29.1 all-reduce.18.cloned.1.call-done
  1473.5 3.6 fusion.222
  1484.5 4.1 copy.113
  1489.7 4.2 copy.112
  1494.0 7.0 reshape.516
  1501.0 14.3 all-reduce.20.cloned.1.call-done
  1517.4 2.7 multiply_reduce_fusion.3
  1529.2 74.6 %while.41 = (s32[]{:T(128)}, f32[6,128,64]{1,2,0:T(8,128)}, f32[6,128,64]{1,2,0:T(8,128)}, bf16[6,128,64]{1,2,0:T(8,128)(2,1)}, f32[6,128,64]{1,2,0:T(8,128)}, /...) while((s32[]{:T(128)}, f32[6,128,64]{1,2,0:T(8,128)}, ...), condition=%wide.region_25.26_spmd.clone.clone, body=%wide.region_22.25_spmd.clone.clone.sunk | while | flops 21356288 | bytes 1622717 | solution.py:311
  1610.3 19.3 pad_maximum_fusion
  1633.6 2.9 fusion.221
  1645.2 3.1 reshape.507
  1648.3 3.2 reshape.506
  1651.6 3.3 reshape.505
  1654.9 3.2 reshape.504
  1658.1 3.6 convolution_bitcast_fusion.7
  1661.7 6.6 copy.104
  1668.3 7.0 reshape.508
  1675.3 3.6 convolution_bitcast_fusion.6
  1678.9 6.6 copy.105
  1685.5 6.9 reshape.509
  1692.4 3.7 constant_dynamic-update-slice_fusion.12
  1702.5 3.5 constant_dynamic-update-slice_fusion.8
  1707.0 2.8 constant_dynamic-update-slice_fusion.7
  1712.7 3.7 fusion.198
  1716.3 6.9 reshape.510
  1723.3 4.8 constant_dynamic-update-slice_fusion.6
  1733.3 128.0 %while.39 = (u32[]{:T(128)}, f32[7079424]{0:T(1024)}, f32[1,1,7079424]{2,1,0:T(1,128)}) while((u32[]{:T(128)}, f32[7079424]{0:T(1024)}, f32[1,1,7079424]{2,1,0:T(1,128)}) %tuple.158), condition=%cond.1, body=%body.1 | while | flops 9 | bytes 113272976
  1733.4 21.7 dynamic-slice.10
  1755.0 106.3 %reshape_dynamic-update-slice_fusion.1 = f32[1,1,7079424]{2,1,0:T(1,128)} fusion(f32[1,1,7079424]{2,1,0:T(1,128)} %get-tuple-element.988, u32[]{:T(128)S(6)} %multiply.128, u32[]{:T(128)S(6)} %multiply.129, f32[7079424]{0:T(1024)} %dynamic-slice.10), kind=kLoop, calls=%fused_computation.401 | loop fusion | bytes 56637448
  1861.8 36.4 %all-reduce.7 = f32[6144]{0:T(1024)S(1)} all-reduce(f32[6144]{0:T(1024)S(1)} %pad_maximum_fusion.3), channel_id=4, replica_groups=mesh['dp'=8,'mp'=4] {'dp'}, use_global_device_ids=true, to_apply=%region_41.42.clone | all-reduce | flops 6144 | bytes 49152
  1900.6 312.1 %all-reduce.28.cloned.1.call-done = f32[1,4718592]{1,0:T(1,128)} async-done(((f32[1,4718592]{1,0:T(1,128)}), f32[1,4718592]{1,0:T(1,128)}) %all-reduce.28.cloned.1.call-update) | async-done | bytes 18874384
  2212.7 27.9 fusion.203
  2240.6 806.8 %all-reduce.26.cloned.1.call-done = f32[1,7079424]{1,0:T(1,128)} async-done(((f32[1,7079424]{1,0:T(1,128)}), f32[1,7079424]{1,0:T(1,128)}) %all-reduce.26.cloned.1.call-update) | async-done | bytes 28317712
  3047.4 27.0 fusion.205
  (522 shorter events, 204.7 us)
Async XLA Ops:
  7.2 834.2 %copy-start = (bf16[1,4,32,4096]{3,2,1,0:T(8,128)(2,1)S(1)}, bf16[1,4,32,4096]{3,2,1,0:T(8,128)(2,1)}, u32[]{:S(2)}) copy-start(bf16[1,4,32,4096]{3,2,1,0:T(8,128)(2,1)} %param.20) | copy-start | bytes 3145732
  7.2 35.4 %copy-start.111 = (u32[32]{0:T(128)S(1)}, u32[32]{0:T(128)}, u32[]{:S(2)}) copy-start(u32[32]{0:T(128)} %constant.184) | copy-start | bytes 388
  7.2 508.4 %all-reduce.24.cloned.1.call-start = ((), (), s32[]{:S(2)}) async-start(), calls=%async_computation.5 | async-start | bytes 28319744
  76.8 32.9 %copy-start.17 = (bf16[128,1536]{1,0:T(8,128)(2,1)S(1)}, bf16[128,1536]{1,0:T(8,128)(2,1)}, u32[]{:S(2)}) copy-start(bf16[128,1536]{1,0:T(8,128)(2,1)} %param.19) | copy-start | bytes 1179652
  76.8 34.2 %copy-start.121 = (s32[1,4]{1,0:T(1,128)S(1)}, s32[1,4]{1,0:T(1,128)}, u32[]{:S(2)}) copy-start(s32[1,4]{1,0:T(1,128)} %param.22) | copy-start | bytes 52
  76.9 873.1 %all-reduce.16.cloned.1.call-start = ((), (), s32[]{:S(2)}) async-start(), calls=%async_computation | async-start | bytes 786432 | tf_op jit(solution)/shard_map/psum | solution.py:250
  107.6 772.2 %copy-start.64 = (f32[1536]{0:T(1024)}, f32[1536]{0:T(1024)S(1)}, u32[]{:S(2)}) copy-start(f32[1536]{0:T(1024)S(1)} %reshape.528) | copy-start | bytes 18436
  109.9 405.7 %copy-start.112 = (f32[128]{0:T(128)}, f32[128]{0:T(128)S(1)}, u32[]{:S(2)}) copy-start(f32[128]{0:T(128)S(1)} %fusion.118) | copy-start | bytes 1540
  825.3 58.3 %copy-start.10 = (bf16[1536,384]{1,0:T(8,128)(2,1)}, bf16[1536,384]{1,0:T(8,128)(2,1)S(1)}, u32[]{:S(2)}) copy-start(bf16[1536,384]{1,0:T(8,128)(2,1)S(1)} %reshape.494) | copy-start | bytes 3538948
  828.0 7.5 copy-start.14
  871.5 8.3 copy-start.18
  871.5 8.3 copy-start.106
  871.5 9.9 copy-start.29
  871.5 10.4 copy-start.28
  882.3 5.5 copy-start.36
  886.9 28.2 copy-start.12
  913.8 7.9 copy-start.27
  913.8 7.9 copy-start.38
  913.8 7.9 copy-start.42
  915.0 6.6 copy-start.56
  916.2 5.5 copy-start.90
  916.2 6.1 copy-start.89
  916.3 35.5 %copy-start.19 = (bf16[128,1536]{1,0:T(8,128)(2,1)S(1)}, bf16[128,1536]{1,0:T(8,128)(2,1)}, u32[]{:S(2)}) copy-start(bf16[128,1536]{1,0:T(8,128)(2,1)} %param.19) | copy-start | bytes 1179652
  916.3 35.5 %copy-start.61 = (f32[4,4,1536]{2,0,1:T(4,128)S(1)}, f32[4,4,1536]{2,0,1:T(4,128)}, u32[]{:S(2)}) copy-start(f32[4,4,1536]{2,0,1:T(4,128)} %copy-done.60) | copy-start | bytes 294916
  916.3 398.4 %all-gather.3.cloned.1.call-start = ((), (), s32[]{:S(2)}) async-start(), calls=%async_computation.1 | async-start | bytes 21233664 | tf_op jit(solution)/shard_map/all_gather | solution.py:155
  921.7 545.4 %all-reduce.18.cloned.1.call-start = ((), (), s32[]{:S(2)}) async-start(), calls=%async_computation.2 | async-start | bytes 786432 | tf_op jit(solution)/shard_map/psum | solution.py:259
  1432.1 5.2 copy-start.88
  1434.3 81.0 %all-reduce.20.cloned.1.call-start = ((), (), s32[]{:S(2)}) async-start(), calls=%async_computation.3 | async-start | bytes 786432 | tf_op jit(solution)/shard_map/psum | solution.py:274
  1438.0 39.1 %copy-start.43 = (bf16[6,128,64]{1,2,0:T(8,128)(2,1)}, bf16[6,128,64]{1,2,0:T(8,128)(2,1)S(1)}, u32[]{:S(2)}) copy-start(bf16[6,128,64]{1,2,0:T(8,128)(2,1)S(1)} %fusion.213) | copy-start | bytes 294916
  1467.1 6.4 copy-start.40
  1468.3 8.8 copy-start.114
  1470.9 6.2 copy-start.57
  1482.5 228.5 %all-reduce.22.cloned.1.call-start = ((), (), s32[]{:S(2)}) async-start(), calls=%async_computation.4 | async-start | bytes 786432 | tf_op jit(solution)/shard_map/psum | solution.py:343
  1494.0 21.3 copy-start.62
  1494.0 21.3 copy-start.104
  1494.0 23.4 copy-start.119
  1494.0 23.4 copy-start.22
  1494.0 23.4 copy-start.100
  1515.3 5.7 copy-start.101
  1520.1 9.1 copy-start.47
  1610.2 602.5 %all-reduce.28.cloned.1.call-start = ((), (), s32[]{:S(2)}) async-start(), calls=%async_computation.7 | async-start | bytes 37748736
  1629.6 1417.8 %all-reduce.26.cloned.1.call-start = ((), (), s32[]{:S(2)}) async-start(), calls=%async_computation.6 | async-start | bytes 56635392
  1638.5 5.1 copy-start.33
  1638.5 5.1 copy-start.41
  1638.5 5.1 copy-start.77
  1638.5 5.4 copy-start.79
  1638.5 6.6 copy-start.92
  1638.5 6.6 copy-start.91
  1668.3 7.0 copy-start.46
  1692.4 5.3 copy-start.24
  1696.1 6.3 slice-start
  1700.8 5.1 slice-start.2
  1723.3 8.7 copy-start.97
  1723.3 8.7 copy-start.98
  1733.3 128.1 %copy-start.21 = (bf16[128,1536]{1,0:T(8,128)(2,1)S(1)}, bf16[128,1536]{1,0:T(8,128)(2,1)}, u32[]{:S(2)}) copy-start(bf16[128,1536]{1,0:T(8,128)(2,1)} %param.19) | copy-start | bytes 1179652
  1733.3 128.1 %copy-start.26 = (f32[128,1536]{1,0:T(8,128)S(1)}, f32[128,1536]{1,0:T(8,128)}, u32[]{:S(2)}) copy-start(f32[128,1536]{1,0:T(8,128)} %get-tuple-element.640) | copy-start | bytes 2359300
  1733.3 128.1 %copy-start.48 = (bf16[128,1536]{1,0:T(8,128)(2,1)S(1)}, bf16[128,1536]{1,0:T(8,128)(2,1)}, u32[]{:S(2)}) copy-start(bf16[128,1536]{1,0:T(8,128)(2,1)} %all-reduce.22.cloned.1.call-done) | copy-start | bytes 1179652
  1733.3 128.1 %copy-start.66 = (f32[1536]{0:T(1024)S(1)}, f32[1536]{0:T(1024)}, u32[]{:S(2)}) copy-start(f32[1536]{0:T(1024)} %copy-done.64) | copy-start | bytes 18436
  1733.3 128.1 %copy-start.108 = (f32[128]{0:T(128)S(1)}, f32[128]{0:T(128)}, u32[]{:S(2)}) copy-start(f32[128]{0:T(128)} %fusion.190) | copy-start | bytes 1540
  1733.3 128.5 %copy-start.85 = (f32[1536]{0:T(1024)S(1)}, f32[1536]{0:T(1024)}, u32[]{:S(2)}) copy-start(f32[1536]{0:T(1024)} %get-tuple-element.486) | copy-start | bytes 18436
  1733.3 128.5 %copy-start.86 = (f32[1536]{0:T(1024)S(1)}, f32[1536]{0:T(1024)}, u32[]{:S(2)}) copy-start(f32[1536]{0:T(1024)} %get-tuple-element.484) | copy-start | bytes 18436
  1733.3 128.5 %copy-start.96 = (f32[1536]{0:T(1024)S(1)}, f32[1536]{0:T(1024)}, u32[]{:S(2)}) copy-start(f32[1536]{0:T(1024)} %get-tuple-element.490) | copy-start | bytes 18436
  1733.3 164.8 %copy-start.113 = (f32[128]{0:T(128)S(1)}, f32[128]{0:T(128)}, u32[]{:S(2)}) copy-start(f32[128]{0:T(128)} %copy-done.112) | copy-start | bytes 1540
  3047.4 27.0 copy-start.1
  (71 other events, 181.6 us)
Sparse Core Ops, SparseCore 0:
  77.0 438.5 all-reduce.23
  916.4 33.6 all-reduce.15
  952.2 362.4 all-gather.2
  1434.4 32.5 all-reduce.17
  1482.7 32.5 all-reduce.19
  1610.4 32.6 all-reduce.21
  1647.0 565.6 all-reduce.27
  2216.9 830.4 all-reduce.25
where the time goes:
time: 3100 us; the launch traced here: 3080 us
  waiting for transfers between devices  1950 us (63%)
  local copies, waits for them, and re-layouts  731 us (24%)
  matrix products  156 us (5%)
  other arithmetic  152 us (5%)
  blocking collectives  70.3 us (2%)
    unnamed x11, waiting for transfers between devices  1520 us
    unnamed x278, local copies, waits for them, and re-layouts  374 us
    all_gather x1, waiting for transfers between devices, local(): lax.all_gather(ffn_master.astype(jnp.bfloat16), 'dp', axis=1, tiled=True)  358 us
    slice x3, local copies, waits for them, and re-layouts, split_flat(): lax.slice_in_dim(flat_row, offset, offset + piece_size).reshape(piece_shape)  229 us
  transfers between devices with their start and end apart: 8, of which 7 were waited for; matrix products, arithmetic and copies ran while one was open for 10% of the time, Pallas kernels for 0%

commit v1 on v0

v1 whole, which is shorter than its diff:
```python
import functools
import math

import jax
import jax.numpy as jnp
from jax import lax
from jax.experimental import pallas as pl
from jax.experimental.pallas import tpu as pltpu
from jax.sharding import PartitionSpec as P

HEAD_DIM = 64
COND = 1024
FRAME_TOK = 8
LANES = 128
TILE = 16

EPS = 1e-06
NEG = -1e30
BETA_ONE = 0.9
BETA_TWO = 0.95
RATE = 0.03
RATE_NORM = 0.3
DECAY = 0.1
ADAM_EPS = 1e-08

F32 = jnp.float32
BF16 = jnp.bfloat16
VMEM = pl.BlockSpec(memory_space=pltpu.VMEM)
SMEM = pl.BlockSpec(memory_space=pltpu.SMEM)
ANY = pl.BlockSpec(memory_space=pl.ANY)


def params(mib):
    return pltpu.CompilerParams(vmem_limit_bytes=mib << 20)


def round_up(value, unit):
    return -(-value // unit) * unit


class Layout:
    def __init__(self, total, width, parts, tile, spare=0):
        self.total, self.width, self.parts, self.spare = total, width, parts, spare
        self.unit = tile * width
        self.size = total // parts
        self.base = [d * self.size // self.unit * tile for d in range(parts)] + [
            round_up(-(-total // width), tile)
        ]
        self.off = [d * self.size - self.base[d] * width for d in range(parts)]
        self.used = round_up(max(-(-(o + self.size) // width) for o in self.off), tile)
        self.rows = self.used + spare
        self.lanes = width // LANES
        self.edge = round_up(max(self.off), TILE * LANES)

    def offset(self, index):
        return (index * self.size) % self.unit

    def spans(self, low, high):
        found = []
        for d in range(self.parts):
            first, last = max(low, self.base[d]), min(high, self.base[d + 1])
            if first < last:
                found.append((d, first - self.base[d], last - first, first - low))
        return found

    def pick(self, held, low, high):
        found = [held[d, first : first + rows] for d, first, rows, _ in self.spans(low, high)]
        return found[0] if len(found) == 1 else jnp.concatenate(found, 0)

    def cut(self, matrices, spares=None):
        short = self.base[self.parts - 1] + self.used - sum(m.shape[0] for m in matrices)
        if short > 0:
            matrices = matrices + [jnp.zeros((short, self.width), matrices[0].dtype)]
        whole = jnp.concatenate(matrices, 0)
        if spares is None and self.used * self.parts == whole.shape[0]:
            return whole.reshape(self.parts, self.used, self.width)
        pieces = [whole[b : b + self.used] for b in self.base[: self.parts]]
        if spares is not None:
            pieces = [jnp.concatenate([p, spares[d]], 0) for d, p in enumerate(pieces)]
        return jnp.stack(pieces)


class Pieces:
    def __init__(self, layout, high, ring):
        self.width = layout.width
        parts = layout.parts
        self.rows = round_up(-(-high // parts), LANES)
        self.holders = sum(base < high for base in layout.base[:parts])
        free = list(range(self.holders, parts))
        self.where, self.pairs = [], {}
        for d in range(self.holders):
            last = min(layout.base[d + 1], high)
            for number, low in enumerate(range(layout.base[d], last, self.rows)):
                owner = d
                if number:
                    near = [f for f in free if (f - d) % ring.inner == 0] or free
                    owner = near[-1]
                    free.remove(owner)
                    self.pairs.setdefault(number, []).append((d, owner))
                self.where.append((low, min(low + self.rows, last), owner))

    def send(self, block):
        self.first = block[: self.rows]
        self.sent = {
            number: lax.ppermute(
                block[number * self.rows : (number + 1) * self.rows], "dp", pairs
            )
            for number, pairs in self.pairs.items()
        }
        return self

    def moving(self):
        return self.sent

    def land(self, moved):
        self.got = functools.reduce(jnp.add, moved.values())

    def piece(self, index):
        return jnp.where(index < self.holders, self.first, self.got)

    def spans(self, low, high):
        found = []
        for start, end, owner in self.where:
            first, last = max(low, start), min(high, end)
            if first < last:
                found.append((owner, first - start, last - first, first - low))
        return found

    def pick(self, held, low, high):
        found = [held[d, first : first + rows] for d, first, rows, _ in self.spans(low, high)]
        return found[0] if len(found) == 1 else jnp.concatenate(found, 0)


def to_rows(layout, flat, index, spare=None):
    rows, lanes, size = layout.used, layout.lanes, layout.size
    whole = size // (8 * LANES) * 8
    tail = size - whole * LANES
    head = max(layout.edge // LANES, 8)
    depth = round_up(max(rows * lanes + head, head + whole + 8) + 8, 8)
    offset = layout.offset(index).astype(jnp.int32)[None]
    operands = [offset, flat]
    if layout.edge:
        tails = flat[:, size - layout.edge :].reshape(head, LANES)
        chain = [(d, d + 1) for d in range(layout.parts - 1)]
        operands.append(lax.ppermute(tails.astype(BF16), "dp", chain).astype(F32))
    if layout.spare:
        operands.append(spare)

    def kernel(off_ref, x_ref, *rest):
        if layout.spare:
            rest[-2][rows : rows + layout.spare, :] = rest[-3][...].astype(BF16)
        edge_ref = rest[0] if layout.edge else None
        out_ref, pad_ref = rest[-2:]
        if layout.edge:
            pad_ref[0:head, :] = edge_ref[...]
        pad_ref[pl.ds(head, whole), :] = x_ref[:, pl.ds(0, whole * LANES)].reshape(whole, LANES)
        left = depth - head - whole
        pad_ref[pl.ds(head + whole, left), :] = jnp.zeros((left, LANES), F32)
        for row in range(-(-tail // LANES)):
            count = min(LANES, tail - row * LANES)
            pad_ref[pl.ds(head + whole + row, 1), 0:count] = x_ref[
                :, pl.ds((whole + row) * LANES, count)
            ]
        off_rows, off_lane = off_ref[0] // LANES, off_ref[0] % LANES
        lane = lax.broadcasted_iota(jnp.int32, (rows, LANES), 1)
        for j in range(lanes):
            if layout.edge:
                before = pad_ref[pl.ds(head + j - off_rows - 1, rows, stride=lanes), :]
                here = pad_ref[pl.ds(head + j - off_rows, rows, stride=lanes), :]
                value = jnp.where(
                    lane < off_lane,
                    pltpu.roll(before, off_lane, 1),
                    pltpu.roll(here, off_lane, 1),
                )
            else:
                value = pad_ref[pl.ds(head + j, rows, stride=lanes), :]
            out_ref[0:rows, LANES * j : LANES * j + LANES] = value.astype(BF16)

    return pl.pallas_call(
        kernel,
        out_shape=jax.ShapeDtypeStruct((layout.rows, layout.width), BF16),
        in_specs=[SMEM] + [VMEM] * (len(operands) - 1),
        out_specs=VMEM,
        scratch_shapes=[pltpu.VMEM((depth, LANES), F32)],
        compiler_params=params(40),
    )(*operands)


def block_rows(layout):
    need = -(-layout.size // LANES)
    steps = max(1, need // 864)
    return round_up(-(-need // steps), 8), -(-need // round_up(-(-need // steps), 8))


def to_flat(layout, matrix, index):
    rows, lanes = layout.used, layout.lanes
    block, steps = block_rows(layout)
    depth = round_up(max(rows * lanes, block * steps + layout.unit // LANES + 1), 8) + 8
    offset = layout.offset(index).astype(jnp.int32)[None]

    def kernel(off_ref, x_ref, out_ref, pad_ref):
        for j in range(lanes):
            pad_ref[pl.ds(j, rows, stride=lanes), :] = x_ref[
                0:rows, LANES * j : LANES * j + LANES
            ]
        left = depth - rows * lanes
        pad_ref[pl.ds(rows * lanes, left), :] = jnp.zeros((left, LANES), F32)
        off_rows, off_lane = off_ref[0] // LANES, off_ref[0] % LANES
        turn = (LANES - off_lane) % LANES
        lane = lax.broadcasted_iota(jnp.int32, (block, LANES), 1)

        def body(step, carry):
            start = pl.multiple_of(step * block, 8)
            here = pad_ref[pl.ds(start + off_rows, block), :]
            if layout.edge:
                after = pad_ref[pl.ds(start + off_rows + 1, block), :]
                here = jnp.where(
                    lane < LANES - off_lane, pltpu.roll(here, turn, 1), pltpu.roll(after, turn, 1)
                )
            out_ref[pl.ds(start, block), :] = here
            return carry

        lax.fori_loop(0, steps, body, 0)

    return pl.pallas_call(
        kernel,
        out_shape=jax.ShapeDtypeStruct((block * steps, LANES), F32),
        in_specs=[SMEM, VMEM],
        out_specs=VMEM,
        scratch_shapes=[pltpu.VMEM((depth, LANES), F32)],
        compiler_params=params(48),
    )(offset, matrix)


def adamw(master, first, second, gradient, step_value, rate):
    first_new = BETA_ONE * first + (1.0 - BETA_ONE) * gradient
    second_new = BETA_TWO * second + (1.0 - BETA_TWO) * gradient * gradient
    first_fix = 1.0 - jnp.power(BETA_ONE, step_value)
    second_fix = 1.0 - jnp.power(BETA_TWO, step_value)
    update = rate * (
        first_new / first_fix / (jnp.sqrt(second_new / second_fix) + ADAM_EPS) + DECAY * master
    )
    master_new = master - update
    return (master_new, first_new, second_new, gradient, master_new.astype(BF16))


def adamw_flat(layout, master, first, second, gradient, step_value, rate):
    block, steps = block_rows(layout)
    fixes = jnp.stack(
        [1.0 - jnp.power(BETA_ONE, step_value), 1.0 - jnp.power(BETA_TWO, step_value)]
    )

    def kernel(fix_ref, w_ref, m_ref, v_ref, g_ref, w_out, m_out, v_out, g_out, c_out):
        view = lambda ref: ref.reshape(block, LANES)
        grad = g_ref[...]
        master_old = view(w_ref)[...]
        first_new = BETA_ONE * view(m_ref)[...] + (1.0 - BETA_ONE) * grad
        second_new = BETA_TWO * view(v_ref)[...] + (1.0 - BETA_TWO) * grad * grad
        update = rate * (
            first_new / fix_ref[0] / (jnp.sqrt(second_new / fix_ref[1]) + ADAM_EPS)
            + DECAY * master_old
        )
        view(w_out)[...] = master_old - update
        view(m_out)[...] = first_new
        view(v_out)[...] = second_new
        view(g_out)[...] = grad
        c_out[...] = w_out[...].astype(BF16)

    row = pl.BlockSpec((1, block * LANES), lambda i: (0, i))
    like = jax.ShapeDtypeStruct(master.shape, F32)
    return pl.pallas_call(
        kernel,
        grid=(steps,),
        out_shape=(like, like, like, like, jax.ShapeDtypeStruct(master.shape, BF16)),
        in_specs=[SMEM, row, row, row, pl.BlockSpec((block, LANES), lambda i: (i, 0))],
        out_specs=(row,) * 5,
        compiler_params=params(48),
    )(fixes, master, first, second, gradient)


class Ring:
    def __init__(self, parts):
        self.parts = parts
        self.inner = 2 if parts % 2 == 0 else 1
        self.outer = parts // self.inner
        self.small = self.outer <= 8
        self.next = [(d, (d + self.inner) % parts) for d in range(parts)]
        self.pair = [(d, d ^ 1) for d in range(parts)]

    def swap(self, block):
        return lax.ppermute(block, "dp", self.pair)

    def onward(self, block):
        return lax.ppermute(block, "dp", self.next)


def join(runs, *work):
    moving = [run.moving() for run in runs]
    moving, work = lax.optimization_barrier((moving, list(work)))
    for run, moved in zip(runs, moving):
        run.land(moved)
    return work[0] if len(work) == 1 else work


class Gathering:
    def __init__(self, ring, block, index):
        self.ring, self.block, self.round = ring, block, 0
        self.rounds = ring.outer if ring.small else 1
        self.at, self.side = index // ring.inner, index % ring.inner
        self.zero = jnp.zeros((), index.dtype)
        self.held = jnp.zeros((ring.outer, ring.inner) + block.shape, block.dtype)

    def send(self):
        ring = self.ring
        self.sent = {}
        if self.round >= self.rounds:
            return self
        if not ring.small:
            self.sent["all"] = gather_small(self.block[None], ring.parts)
            return self
        if ring.inner == 2:
            self.sent["other"] = ring.swap(self.block)
        if self.round < ring.outer - 1:
            self.sent["after"] = ring.onward(self.block)
        return self

    def moving(self):
        return self.sent

    def put(self, value, side):
        slot = lax.rem(self.at - self.round + self.ring.outer, self.ring.outer)
        self.held = lax.dynamic_update_slice(
            self.held, value[None, None], (slot, side) + (self.zero,) * value.ndim
        )

    def land(self, moved):
        if self.round >= self.rounds:
            return
        if "all" in moved:
            self.held = moved["all"]
        else:
            if "other" in moved:
                self.put(moved["other"], 1 - self.side)
            self.put(self.block, self.side)
            self.block = moved.get("after")
        self.round += 1

    def result(self):
        while self.round < self.rounds:
            join([self.send()])
        return self.held.reshape((self.ring.parts,) + self.held.shape[-2:])


class Shared(Gathering):
    def __init__(self, ring, block, index, share):
        super().__init__(ring, block, index)
        self.share = share
        self.far_held = jnp.zeros(self.held.shape[:2] + (share,) + block.shape[1:], block.dtype)
        self.rounds += 1
        self.chunk = None

    def send(self):
        if self.round < self.rounds - 1:
            super().send()
        else:
            self.sent = {}
        if self.chunk is not None and self.round < self.rounds:
            pairs = [(m, m ^ 2) for m in range(lax.axis_size("mp"))]
            self.sent["far"] = lax.ppermute(self.chunk, "mp", pairs)
        return self

    def land(self, moved):
        if self.round >= self.rounds:
            return
        far = moved.pop("far", None)
        if far is not None:
            if not self.ring.small:
                self.far_held = far
            else:
                slot = lax.rem(self.at - self.round + 1 + self.ring.outer, self.ring.outer)
                for number, side in ((0, self.side), (1, 1 - self.side)):
                    self.far_held = lax.dynamic_update_slice(
                        self.far_held,
                        far[number][None, None],
                        (slot, side) + (self.zero,) * (far.ndim - 1),
                    )
        if self.round == self.rounds - 1:
            self.round += 1
            return
        if "all" in moved:
            super().land(moved)
            self.chunk = self.held[:, : self.share]
        else:
            self.chunk = jnp.stack([self.block[: self.share], moved["other"][: self.share]])
            super().land(moved)

    def both(self):
        own = self.result()[:, : self.share]
        return own, self.far_held.reshape(own.shape)


class Scattering:
    def __init__(self, ring, blocks, index):
        self.ring, self.blocks = ring, blocks
        self.at, self.side = index // ring.inner, index % ring.inner
        self.left = ring.outer if ring.small else 1
        self.pending = None

    def send(self):
        ring = self.ring
        self.sent = {}
        if not self.left:
            return self
        self.left -= 1
        if not ring.small:
            self.sent["all"] = scatter_halves(self.blocks, ring.parts)
            return self
        if self.pending is not None:
            self.sent["carried"] = ring.onward(self.pending.astype(BF16))
        first = lax.rem(self.at + self.left, ring.outer) * ring.inner
        self.mine = lax.dynamic_index_in_dim(self.blocks, first + self.side, 0, False)
        if ring.inner == 2:
            given = lax.dynamic_index_in_dim(self.blocks, first + 1 - self.side, 0, False)
            self.sent["other"] = ring.swap(given)
        return self

    def moving(self):
        return self.sent

    def land(self, moved):
        if "all" in moved:
            self.pending = moved["all"]
        if "all" in moved or not moved:
            return
        total = self.mine.astype(F32)
        for value in moved.values():
            total = total + value.astype(F32)
        self.pending = total

    def result(self):
        while self.left:
            join([self.send()])
        return self.pending


def step(runs):
    runs[:] = [run for run in runs if run.round < run.rounds]
    for run in runs:
        run.send()


class Once:
    def __init__(self, arrays, steps):
        self.sent = {}
        count = lax.axis_size("mp")
        for name, array in arrays.items():
            pairs = [(m, m ^ steps) for m in range(count)]
            self.sent[name] = lax.ppermute(array, "mp", pairs)

    def moving(self):
        return self.sent

    def land(self, moved):
        self.got = moved


def in_order(pieces):
    me = lax.axis_index("mp")
    first = pieces[0]
    held = jnp.zeros((len(pieces),) + first.shape, first.dtype)
    zero = jnp.zeros((), me.dtype)
    for key, piece in pieces.items():
        held = lax.dynamic_update_slice(held, piece[None], (me ^ key,) + (zero,) * piece.ndim)
    return held


def scatter_halves(blocks, parts):
    index = lax.axis_index("dp")
    step = parts // 2
    while step:
        upper = (index // step) % 2 == 1
        low, high = blocks[:step], blocks[step:]
        mine, given = jnp.where(upper, high, low), jnp.where(upper, low, high)
        got = lax.ppermute(given.astype(BF16), "dp", [(d, d ^ step) for d in range(parts)])
        blocks = mine.astype(F32) + got.astype(F32)
        step //= 2
    return blocks[0]


def gather_small(values, parts):
    index = lax.axis_index("dp")
    step = 1
    while step < parts:
        other = lax.ppermute(values, "dp", [(d, d ^ step) for d in range(parts)])
        upper = (index // step) % 2 == 1
        values = jnp.where(
            upper, jnp.concatenate([other, values], 0), jnp.concatenate([values, other], 0)
        )
        step *= 2
    return values


def sum_mp(part):
    count = lax.axis_size("mp")
    near = [(m, m ^ 1) for m in range(count)]
    half = part.shape[0] // 2
    side = lax.axis_index("mp") % 2
    low, high = part[:half], part[half:]
    mine, given = jnp.where(side == 0, low, high), jnp.where(side == 0, high, low)
    total = mine.astype(F32) + lax.ppermute(given, "mp", near).astype(F32)
    step = 2
    while step < count:
        total = total.astype(BF16)
        far = [(m, m ^ step) for m in range(count)]
        total = total.astype(F32) + lax.ppermute(total, "mp", far).astype(F32)
        step *= 2
    total = total.astype(BF16)
    other = lax.ppermute(total, "mp", near)
    return jnp.concatenate(
        [jnp.where(side == 0, total, other), jnp.where(side == 0, other, total)], 0
    )


def rope_tables(positions, head_size, repeats):
    half_size = head_size // 2
    frequency = jnp.exp(
        -jnp.log(10000.0) * 2.0 * jnp.arange(half_size, dtype=jnp.float32) / head_size
    )
    frequency = jnp.tile(frequency, 2 * repeats)
    angles = positions.astype(jnp.float32)[:, None] * frequency[None, :]
    return jnp.cos(angles), jnp.sin(angles)


def clip_layout(frames_row, length, frame_tok, clip_slots):
    clip_len = frames_row * frame_tok
    slots = jnp.arange(clip_slots, dtype=jnp.int32)
    clip_end = jnp.sum(
        jnp.where(slots[:, None] >= slots[None, :], clip_len[None, :], 0), 1, dtype=jnp.int32
    )
    clip_start = clip_end - clip_len
    row_index = jnp.arange(length, dtype=jnp.int32)
    segment = jnp.sum(
        (row_index[:, None] >= clip_end[None, :]).astype(jnp.int32), 1, dtype=jnp.int32
    )
    member = segment[:, None] == slots[None, :]
    begin_row = jnp.sum(jnp.where(member, clip_start[None, :], 0), 1, dtype=jnp.int32)
    begin_row = begin_row + jnp.where(segment == clip_slots, clip_end[clip_slots - 1], 0)
    return segment, row_index - begin_row


def condition_rows(steps, cond_width):
    packs, clips = steps.shape
    column = jnp.arange(4 * cond_width, dtype=jnp.int32)
    half_size = cond_width // 2
    k = column // 4
    place = lax.rem(k, half_size).astype(F32)
    frequency = jnp.exp(-jnp.log(10000.0) * place / half_size)
    angles = steps.reshape(-1)[:, None] * frequency[None, :]
    waves = jnp.where((k < half_size)[None, :], jnp.cos(angles), jnp.sin(angles))
    cond = jax.nn.silu(waves).astype(BF16).reshape(packs, 1, clips, 4 * cond_width)
    part = jnp.arange(4, dtype=jnp.int32)
    own = (lax.rem(column, 4)[None, :] == part[:, None])[None, :, None, :]
    return jnp.where(own, cond, jnp.zeros((), BF16)).reshape(packs, 4 * clips, 4 * cond_width)


def dot(left, right):
    return jnp.dot(left, right, preferred_element_type=F32)


def dot_t(left, right):
    return lax.dot_general(left, right, (((1,), (1,)), ((), ())), preferred_element_type=F32)


def t_dot(left, right):
    return lax.dot_general(left, right, (((0,), (0,)), ((), ())), preferred_element_type=F32)


def row_mean(values):
    return jnp.mean(values, -1, keepdims=True)


def per_token(seg, mod_ref, part):
    total = jnp.where(seg == 0, mod_ref[part, 0:1, :], 0.0)
    for clip in range(1, mod_ref.shape[1]):
        total = total + jnp.where(seg == clip, mod_ref[part, clip : clip + 1, :], 0.0)
    return total


def per_clip(seg, values, out_ref):
    for clip in range(out_ref.shape[0]):
        out_ref[clip : clip + 1, :] = jnp.sum(jnp.where(seg == clip, values, 0.0), 0, keepdims=True)


def column_sum(values):
    return jnp.sum(values, 0, keepdims=True)


def rms_back(unit, scale, grad):
    return scale * (grad - unit * row_mean(unit * grad))


def branch_back(grad, branch, gate_tok, gain):
    scale = lax.rsqrt(row_mean(branch * branch) + EPS)
    unit = branch * scale
    opened = jnp.tanh(gate_tok)
    grad_unit = grad * opened
    dgate = grad * unit * gain * (1.0 - opened * opened)
    return rms_back(unit, scale, grad_unit * gain), dgate, column_sum(grad_unit * unit)


def modulate_back(grad, values, gain, scale_tok):
    scale = lax.rsqrt(row_mean(values * values) + EPS)
    unit = values * scale
    grad_unit = grad * unit
    dscale = grad_unit * gain
    dgain = column_sum(grad_unit * (1.0 + scale_tok))
    return rms_back(unit, scale, grad * gain * (1.0 + scale_tok)), dscale, dgain


def head_mean(values):
    width = values.shape[-1]
    rows = lax.broadcasted_iota(jnp.int32, (width, width), 0) // HEAD_DIM
    columns = lax.broadcasted_iota(jnp.int32, (width, width), 1) // HEAD_DIM
    same = jnp.where(rows == columns, 1.0 / HEAD_DIM, 0.0)
    return jnp.dot(values, same, precision=lax.Precision.HIGHEST, preferred_element_type=F32)


def turn(values, sign):
    width = values.shape[-1]
    half = HEAD_DIM // 2
    lane = lax.broadcasted_iota(jnp.int32, values.shape, 1) % HEAD_DIM
    ahead = pltpu.roll(values, width - half, 1)
    behind = pltpu.roll(values, half, 1)
    return jnp.where(lane < half, -sign * ahead, sign * behind)


def head_rms(linear):
    scale = lax.rsqrt(head_mean(linear * linear) + EPS)
    return linear * scale, scale


def head_rms_back(linear, grad, gain):
    unit, scale = head_rms(linear)
    scaled = grad * gain
    return scale * (scaled - unit * head_mean(unit * scaled)), column_sum(grad * unit)


def soft(query, keys, mask):
    scores = dot_t(query, keys) * HEAD_DIM ** (-0.5)
    scores = jnp.where(mask, scores, NEG)
    raised = jnp.exp(scores - jnp.max(scores, -1, keepdims=True))
    return raised / jnp.sum(raised, -1, keepdims=True)


def soft_back(query, keys, values, probs, grad_out):
    grad_probs = dot_t(grad_out, values)
    grad_values = t_dot(probs.astype(BF16), grad_out)
    inner_sum = jnp.sum(probs * grad_probs, -1, keepdims=True)
    grad_scores = (probs * (grad_probs - inner_sum) * HEAD_DIM ** (-0.5)).astype(BF16)
    return dot(grad_scores, keys), t_dot(grad_scores, query), grad_values


def masks(seg_ref, seg_row_ref, key_count, clip_slots):
    seg = seg_ref[...]
    key_clip = lax.broadcasted_iota(jnp.int32, (1, key_count), 1) // (key_count // clip_slots)
    return seg == seg_row_ref[...], (seg == key_clip) | (seg == clip_slots)


class Fetch:
    def __init__(self, held_ref, layout, low, high, into_ref, sems, first):
        self.copies = []
        for number, (d, start, rows, offset) in enumerate(layout.spans(low, high)):
            copy = pltpu.make_async_copy(
                held_ref.at[d, pl.ds(start, rows)],
                into_ref.at[pl.ds(offset, rows)],
                sems.at[first + number],
            )
            copy.start()
            self.copies.append(copy)

    def wait(self):
        for copy in self.copies:
            copy.wait()


def own_rows(block, i, offset):
    row = lax.broadcasted_iota(jnp.int32, block.shape, 0) + i * block.shape[0]
    lane = lax.broadcasted_iota(jnp.int32, block.shape, 1)
    mine = row * block.shape[1] + lane >= offset
    return jnp.where(mine, block.astype(F32), 0.0).astype(BF16)


def block_place(layout, index):
    first = index * layout.size // layout.unit * (layout.unit // layout.width // LANES)
    return jnp.stack([first, layout.offset(index)]).astype(jnp.int32)


def modulation_share(layout, index, rows, low, cond):
    packs, conds, depth = cond.shape
    blocks = layout.used // LANES
    first_block, count = low // LANES, depth // LANES

    def kernel(place_ref, w_ref, cond_ref, out_ref):
        out_ref[...] = jnp.zeros_like(out_ref)

        def body(i, carry):
            g = place_ref[0] + i - first_block

            @pl.when((g >= 0) & (g < count))
            def _():
                weights = w_ref[pl.ds(pl.multiple_of(i * LANES, LANES), LANES), :]
                lanes = pl.ds(pl.multiple_of(g * LANES, LANES), LANES)
                left = cond_ref[:, :, lanes].reshape(packs * conds, LANES)
                out_ref[...] += dot(left, own_rows(weights, i, place_ref[1]))

            return carry

        lax.fori_loop(0, blocks, body, 0)

    out = pl.pallas_call(
        kernel,
        out_shape=jax.ShapeDtypeStruct((packs * conds, layout.width), F32),
        in_specs=[SMEM, VMEM, VMEM],
        out_specs=VMEM,
        compiler_params=params(40),
    )(block_place(layout, index), rows, cond)
    return out.reshape(packs, conds, layout.width)


def text_share(layout, index, rows, low, text):
    groups, packs, key_count, text_cut = text.shape
    width = layout.width
    blocks = layout.used // LANES
    first_block, count = low // LANES, groups * text_cut // LANES
    step_packs = min(8, packs)
    per_cut = text_cut // LANES

    def kernel(place_ref, w_ref, text_ref, out_ref, sum_ref):
        sum_ref[...] = jnp.zeros_like(sum_ref)

        def body(i, carry):
            g = place_ref[0] + i - first_block

            @pl.when((g >= 0) & (g < 2 * count))
            def _():
                weights = w_ref[pl.ds(pl.multiple_of(i * LANES, LANES), LANES), :]
                sub = g % count
                lanes = pl.ds(pl.multiple_of(sub % per_cut * LANES, LANES), LANES)
                left = text_ref[sub // per_cut, :, :, lanes].reshape(-1, LANES)
                sum_ref[g // count] += dot(left, own_rows(weights, i, place_ref[1]))

            return carry

        lax.fori_loop(0, blocks, body, 0)
        for kind in range(2):
            out_ref[:, :, kind * width : (kind + 1) * width] = (
                sum_ref[kind].astype(BF16).reshape(step_packs, key_count, width)
            )

    return pl.pallas_call(
        kernel,
        grid=(packs // step_packs,),
        out_shape=jax.ShapeDtypeStruct((packs, key_count, 2 * width), BF16),
        in_specs=[
            SMEM,
            pl.BlockSpec(rows.shape, lambda s: (0, 0), pipeline_mode=pl.Buffered(1)),
            pl.BlockSpec(
                (groups, step_packs, key_count, text_cut),
                lambda s: (0, s, 0, 0),
                pipeline_mode=pl.Buffered(1),
            ),
        ],
        out_specs=pl.BlockSpec((step_packs, key_count, 2 * width), lambda s: (s, 0, 0)),
        scratch_shapes=[pltpu.VMEM((2, step_packs * key_count, width), F32)],
        compiler_params=params(48),
    )(block_place(layout, index), rows, text)


def attention_inputs(layout, held, tokens, seg, mods, norms, gains, cosine, sine):
    length, depth = tokens.shape
    width = layout.width
    count = len(layout.spans(0, 3 * depth))

    def kernel(
        held_ref, x_ref, seg_ref, mod_ref, norm_ref, gain_ref, cos_ref, sin_ref,
        normed_ref, q_ref, k_ref, v_ref, q_lin_ref, k_lin_ref, w_ref, sems,
    ):
        fetch = Fetch(held_ref, layout, 0, 3 * depth, w_ref, sems, 0)
        x = x_ref[...].astype(F32)
        unit = x * lax.rsqrt(row_mean(x * x) + EPS)
        normed = unit * norm_ref[0:1, :] * (1.0 + per_token(seg_ref[...], mod_ref, 0))
        normed = normed.astype(BF16)
        normed_ref[...] = normed
        fetch.wait()
        cosine, sine = cos_ref[...], sin_ref[...]
        for place, (lin_ref, out_ref) in enumerate(((q_lin_ref, q_ref), (k_lin_ref, k_ref))):
            linear = dot(normed, w_ref[place * depth : (place + 1) * depth, :])
            lin_ref[...] = linear
            rms = head_rms(linear)[0] * gain_ref[place : place + 1, :]
            out_ref[...] = (rms * cosine + turn(rms, 1.0) * sine).astype(BF16)
        v_ref[...] = dot(normed, w_ref[2 * depth : 3 * depth, :]).astype(BF16)

    low, full = (jax.ShapeDtypeStruct((length, width), t) for t in (BF16, F32))
    return pl.pallas_call(
        kernel,
        out_shape=(jax.ShapeDtypeStruct((length, depth), BF16), low, low, low, full, full),
        in_specs=[ANY] + [VMEM] * 7,
        out_specs=(VMEM,) * 6,
        scratch_shapes=[
            pltpu.VMEM((3 * depth, width), BF16),
            pltpu.SemaphoreType.DMA((count,)),
        ],
        compiler_params=params(48),
    )(held, tokens, seg, mods, norms, gains, cosine, sine)


def attention_forward(query, key, value, text_lin, seg, seg_row, gains, w_out, clips):
    length, width = query.shape
    key_count = text_lin.shape[0]
    model_width = w_out.shape[1]

    def kernel(
        q_ref, k_ref, v_ref, lin_ref, seg_ref, row_ref, gain_ref, w_ref,
        mixed_ref, cross_ref, part_ref, tk_lin_ref, tk_ref, tv_ref,
    ):
        linear = lin_ref[:, 0:width]
        tk_lin_ref[...] = linear
        tk_ref[...] = (head_rms(linear)[0] * gain_ref[2:3, :]).astype(BF16)
        tv_ref[...] = lin_ref[:, width : 2 * width].astype(BF16)
        own_mask, cross_mask = masks(seg_ref, row_ref, key_count, clips)
        own = []
        for head in range(width // HEAD_DIM):
            at = slice(head * HEAD_DIM, (head + 1) * HEAD_DIM)
            probs = soft(q_ref[:, at], k_ref[:, at], own_mask)
            own.append(dot(probs.astype(BF16), v_ref[:, at]))
            probs = soft(q_ref[:, at], tk_ref[:, at], cross_mask)
            cross_ref[:, at] = dot(probs.astype(BF16), tv_ref[:, at])
        mixed = jnp.concatenate(own, 1) + jnp.tanh(gain_ref[3:4, :]) * cross_ref[...]
        mixed = mixed.astype(BF16)
        mixed_ref[...] = mixed
        part_ref[...] = dot(mixed, w_ref[...]).astype(BF16)

    return pl.pallas_call(
        kernel,
        out_shape=(
            jax.ShapeDtypeStruct((length, width), BF16),
            jax.ShapeDtypeStruct((length, width), F32),
            jax.ShapeDtypeStruct((length, model_width), BF16),
            jax.ShapeDtypeStruct((key_count, width), F32),
            jax.ShapeDtypeStruct((key_count, width), BF16),
            jax.ShapeDtypeStruct((key_count, width), BF16),
        ),
        in_specs=[VMEM] * 8,
        out_specs=(VMEM,) * 6,
        compiler_params=params(48),
    )(query, key, value, text_lin, seg, seg_row, gains, w_out)


def ffn_forward(layout, held, tokens, attn_out, seg, mods, norms, w_down):
    length, depth = tokens.shape
    width = layout.width
    counts = [len(layout.spans(i * depth, (i + 1) * depth)) for i in range(2)]

    def kernel(
        held_ref, x_ref, branch_ref, seg_ref, mod_ref, norm_ref, down_hbm,
        middle_ref, ffn_in_ref, gate_ref, up_ref, hidden_ref, part_ref,
        wg_ref, wu_ref, wd_ref, sems,
    ):
        for_gate = Fetch(held_ref, layout, 0, depth, wg_ref, sems, 0)
        for_up = Fetch(held_ref, layout, depth, 2 * depth, wu_ref, sems, counts[0])
        for_down = pltpu.make_async_copy(down_hbm, wd_ref, sems.at[sum(counts)])
        for_down.start()
        seg = seg_ref[...]
        branch = branch_ref[...].astype(F32)
        unit = branch * lax.rsqrt(row_mean(branch * branch) + EPS)
        opened = jnp.tanh(per_token(seg, mod_ref, 1))
        middle = x_ref[...].astype(F32) + opened * unit * norm_ref[1:2, :]
        middle_ref[...] = middle
        unit = middle * lax.rsqrt(row_mean(middle * middle) + EPS)
        ffn_in = (unit * norm_ref[2:3, :] * (1.0 + per_token(seg, mod_ref, 2))).astype(BF16)
        ffn_in_ref[...] = ffn_in
        for_gate.wait()
        gate = dot(ffn_in, wg_ref[...])
        gate_ref[...] = gate
        for_up.wait()
        up = dot(ffn_in, wu_ref[...])
        up_ref[...] = up
        hidden = (jax.nn.silu(gate) * up).astype(BF16)
        hidden_ref[...] = hidden
        for_down.wait()
        part_ref[...] = dot(hidden, wd_ref[...]).astype(BF16)

    def like(columns, kind):
        return jax.ShapeDtypeStruct((length, columns), kind)

    return pl.pallas_call(
        kernel,
        out_shape=(
            like(depth, F32),
            like(depth, BF16),
            like(width, F32),
            like(width, F32),
            like(width, BF16),
            like(depth, BF16),
        ),
        in_specs=[ANY] + [VMEM] * 5 + [ANY],
        out_specs=(VMEM,) * 6,
        scratch_shapes=[
            pltpu.VMEM((depth, width), BF16),
            pltpu.VMEM((depth, width), BF16),
            pltpu.VMEM((width, depth), BF16),
            pltpu.SemaphoreType.DMA((sum(counts) + 1,)),
        ],
        compiler_params=params(56),
    )(held, tokens, attn_out, seg, mods, norms, w_down)


def ffn_backward(
    layout, held, middle, ffn_out, cotangent, ffn_in, gate, up, hidden, seg, mods, norms, w_down
):
    length, depth = middle.shape
    width = layout.width
    clips = mods.shape[1]
    counts = [len(layout.spans(i * depth, (i + 1) * depth)) for i in range(2)]
    cut = 256

    def kernel(
        held_ref, middle_ref, branch_ref, cot_ref, in_ref, gate_ref, up_ref, hidden_ref,
        seg_ref, mod_ref, norm_ref, down_hbm,
        output_ref, part_ref, gg_ref, gu_ref, gd_ref, dmod_ref, dgain_ref,
        wg_ref, wu_ref, wd_ref, sems,
    ):
        for_down = pltpu.make_async_copy(down_hbm, wd_ref, sems.at[sum(counts)])
        for_down.start()
        for_gate = Fetch(held_ref, layout, 0, depth, wg_ref, sems, 0)
        for_up = Fetch(held_ref, layout, depth, 2 * depth, wu_ref, sems, counts[0])
        seg = seg_ref[...]
        branch = branch_ref[...].astype(F32)
        gate_tok = per_token(seg, mod_ref, 3)
        gain = norm_ref[3:4, :]
        unit = branch * lax.rsqrt(row_mean(branch * branch) + EPS)
        output_ref[...] = (middle_ref[...] + jnp.tanh(gate_tok) * unit * gain).astype(BF16)
        dbranch, dgate_tok, dgain = branch_back(cot_ref[...].astype(F32), branch, gate_tok, gain)
        per_clip(seg, dgate_tok, dmod_ref)
        dgain_ref[...] = dgain
        dlow = dbranch.astype(BF16)
        for_down.wait()
        dhidden = dot_t(dlow, wd_ref[...])
        gate, up = gate_ref[...], up_ref[...]
        sigma = jax.nn.sigmoid(gate)
        dup = (dhidden * gate * sigma).astype(BF16)
        dgate = (dhidden * up * (sigma * (1.0 + gate * (1.0 - sigma)))).astype(BF16)
        for start in range(0, width, cut):
            hidden_t = hidden_ref[:, start : start + cut].T
            gd_ref[start : start + cut, :] = dot(hidden_t, dlow).astype(BF16)
        for_gate.wait()
        part = dot_t(dgate, wg_ref[...])
        for_up.wait()
        part_ref[...] = (part + dot_t(dup, wu_ref[...])).astype(BF16)
        for start in range(0, depth, cut):
            in_t = in_ref[:, start : start + cut].T
            gg_ref[start : start + cut, :] = dot(in_t, dgate).astype(BF16)
            gu_ref[start : start + cut, :] = dot(in_t, dup).astype(BF16)

    def like(rows, columns, kind):
        return jax.ShapeDtypeStruct((rows, columns), kind)

    return pl.pallas_call(
        kernel,
        out_shape=(
            like(length, depth, BF16),
            like(length, depth, BF16),
            like(depth, width, BF16),
            like(depth, width, BF16),
            like(width, depth, BF16),
            like(clips, depth, F32),
            like(1, depth, F32),
        ),
        in_specs=[ANY] + [VMEM] * 10 + [ANY],
        out_specs=(VMEM,) * 7,
        scratch_shapes=[
            pltpu.VMEM((depth, width), BF16),
            pltpu.VMEM((depth, width), BF16),
            pltpu.VMEM((width, depth), BF16),
            pltpu.SemaphoreType.DMA((sum(counts) + 1,)),
        ],
        compiler_params=params(56),
    )(
        held, middle, ffn_out, cotangent, ffn_in, gate, up, hidden, seg, mods, norms, w_down
    )


def branch_backward(dffn_in, middle, cotangent, attn_out, seg, mods, norms, w_out):
    length, depth = middle.shape
    width = w_out.shape[0]
    clips = mods.shape[1]

    def kernel(
        din_ref, middle_ref, cot_ref, branch_ref, seg_ref, mod_ref, norm_ref, wo_ref,
        dmiddle_ref, dlow_ref, dmixed_ref, dscale_ref, dgate_ref, dnorm_ref,
    ):
        seg = seg_ref[...]
        dpre, dscale, dgain = modulate_back(
            din_ref[...].astype(F32), middle_ref[...], norm_ref[2:3, :], per_token(seg, mod_ref, 2)
        )
        per_clip(seg, dscale, dscale_ref)
        dnorm_ref[1:2, :] = dgain
        dmiddle = cot_ref[...].astype(F32) + dpre
        dmiddle_ref[...] = dmiddle
        dbranch, dgate_tok, dgain = branch_back(
            dmiddle, branch_ref[...].astype(F32), per_token(seg, mod_ref, 1), norm_ref[1:2, :]
        )
        per_clip(seg, dgate_tok, dgate_ref)
        dnorm_ref[0:1, :] = dgain
        dlow = dbranch.astype(BF16)
        dlow_ref[...] = dlow
        dmixed_ref[...] = dot_t(dlow, wo_ref[...]).astype(BF16)

    def like(rows, columns, kind):
        return jax.ShapeDtypeStruct((rows, columns), kind)

    return pl.pallas_call(
        kernel,
        out_shape=(
            like(length, depth, F32),
            like(length, depth, BF16),
            like(length, width, BF16),
            like(clips, depth, F32),
            like(clips, depth, F32),
            like(2, depth, F32),
        ),
        in_specs=[VMEM] * 8,
        out_specs=(VMEM,) * 6,
        compiler_params=params(48),
    )(dffn_in, middle, cotangent, attn_out, seg, mods, norms, w_out)


def attention_backward(
    layout, held, dmixed, query, key, value, q_lin, k_lin,
    text_key, text_value, tk_lin, cross, seg, seg_row, gains, cosine, sine, clips,
):
    length, width = query.shape
    depth = layout.width * lax.axis_size("mp")
    key_count = text_key.shape[0]
    count = len(layout.spans(0, 3 * depth))

    def kernel(
        held_ref, dmixed_ref, q_ref, k_ref, v_ref, q_lin_ref, k_lin_ref, tk_ref, tv_ref,
        tk_lin_ref, cross_ref, seg_ref, row_ref, gain_ref, cos_ref, sin_ref,
        part_ref, acts_ref, dgains_ref, w_ref, dq_ref, dk_ref, dv_ref, dtk_ref, dtv_ref, sems,
    ):
        fetch = Fetch(held_ref, layout, 0, 3 * depth, w_ref, sems, 0)
        opened = jnp.tanh(gain_ref[3:4, :])
        dmixed = dmixed_ref[...]
        wide = dmixed.astype(F32)
        dgains_ref[3:4, :] = column_sum(wide * cross_ref[...]) * (1.0 - opened * opened)
        dcross = (wide * opened).astype(BF16)
        own_mask, cross_mask = masks(seg_ref, row_ref, key_count, clips)
        for head in range(width // HEAD_DIM):
            at = slice(head * HEAD_DIM, (head + 1) * HEAD_DIM)
            query = q_ref[:, at]
            probs = soft(query, k_ref[:, at], own_mask)
            dq, dk, dv = soft_back(query, k_ref[:, at], v_ref[:, at], probs, dmixed[:, at])
            probs = soft(query, tk_ref[:, at], cross_mask)
            dq_cross, dtk, dtv = soft_back(
                query, tk_ref[:, at], tv_ref[:, at], probs, dcross[:, at]
            )
            dq_ref[:, at] = dq + dq_cross
            dk_ref[:, at] = dk
            dv_ref[:, at] = dv
            dtk_ref[:, at] = dtk
            dtv_ref[:, at] = dtv
        cosine, sine = cos_ref[...], sin_ref[...]
        lows = []
        for place, (grad_ref, lin_ref) in enumerate(((dq_ref, q_lin_ref), (dk_ref, k_lin_ref))):
            grad = grad_ref[...]
            grad = grad * cosine + turn(grad * sine, -1.0)
            dlin, dgain = head_rms_back(lin_ref[...], grad, gain_ref[place : place + 1, :])
            dgains_ref[place : place + 1, :] = dgain
            lows.append(dlin.astype(BF16))
        lows.append(dv_ref[...].astype(BF16))
        dlin, dgain = head_rms_back(tk_lin_ref[...], dtk_ref[...], gain_ref[2:3, :])
        dgains_ref[2:3, :] = dgain
        for place in range(3):
            acts_ref[place * length : (place + 1) * length, :] = lows[place]
        acts_ref[3 * length : 3 * length + key_count, :] = dlin.astype(BF16)
        acts_ref[3 * length + key_count :, :] = dtv_ref[...].astype(BF16)
        fetch.wait()
        part = dot_t(lows[0], w_ref[0:depth, :])
        part = part + dot_t(lows[1], w_ref[depth : 2 * depth, :])
        part_ref[...] = (part + dot_t(lows[2], w_ref[2 * depth : 3 * depth, :])).astype(BF16)

    return pl.pallas_call(
        kernel,
        out_shape=(
            jax.ShapeDtypeStruct((length, depth), BF16),
            jax.ShapeDtypeStruct((3 * length + 2 * key_count, width), BF16),
            jax.ShapeDtypeStruct((4, width), F32),
        ),
        in_specs=[ANY] + [VMEM] * 15,
        out_specs=(VMEM,) * 3,
        scratch_shapes=[pltpu.VMEM((3 * depth, width), BF16)]
        + [pltpu.VMEM((length, width), F32)] * 3
        + [pltpu.VMEM((key_count, width), F32)] * 2
        + [pltpu.SemaphoreType.DMA((count,))],
        compiler_params=params(56),
    )(
        held, dmixed, query, key, value, q_lin, k_lin, text_key, text_value, tk_lin, cross, seg,
        seg_row, gains, cosine, sine,
    )


def shard_gradient(layout, index, normed, dattn, text, mixed, acts, ends, cond):
    groups, packs, length, width = normed.shape
    key_count, text_cut = text.shape[2:]
    conds = cond.shape[1]
    cut = LANES
    step_packs = min(8, packs)
    blocks = layout.used // cut
    first = (index * layout.size // layout.unit * (layout.unit // width // cut)).astype(jnp.int32)
    per_in = groups * width // cut
    per_text = groups * text_cut // cut
    per_cond = cond.shape[2] // cut
    kinds = [3 * per_in, 4 * per_in, 4 * per_in + 2 * per_text, 4 * per_in + 2 * per_text + per_cond]

    def kernel(first_ref, n_ref, d_ref, t_ref, m_ref, a_ref, e_ref, c_ref, out_ref, woven_ref):
        @pl.when(pl.program_id(0) == 0)
        def _():
            out_ref[...] = jnp.zeros_like(out_ref)

        def tall(block):
            return block.reshape(-1, block.shape[-1])

        def body(i, carry):
            g = first_ref[0] + i
            start = pl.multiple_of(i * cut, cut)
            rows = pl.ds(start, cut)

            @pl.when(g < kinds[0])
            def _():
                sub = g % per_in
                lanes = pl.ds(pl.multiple_of(sub % (width // cut) * cut, cut), cut)
                grads = pl.ds(pl.multiple_of(g // per_in * length, length), length)
                left = tall(n_ref[sub // (width // cut), :, :, lanes])
                out_ref[rows, :] += t_dot(left, tall(a_ref[:, grads, :]))

            @pl.when((g >= kinds[0]) & (g < kinds[1]))
            def _():
                each = cut // groups
                at = (g - kinds[0]) * each
                lanes = pl.ds(pl.multiple_of(at // LANES * LANES, LANES), LANES)
                slab = tall(m_ref[:, length : 2 * length, lanes]).astype(F32)
                slab = pltpu.roll(slab, (LANES - at % LANES) % LANES, 1)
                left = slab.T[0:each, :].astype(BF16)
                for part in range(groups):
                    value = dot(left, tall(d_ref[part]))
                    for j in range(width // LANES):
                        woven_ref[j, pl.ds(part, each, stride=groups), :] = value[
                            :, j * LANES : (j + 1) * LANES
                        ]
                woven = [woven_ref[j] for j in range(width // LANES)]
                out_ref[rows, :] += jnp.concatenate(woven, 1)

            @pl.when((g >= kinds[1]) & (g < kinds[2]))
            def _():
                sub = (g - kinds[1]) % per_text
                lanes = pl.ds(pl.multiple_of(sub % (text_cut // cut) * cut, cut), cut)
                at = 3 * length + (g - kinds[1]) // per_text * key_count
                grads = pl.ds(pl.multiple_of(at, key_count), key_count)
                left = tall(t_ref[sub // (text_cut // cut), :, :, lanes])
                out_ref[rows, :] += t_dot(left, tall(a_ref[:, grads, :]))

            @pl.when((g >= kinds[2]) & (g < kinds[3]))
            def _():
                lanes = pl.ds(pl.multiple_of((g - kinds[2]) * cut, cut), cut)
                left = tall(c_ref[:, :, lanes])
                out_ref[rows, :] += t_dot(left, tall(e_ref[:, 0:conds, :]))

            @pl.when(g == kinds[3])
            def _():
                total = jnp.sum(e_ref[:, conds : conds + 16, :].astype(F32), 0)
                out_ref[pl.ds(start, 16), :] += total

            return carry

        lax.fori_loop(0, blocks, body, 0)

    def spec(array, packs_dim):
        shape = list(array.shape)
        shape[packs_dim] = step_packs
        return pl.BlockSpec(
            tuple(shape),
            lambda s: tuple(s if d == packs_dim else 0 for d in range(len(shape))),
            pipeline_mode=pl.Buffered(1),
        )

    operands = [(normed, 1), (dattn, 1), (text, 1), (mixed, 0), (acts, 0), (ends, 0), (cond, 0)]
    return pl.pallas_call(
        kernel,
        grid=(packs // step_packs,),
        out_shape=jax.ShapeDtypeStruct((layout.used, width), F32),
        in_specs=[SMEM] + [spec(*o) for o in operands],
        out_specs=pl.BlockSpec((layout.used, width), lambda s: (0, 0)),
        scratch_shapes=[pltpu.VMEM((width // LANES, cut, LANES), F32)],
        compiler_params=params(58),
    )(first[None], *[o[0] for o in operands])


def input_backward(dnormed, tokens, dmiddle, seg, mods, norms):
    length, depth = tokens.shape
    clips = mods.shape[1]

    def kernel(d_ref, x_ref, dmiddle_ref, seg_ref, mod_ref, norm_ref, out_ref, dmod_ref, dgain_ref):
        seg = seg_ref[...]
        dpre, dscale, dgain = modulate_back(
            d_ref[...].astype(F32),
            x_ref[...].astype(F32),
            norm_ref[0:1, :],
            per_token(seg, mod_ref, 0),
        )
        per_clip(seg, dscale, dmod_ref)
        dgain_ref[...] = dgain
        out_ref[...] = (dmiddle_ref[...] + dpre).astype(BF16)

    return pl.pallas_call(
        kernel,
        out_shape=(
            jax.ShapeDtypeStruct((length, depth), BF16),
            jax.ShapeDtypeStruct((clips, depth), F32),
            jax.ShapeDtypeStruct((1, depth), F32),
        ),
        in_specs=[VMEM] * 6,
        out_specs=(VMEM,) * 3,
        compiler_params=params(32),
    )(dnormed, tokens, dmiddle, seg, mods, norms)


def local(
    tokens_in,
    text_feats,
    frame_counts,
    time_steps,
    attn_master,
    attn_first,
    attn_second,
    ffn_master,
    ffn_first,
    ffn_second,
    norm_master,
    norm_first,
    norm_second,
    step_count,
    cotangent,
):
    parts, index = lax.axis_size("dp"), lax.axis_index("dp")
    length, model_width = tokens_in.shape
    width = model_width // lax.axis_size("mp")
    clip_slots, text_len, text_width = text_feats.shape[1:]
    key_count = clip_slots * text_len
    ring = Ring(parts)
    hidden_width = ffn_master.shape[1] * parts // (3 * model_width)
    attn_lay = Layout(attn_master.shape[1] * parts, width, parts, LANES)
    ffn_lay = Layout(ffn_master.shape[1] * parts, hidden_width, parts, TILE)
    norm_size = norm_master.shape[0]
    norm_rows = -(-norm_size // width)

    def as_rows(flat):
        flat = jnp.pad(flat, ((0, 0), (0, TILE * width - norm_size)))
        return flat.reshape(flat.shape[0], TILE, width)

    segment, positions = clip_layout(frame_counts[0], length, FRAME_TOK, clip_slots)
    seg, seg_row = segment[:, None], segment[None, :]
    cosine, sine = rope_tables(positions, HEAD_DIM, width // HEAD_DIM)
    rank = lax.axis_index("mp")

    def own_cut(values):
        size = values.shape[1] // lax.axis_size("mp")
        return lax.dynamic_slice_in_dim(values, rank * size, size, 1)

    text_rows = text_feats[0].reshape(key_count, text_width)

    sizes = [model_width] * 4 + [text_width, text_width, 4 * COND, 4]
    starts = [sum(sizes[:i]) for i in range(len(sizes) + 1)]
    attn_rows = to_rows(attn_lay, attn_master, index)
    ffn_piece = to_rows(ffn_lay, ffn_master, index)
    pieces = Pieces(attn_lay, starts[4], ring)
    digits = jnp.stack([time_steps[0] // 32, time_steps[0] % 32]).astype(BF16)
    near_text = own_cut(text_rows)
    digits = jnp.pad(digits, ((0, TILE - 2), (0, near_text.shape[1] - clip_slots)))
    text_run = Shared(ring, jnp.concatenate([near_text, digits], 0), index, key_count)
    last = starts[7] - attn_lay.base[parts - 1]
    pieces.send(attn_rows)
    for _ in range(3):
        join([text_run.send()])
    cosine, sine, ffn_piece = join([pieces, text_run.send()], cosine, sine, ffn_piece)
    attn_run = Gathering(
        ring,
        jnp.concatenate(
            [
                pieces.piece(index),
                as_rows(norm_master[None])[0].astype(BF16),
                attn_rows[last : last + TILE],
            ],
            0,
        ),
        index,
    )
    ffn_run = Gathering(ring, ffn_piece, index)
    attn_run.send()
    join([text_run.send()])
    text_own, text_far = text_run.both()
    digits = text_run.result()[:, key_count : key_count + 2, :clip_slots].astype(F32)
    cond_all = condition_rows(digits[:, 0] * 32.0 + digits[:, 1], COND)
    near = Once({"own": text_own, "far": text_far}, 1)
    mod_share = join(
        [attn_run, near],
        modulation_share(attn_lay, index, attn_rows, starts[6], cond_all),
    )
    attn_run.send()
    ffn_run.send()
    text_four = in_order({0: text_own, 2: text_far, 1: near.got["own"], 3: near.got["far"]})
    text_sum = Scattering(
        ring, text_share(attn_lay, index, attn_rows, starts[4], text_four), index
    )
    text_four = join([attn_run, ffn_run, text_sum.send()], text_four)
    attn_run.send()
    ffn_run.send()
    mod_local = lax.all_to_all(mod_share, "dp", 0, 0).sum(0)
    mods = join(
        [attn_run, ffn_run, text_sum.send()],
        lax.all_gather(mod_local.reshape(4, clip_slots, width), "mp", axis=2, tiled=True),
    )
    attn_run.send()
    ffn_run.send()
    join([text_sum.send()])
    join([attn_run, ffn_run, text_sum.send()])
    attn_all = attn_run.result()
    text_lin = text_sum.result()
    ffn_run.send()
    w_out = pieces.pick(attn_all, starts[3], starts[4]).reshape(width, model_width)
    gains = attn_all[parts - 1, pieces.rows + TILE : pieces.rows + TILE + 4].astype(F32)
    norm_flat = attn_all[:, pieces.rows : pieces.rows + norm_rows].reshape(parts, -1)
    norms = norm_flat[:, :norm_size].astype(F32).reshape(4, model_width)
    normed, query, key, value, q_lin, k_lin = attention_inputs(
        pieces, attn_all, tokens_in, seg, mods, norms, gains, cosine, sine
    )
    mixed, cross, attn_part, tk_lin, text_key, text_value = attention_forward(
        query, key, value, text_lin, seg, seg_row, gains, w_out, clip_slots
    )
    attn_out = join([ffn_run], sum_mp(attn_part))
    ffn_all = ffn_run.result()

    ffn_all, near_in = join([], ffn_all, jnp.concatenate([own_cut(normed), mixed], 0))
    w_down = ffn_lay.pick(ffn_all, 2 * model_width, 3 * model_width).reshape(
        hidden_width, model_width
    )
    in_run = Shared(ring, near_in, index, length)
    early = [in_run.send()]
    middle, ffn_in, gate, up, hidden, ffn_part = join(
        early,
        *ffn_forward(ffn_lay, ffn_all, tokens_in, attn_out, seg, mods, norms, w_down),
    )
    step(early)
    ffn_out = join(early, sum_mp(ffn_part))
    step(early)
    output, dffn_part, g_gate, g_up, g_down, dmod_gate_ffn, dnorm_four = join(
        early,
        *ffn_backward(
            ffn_lay,
            ffn_all,
            middle,
            ffn_out,
            cotangent,
            ffn_in,
            gate,
            up,
            hidden,
            seg,
            mods,
            norms,
            w_down,
        ),
    )
    ffn_grads = ffn_lay.cut([g_gate, g_up, g_down.reshape(model_width, hidden_width)])
    ffn_run = Scattering(ring, ffn_grads, index)
    step(early)
    (
        dmiddle,
        dattn,
        dmixed,
        dmod_scale_ffn,
        dmod_gate_attn,
        dnorm_mid,
    ) = join(
        early + [ffn_run.send()],
        *branch_backward(
            sum_mp(dffn_part), middle, cotangent, attn_out, seg, mods, norms, w_out
        ),
    )
    step(early)
    dattn_run = Shared(ring, own_cut(dattn), index, length)
    ffn_run.send()
    join([dattn_run.send()])
    dnormed_part, acts, gain_grads = join(
        [ffn_run, dattn_run.send()] + early,
        *attention_backward(
            pieces,
            attn_all,
            dmixed,
            query,
            key,
            value,
            q_lin,
            k_lin,
            text_key,
            text_value,
            tk_lin,
            cross,
            seg,
            seg_row,
            gains,
            cosine,
            sine,
            clip_slots,
        ),
    )
    acts_run = Gathering(ring, acts, index)
    in_own, in_far = in_run.both()
    ffn_run.send()
    acts_run.send()
    join([dattn_run.send()])
    dattn_run.send()
    dnormed = join([ffn_run, acts_run, dattn_run], sum_mp(dnormed_part))
    near = Once({"own": in_own, "far": in_far}, 1)
    input_grad, dmod_scale_attn, dnorm_one = join(
        [ffn_run.send(), acts_run.send(), dattn_run.send(), near],
        *input_backward(dnormed, tokens_in, dmiddle, seg, mods, norms),
    )
    dmods = jnp.concatenate([dmod_scale_attn, dmod_gate_attn, dmod_scale_ffn, dmod_gate_ffn], 0)
    norm_grads = jnp.concatenate([dnorm_one, dnorm_mid, dnorm_four], 0)
    ends = jnp.concatenate(
        [
            own_cut(dmods),
            jnp.pad(gain_grads, ((0, TILE - 4), (0, 0))),
            norm_grads.reshape(-1, width),
        ],
        0,
    ).astype(BF16)
    normed_four = in_order({0: in_own, 2: in_far, 1: near.got["own"], 3: near.got["far"]})
    dattn_own, dattn_far = dattn_run.both()
    near = Once({"own": dattn_own, "far": dattn_far}, 1)
    ends_all, ffn_shard, normed_four = join(
        [acts_run.send(), near],
        gather_small(ends[None], parts),
        to_flat(ffn_lay, ffn_run.result(), index),
        normed_four,
    )
    dattn_four = in_order(
        {0: dattn_own, 2: dattn_far, 1: near.got["own"], 3: near.got["far"]}
    )
    step_value = step_count[0].astype(F32)
    dattn_four, *ffn_result = join(
        [acts_run.send()],
        dattn_four,
        *adamw_flat(ffn_lay, ffn_master, ffn_first, ffn_second, ffn_shard, step_value, RATE),
    )
    attn_sum = shard_gradient(
        attn_lay,
        index,
        normed_four,
        dattn_four,
        text_four,
        in_run.result(),
        acts_run.result(),
        ends_all,
        cond_all,
    )
    attn_shard = to_flat(attn_lay, attn_sum, index)
    norm_sum = ends_all[:, 2 * TILE :].astype(F32).sum(0).reshape(-1)
    norm_shard = lax.dynamic_slice_in_dim(norm_sum, index * norm_size, norm_size, 0)
    attn_result = adamw_flat(
        attn_lay, attn_master, attn_first, attn_second, attn_shard, step_value, RATE
    )
    norm_result = adamw(norm_master, norm_first, norm_second, norm_shard, step_value, RATE_NORM)
    return (
        (output, input_grad)
        + tuple(attn_result)
        + tuple(ffn_result)
        + norm_result
        + (gain_grads[3:4],)
    )


def solution(mesh):
    tokens, flat, norm = P("dp", None), P("mp", "dp"), P("dp")
    return jax.shard_map(
        local,
        mesh=mesh,
        in_specs=(tokens, P("dp", None, None, None), tokens, tokens)
        + (flat,) * 6
        + (norm,) * 3
        + (P(), tokens),
        out_specs=(tokens,) * 2 + (flat,) * 10 + (norm,) * 5 + (P("dp", "mp"),),
        check_vma=False,
    )
```

time: 3100 us -> 637 us (0.21)
  waiting for transfers between devices: 1950 us -> 212 us
  local copies, waits for them, and re-layouts: 731 us -> 140 us
  matrix products: 156 us -> 0 us
  starting transfers between devices: 0.91 us -> 115 us
  other arithmetic: 152 us -> 42.3 us
  Pallas kernels: 0 us -> 107 us
  blocking collectives: 70.3 us -> 5.34 us
    unnamed x11 -> x0, waiting for transfers between devices: 1520 us -> none
    all_gather x1 -> x0, waiting for transfers between devices: 358 us -> none  [local(): lax.all_gather(ffn_master.astype(jnp.bfloat16), 'dp', axis=1, tiled=True)]
    unnamed x278 -> x152, local copies, waits for them, and re-layouts: 374 us -> 16.8 us
    slice x8 -> x6, local copies, waits for them, and re-layouts: 231 us -> 5.19 us  [the longest x2 3.7 us: both(): own = self.result()[:, :self.share]]
    ppermute x0 -> x92, waiting for transfers between devices: none -> 202 us  [the longest x24 96.2 us: onward(): return lax.ppermute(block, 'dp', self.next)]
    dot_general x119 -> x0, matrix products: 156 us -> none  [the longest x12 18.8 us: attend_back(): jnp.dot(grad_scores.T, query, preferred_element_type=jnp.float32)]
    pallas_call x0 -> x16, Pallas kernels: none -> 107 us  [the longest x2 24.1 us: adamw_flat(): pl.pallas_call(kernel, grid=(steps,), out_shape=(like, like, like, like,...]
    ppermute x0 -> x92, starting transfers between devices: none -> 105 us  [the longest x32 37 us: swap(): return lax.ppermute(block, 'dp', self.pair)]
  transfers between devices with their start and end apart: 8 -> 93, of which waited for: 7 -> 33; matrix products, arithmetic and copies ran while one was open for 10% -> 24% of each run, Pallas kernels for 0% -> 11%
where the time goes in v1:
time: 637 us; the launch traced here: 626 us
  waiting for transfers between devices  212 us (33%)
  local copies, waits for them, and re-layouts  140 us (22%)
  starting transfers between devices  115 us (18%)
  Pallas kernels  107 us (17%)
  other arithmetic  42.3 us (7%)
    ppermute x24, waiting for transfers between devices, onward(): return lax.ppermute(block, 'dp', self.next)  96.2 us
    ppermute x32, waiting for transfers between devices, swap(): return lax.ppermute(block, 'dp', self.pair)  53 us
    dynamic_update_slice x46, local copies, waits for them, and re-layouts, put(): lax.dynamic_update_slice(self.held, value[None, None], (slot, side) + (se...  43.9 us
    ppermute x32, starting transfers between devices, swap(): return lax.ppermute(block, 'dp', self.pair)  37 us
    ppermute x24, starting transfers between devices, onward(): return lax.ppermute(block, 'dp', self.next)  34.9 us
    pallas_call x2, Pallas kernels, adamw_flat(): pl.pallas_call(kernel, grid=(steps,), out_shape=(like, like, like, like,...  24.1 us
    ppermute x12, waiting for transfers between devices, send(): self.sent['far'] = lax.ppermute(self.chunk, 'mp', pairs)  24 us
    pallas_call x1, Pallas kernels, shard_gradient(): pl.pallas_call(kernel, grid=(packs // step_packs,), out_shape=jax.ShapeDt...  21.3 us
  transfers between devices with their start and end apart: 93, of which 33 were waited for; matrix products, arithmetic and copies ran while one was open for 24% of the time, Pallas kernels for 11%

profile of v1, /device:TPU:8, one launch (start us, length us, event | category | flops | bytes accessed | tf_op | source)
XLA Modules:
  0.0 625.8 jit_solution(8866993320044979971)
XLA Ops:
  7.3 2.4 collective-permute-start
  22.2 4.6 collective-permute-start.1
  32.6 25.6 %collective-permute-done.5 = bf16[144,1024]{1,0:T(8,128)(2,1)S(1)} collective-permute-done((bf16[144,1024]{1,0:T(8,128)(2,1)}, bf16[144,1024]{1,0:T(8,128)(2,1)S(1)}, u32[]{:S(2)}, u32[]{:S(2)}) %collective-permute-start.5) | collective-permute-done | bytes 294944 | tf_op jit(solution)/shard_map/ppermute | solution.py:294
  68.3 5.1 collective-permute-done.9
  78.4 2.8 collective-permute-done.12
  81.2 6.2 collective-permute-done.11
  94.9 8.3 %collective-permute-done.15 = bf16[2,128,1024]{2,1,0:T(8,128)(2,1)S(1)} collective-permute-done((bf16[2,128,1024]{2,1,0:T(8,128)(2,1)S(1)}, bf16[2,128,1024]{2,1,0:T(8,128)(2,1)S(1)}, u32[]{:S(2)}, u32[]{:S(2)}) %collective-permute-start.15) | collective-permute-done | bytes 524320 | tf_op jit(solution)/shard_map/ppermute | solution.py:369
  104.6 4.3 fusion.7
  110.4 2.1 broadcast_in_dim.318
  125.6 3.2 copy-done.38
  128.8 6.5 %shard_map.289 = bf16[8,128,768]{2,1,0:T(8,128)(2,1)S(1)} custom-call(s32[2]{0:T(128)S(1)} %pad_add_fusion.place_ref, bf16[2432,384]{1,0:T(8,128)(2,1)S(1)} %shard_map.286.w_ref, bf16[4,8,128,1024]{3,2,1,0:T(8,128)(2,1)} %copy-done.38), custom_call_target="tpu_custom_call" | custom-call | tf_op jit(solution)/shard_map/pallas_call | solution.py:760
  136.5 5.4 collective-permute-start.22
  141.9 9.8 %all-to-all-start = ((f32[8,16,384]{2,1,0:T(8,128)}), f32[8,16,384]{2,1,0:T(8,128)S(1)}, u32[]{:S(2)}, u32[]{:S(2)}) async-start(f32[8,16,384]{2,1,0:T(8,128)} %bitcast.35), calls=%async_computation | async-start | bytes 393216 | tf_op jit(solution)/shard_map/all_to_all | solution.py:1328
  151.7 2.6 broadcast_in_dim.330
  157.2 10.2 %all-to-all-done = f32[8,16,384]{2,1,0:T(8,128)S(1)} async-done(((f32[8,16,384]{2,1,0:T(8,128)}), f32[8,16,384]{2,1,0:T(8,128)S(1)}, u32[]{:S(2)}, u32[]{:S(2)}) %all-to-all-start) | async-done | bytes 196640 | tf_op jit(solution)/shard_map/all_to_all | solution.py:1328
  167.4 5.3 all_gather.3.mod_ref
  175.2 6.0 collective-permute-start.25
  190.8 28.7 %collective-permute-done.27 = bf16[128,768]{1,0:T(8,128)(2,1)S(1)} collective-permute-done((bf16[128,768]{1,0:T(8,128)(2,1)S(1)}, bf16[128,768]{1,0:T(8,128)(2,1)S(1)}, u32[]{:S(2)}, u32[]{:S(2)}) %collective-permute-start.27) | collective-permute-done | bytes 196640 | tf_op jit(solution)/shard_map/ppermute | solution.py:294
  220.5 3.8 collective-permute-start.30
  227.3 2.5 collective-permute-start.32
  234.0 21.5 %collective-permute-done.32 = bf16[128,768]{1,0:T(8,128)(2,1)S(1)} collective-permute-done((bf16[128,768]{1,0:T(8,128)(2,1)S(1)}, bf16[128,768]{1,0:T(8,128)(2,1)S(1)}, u32[]{:S(2)}, u32[]{:S(2)}) %collective-permute-start.32) | collective-permute-done | bytes 196640 | tf_op jit(solution)/shard_map/ppermute | solution.py:294
  258.6 9.6 %collective-permute-done.35 = bf16[128,768]{1,0:T(8,128)(2,1)S(1)} collective-permute-done((bf16[128,768]{1,0:T(8,128)(2,1)S(1)}, bf16[128,768]{1,0:T(8,128)(2,1)S(1)}, u32[]{:S(2)}, u32[]{:S(2)}) %collective-permute-start.35) | collective-permute-done | bytes 196640 | tf_op jit(solution)/shard_map/ppermute | solution.py:291
  275.9 2.4 reshape.289.w_ref.wo_ref
  279.4 3.8 shard_map.290
  284.6 4.6 shard_map.291
  293.6 4.3 collective-permute-done.38
  300.3 2.5 bitcast_dynamic-update-slice_fusion.5
  302.8 2.4 bitcast_dynamic-update-slice_fusion.4
  305.2 3.5 collective-permute-start.40
  314.8 5.9 reshape.291.down_hbm
  320.7 6.6 %shard_map.292 = (f32[128,1536]{1,0:T(8,128)}, bf16[128,1536]{1,0:T(8,128)(2,1)}, f32[128,1024]{1,0:T(8,128)}, f32[128,1024]{1,0:T(8,128)}, bf16[128,1024]{1,0:T(8,128)(2,1)}, /*index=5*/bf16[128,1536]{1,0:T(8,128)(2,1)}) custom-call(bf16[8,576,1024]{2,1,0:T(8,128)(2,1)} %bitcast.313, bf16[128,1536]{1,0:T(8,128)(2,1)} %x_ref.9, ...), custom_call_target="tpu_custom_call" | custom-call | tf_op jit(solution)/shard_map/pallas_call | solution.py:896
  327.3 2.5 collective-permute-start.42
  336.8 6.1 collective-permute-done.46
  345.3 3.0 collective-permute-start.48
  351.3 13.5 %shard_map.293 = (bf16[128,1536]{1,0:T(8,128)(2,1)}, bf16[128,1536]{1,0:T(8,128)(2,1)}, bf16[1536,1024]{1,0:T(8,128)(2,1)}, bf16[1536,1024]{1,0:T(8,128)(2,1)}, ...) custom-call(bf16[8,576,1024]{2,1,0:T(8,128)(2,1)} %bitcast.314, ...), custom_call_target="tpu_custom_call" | custom-call | tf_op jit(solution)/shard_map/pallas_call | solution.py:968
  368.9 5.9 reshape.292
  374.8 4.9 pad_maximum_fusion
  381.6 2.4 copy-done.39
  388.5 6.4 %collective-permute-done.55 = bf16[64,1536]{1,0:T(8,128)(2,1)S(1)} collective-permute-done((bf16[64,1536]{1,0:T(8,128)(2,1)S(1)}, bf16[64,1536]{1,0:T(8,128)(2,1)S(1)}, u32[]{:S(2)}, u32[]{:S(2)}) %collective-permute-start.55) | collective-permute-done | bytes 196640 | tf_op jit(solution)/shard_map/ppermute | solution.py:515
  396.6 2.9 shard_map.294
  399.5 13.6 %collective-permute-done.53 = bf16[576,1024]{1,0:T(8,128)(2,1)S(1)} collective-permute-done((bf16[576,1024]{1,0:T(8,128)(2,1)S(1)}, bf16[576,1024]{1,0:T(8,128)(2,1)S(1)}, u32[]{:S(2)}, u32[]{:S(2)}) %collective-permute-start.53) | collective-permute-done | bytes 1179680 | tf_op jit(solution)/shard_map/ppermute | solution.py:291
  414.2 2.8 fusion.1
  420.0 2.1 slice.284
  422.1 11.3 %shard_map.295 = (bf16[128,1536]{1,0:T(8,128)(2,1)}, bf16[640,384]{1,0:T(8,128)(2,1)}, f32[4,384]{1,0:T(4,128)}) custom-call(bf16[8,800,384]{2,1,0:T(8,128)(2,1)} %bitcast.61.held_ref, bf16[128,384]{1,0:T(8,128)(2,1)} %copy-done.35, bf16[128,384]{1,0:T(8,128)(2,1)} %copy-done.25, bf16[128,384]{1,0:T(8,128)(2,1)} %copy-done.26, bf16[128,384]{1,0:T(8,128)(2,1)} %copy-done.27, ...), custom_call_target="tpu_custom_call" | custom-call | tf_op jit(solution)/shard_map/pallas_call | solution.py:1093
  444.9 2.7 collective-permute-done.63
  447.6 2.5 collective-permute-start.69
  456.3 2.8 fusion.3
  459.4 12.8 %collective-permute-done.71 = bf16[128,384]{1,0:T(8,128)(2,1)S(1)} collective-permute-done((bf16[128,384]{1,0:T(8,128)(2,1)S(1)}, bf16[128,384]{1,0:T(8,128)(2,1)S(1)}, u32[]{:S(2)}, u32[]{:S(2)}) %collective-permute-start.71) | collective-permute-done | bytes 98336 | tf_op jit(solution)/shard_map/ppermute | solution.py:291
  473.1 2.8 collective-permute-start.65
  478.6 3.2 collective-permute-done.75
  484.8 3.8 collective-permute-done.73
  490.8 7.4 %collective-permute-done.65 = bf16[576,1024]{1,0:T(8,128)(2,1)S(1)} collective-permute-done((bf16[576,1024]{1,0:T(8,128)(2,1)S(1)}, bf16[576,1024]{1,0:T(8,128)(2,1)S(1)}, u32[]{:S(2)}, u32[]{:S(2)}) %collective-permute-start.65) | collective-permute-done | bytes 1179680 | tf_op jit(solution)/shard_map/ppermute | solution.py:294
  503.7 2.1 broadcast.224.clone.1
  507.9 2.2 broadcast_in_dim.364
  511.7 3.8 collective-permute-done.78
  521.5 3.5 collective-permute-done.81
  525.0 11.7 %collective-permute-done.79 = bf16[640,384]{1,0:T(8,128)(2,1)} collective-permute-done((bf16[640,384]{1,0:T(8,128)(2,1)S(1)}, bf16[640,384]{1,0:T(8,128)(2,1)}, u32[]{:S(2)}, u32[]{:S(2)}) %collective-permute-start.79) | collective-permute-done | bytes 491552 | tf_op jit(solution)/shard_map/ppermute | solution.py:294
  540.7 2.3 fusion.x_ref
  551.3 3.4 collective-permute-start.90
  556.4 2.7 bitcast_dynamic-update-slice_fusion.14
  567.8 9.5 %shard_map.298 = (f32[1,589824]{1,0:T(1,128)}, f32[1,589824]{1,0:T(1,128)}, f32[1,589824]{1,0:T(1,128)}, f32[1,589824]{1,0:T(1,128)}, bf16[1,589824]{1,0:T(2,128)(2,1)}) custom-call(f32[2]{0:T(128)S(1)} %pad_maximum_fusion.24.fix_ref, f32[1,589824]{1,0:T(1,128)S(1)} %copy-done.8, f32[1,589824]{1,0:T(1,128)S(1)} %copy-done.19, f32[1,589824]{1,0:T(1,128)} %v_ref.2, ...), custom_call_target="tpu_custom_call" | custom-call | tf_op jit(solution)/shard_map/pallas_call | solution.py:271
  582.8 21.3 %shard_map.299.x_ref = f32[2432,384]{1,0:T(8,128)} custom-call(s32[1]{0:T(128)} %bitcast.33.first_ref, bf16[4,8,128,384]{3,2,1,0:T(8,128)(2,1)} %bitcast_dynamic-update-slice_fusion.16.n_ref, bf16[4,8,128,384]{3,2,1,0:T(8,128)(2,1)} %bitcast_dynamic-update-slice_fusion.12.d_ref, bf16[4,8,128,1024]{3,2,1,0:T(8,128)(2,1)} %copy-done.38, ...), custom_call_target="tpu_custom_call" | custom-call | tf_op jit(solution)/shard_map/pallas_call | solution.py:1198
  604.2 4.8 shard_map.300.g_ref
  610.8 14.5 %shard_map.301 = (f32[1,884928]{1,0:T(1,128)}, f32[1,884928]{1,0:T(1,128)}, f32[1,884928]{1,0:T(1,128)}, f32[1,884928]{1,0:T(1,128)}, bf16[1,884928]{1,0:T(2,128)(2,1)}) custom-call(f32[2]{0:T(128)S(1)} %pad_maximum_fusion.24.fix_ref, f32[1,884928]{1,0:T(1,128)S(1)} %copy-done.4, f32[1,884928]{1,0:T(1,128)} %m_ref.3, f32[1,884928]{1,0:T(1,128)} %v_ref.3, ...), custom_call_target="tpu_custom_call" | custom-call | tf_op jit(solution)/shard_map/pallas_call | solution.py:271
  (521 shorter events, 212.1 us)
Async XLA Ops:
  3.4 24.2 %collective-permute-start.3 = (bf16[144,1024]{1,0:T(8,128)(2,1)}, bf16[144,1024]{1,0:T(8,128)(2,1)}, u32[]{:S(2)}, u32[]{:S(2)}) collective-permute-start(bf16[144,1024]{1,0:T(8,128)(2,1)} %pad_maximum_fusion.12), channel_id=1, source_target_pairs={{0,8},{4,12},{8,16},{12,20},{16,24},{20,28},{24,0},{28,4},{1,9},{5... | collective-permute-start | bytes 884744 | tf_op jit(solution)/shard_map/ppermute | solution.py:294
  4.9 22.6 %collective-permute-start.4 = (bf16[144,1024]{1,0:T(8,128)(2,1)}, bf16[144,1024]{1,0:T(8,128)(2,1)}, u32[]{:S(2)}, u32[]{:S(2)}) collective-permute-start(bf16[144,1024]{1,0:T(8,128)(2,1)} %pad_maximum_fusion.12), channel_id=1, source_target_pairs={{0,4},{4,0},{8,12},{12,8},{16,20},{20,16},{24,28},{28,24},{1,5},{5... | collective-permute-start | bytes 884744 | tf_op jit(solution)/shard_map/ppermute | solution.py:291
  22.2 56.1 %collective-permute-start.1 = (bf16[768,384]{1,0:T(8,128)(2,1)S(1)}, bf16[768,384]{1,0:T(8,128)(2,1)S(1)}, u32[]{:S(2)}, u32[]{:S(2)}) collective-permute-start(bf16[768,384]{1,0:T(8,128)(2,1)S(1)} %get-tuple-element.366), channel_id=1, source_target_pairs={{0,24},{4,28},{8,12},{1,25},{5,29},{9,13},{2,26},{6,30},{10,14},{3... | collective-permute-start | bytes 1769480 | tf_op jit(solution)/shard_map/ppermute | solution.py:105
  26.8 51.5 %collective-permute-start.2 = (bf16[768,384]{1,0:T(8,128)(2,1)S(1)}, bf16[768,384]{1,0:T(8,128)(2,1)S(1)}, u32[]{:S(2)}, u32[]{:S(2)}) collective-permute-start(bf16[768,384]{1,0:T(8,128)(2,1)S(1)} %get-tuple-element.365), channel_id=1, source_target_pairs={{0,16},{4,20},{1,17},{5,21},{2,18},{6,22},{3,19},{7,23}} | collective-permute-start | bytes 1769480 | tf_op jit(solution)/shard_map/ppermute | solution.py:105
  27.6 30.7 %collective-permute-start.5 = (bf16[144,1024]{1,0:T(8,128)(2,1)}, bf16[144,1024]{1,0:T(8,128)(2,1)S(1)}, u32[]{:S(2)}, u32[]{:S(2)}) collective-permute-start(bf16[144,1024]{1,0:T(8,128)(2,1)} %collective-permute-done.3), channel_id=1, source_target_pairs={{0,8},{4,12},{8,16},{12,20},{16,24},{20,28},{24,0},{28,4},{1,9},{5... | collective-permute-start | bytes 884744 | tf_op jit(solution)/shard_map/ppermute | solution.py:294
  27.6 30.6 %collective-permute-start.7 = (bf16[144,1024]{1,0:T(8,128)(2,1)}, bf16[144,1024]{1,0:T(8,128)(2,1)S(1)}, u32[]{:S(2)}, u32[]{:S(2)}) collective-permute-start(bf16[144,1024]{1,0:T(8,128)(2,1)} %collective-permute-done.3), channel_id=1, source_target_pairs={{0,4},{4,0},{8,12},{12,8},{16,20},{20,16},{24,28},{28,24},{1,5},{5... | collective-permute-start | bytes 884744 | tf_op jit(solution)/shard_map/ppermute | solution.py:291
  28.8 29.5 %collective-permute-start.6 = (bf16[2,128,1024]{2,1,0:T(8,128)(2,1)S(1)}, bf16[2,128,1024]{2,1,0:T(8,128)(2,1)S(1)}, u32[]{:S(2)}, u32[]{:S(2)}) collective-permute-start(bf16[2,128,1024]{2,1,0:T(8,128)(2,1)S(1)} %pad_maximum_fusion.4), channel_id=1, source_target_pairs={{0,2},{1,3},{2,0},{3,1},{4,6},{5,7},{6,4},{7,5},{8,10},{9,11},{10,... | collective-permute-start | bytes 1572872 | tf_op jit(solution)/shard_map/ppermute | solution.py:369
  59.8 13.6 %collective-permute-start.9 = (bf16[2,128,1024]{2,1,0:T(8,128)(2,1)S(1)}, bf16[2,128,1024]{2,1,0:T(8,128)(2,1)S(1)}, u32[]{:S(2)}, u32[]{:S(2)}) collective-permute-start(bf16[2,128,1024]{2,1,0:T(8,128)(2,1)S(1)} %pad_maximum_fusion.5), channel_id=1, source_target_pairs={{0,2},{1,3},{2,0},{3,1},{4,6},{5,7},{6,4},{7,5},{8,10},{9,11},{10,... | collective-permute-start | bytes 1572872 | tf_op jit(solution)/shard_map/ppermute | solution.py:369
  88.4 31.1 %collective-permute-start.13 = (bf16[800,384]{1,0:T(8,128)(2,1)}, bf16[800,384]{1,0:T(8,128)(2,1)S(1)}, u32[]{:S(2)}, u32[]{:S(2)}) collective-permute-start(bf16[800,384]{1,0:T(8,128)(2,1)} %pad_maximum_fusion.3), channel_id=1, source_target_pairs={{0,8},{4,12},{8,16},{12,20},{16,24},{20,28},{24,0},{28,4},{1,9},{5... | collective-permute-start | bytes 1843208 | tf_op jit(solution)/shard_map/ppermute | solution.py:294
  89.1 31.6 %collective-permute-start.14 = (bf16[800,384]{1,0:T(8,128)(2,1)}, bf16[800,384]{1,0:T(8,128)(2,1)}, u32[]{:S(2)}, u32[]{:S(2)}) collective-permute-start(bf16[800,384]{1,0:T(8,128)(2,1)} %pad_maximum_fusion.3), channel_id=1, source_target_pairs={{0,4},{4,0},{8,12},{12,8},{16,20},{20,16},{24,28},{28,24},{1,5},{5... | collective-permute-start | bytes 1843208 | tf_op jit(solution)/shard_map/ppermute | solution.py:291
  93.4 27.3 %collective-permute-start.17 = (bf16[8,128,1024]{2,1,0:T(8,128)(2,1)}, bf16[8,128,1024]{2,1,0:T(8,128)(2,1)}, u32[]{:S(2)}, u32[]{:S(2)}) collective-permute-start(bf16[8,128,1024]{2,1,0:T(8,128)(2,1)} %slice.276), channel_id=1, source_target_pairs={{0,1},{1,0},{2,3},{3,2},{4,5},{5,4},{6,7},{7,6},{8,9},{9,8},{10,11... | collective-permute-start | bytes 6291464 | tf_op jit(solution)/shard_map/ppermute | solution.py:458
  104.6 16.1 %collective-permute-start.16 = (bf16[8,128,1024]{2,1,0:T(8,128)(2,1)}, bf16[8,128,1024]{2,1,0:T(8,128)(2,1)}, u32[]{:S(2)}, u32[]{:S(2)}) collective-permute-start(bf16[8,128,1024]{2,1,0:T(8,128)(2,1)} %bitcast.23), channel_id=1, source_target_pairs={{0,1},{1,0},{2,3},{3,2},{4,5},{5,4},{6,7},{7,6},{8,9},{9,8},{10,11... | collective-permute-start | bytes 6291464 | tf_op jit(solution)/shard_map/ppermute | solution.py:458
  112.5 60.3 %collective-permute-start.20 = (bf16[576,1024]{1,0:T(8,128)(2,1)}, bf16[576,1024]{1,0:T(8,128)(2,1)}, u32[]{:S(2)}, u32[]{:S(2)}) collective-permute-start(bf16[576,1024]{1,0:T(8,128)(2,1)} %shard_map.287), channel_id=1, source_target_pairs={{0,8},{4,12},{8,16},{12,20},{16,24},{20,28},{24,0},{28,4},{1,9},{5... | collective-permute-start | bytes 3538952 | tf_op jit(solution)/shard_map/ppermute | solution.py:294
  119.5 54.3 %collective-permute-start.21 = (bf16[576,1024]{1,0:T(8,128)(2,1)}, bf16[576,1024]{1,0:T(8,128)(2,1)}, u32[]{:S(2)}, u32[]{:S(2)}) collective-permute-start(bf16[576,1024]{1,0:T(8,128)(2,1)} %shard_map.287), channel_id=1, source_target_pairs={{0,4},{4,0},{8,12},{12,8},{16,20},{20,16},{24,28},{28,24},{1,5},{5... | collective-permute-start | bytes 3538952 | tf_op jit(solution)/shard_map/ppermute | solution.py:291
  120.7 53.2 %collective-permute-start.18 = (bf16[800,384]{1,0:T(8,128)(2,1)S(1)}, bf16[800,384]{1,0:T(8,128)(2,1)}, u32[]{:S(2)}, u32[]{:S(2)}) collective-permute-start(bf16[800,384]{1,0:T(8,128)(2,1)S(1)} %collective-permute-done.13), channel_id=1, source_target_pairs={{0,8},{4,12},{8,16},{12,20},{16,24},{20,28},{24,0},{28,4},{1,9},{5... | collective-permute-start | bytes 1843208 | tf_op jit(solution)/shard_map/ppermute | solution.py:294
  120.8 53.1 %collective-permute-start.19 = (bf16[800,384]{1,0:T(8,128)(2,1)S(1)}, bf16[800,384]{1,0:T(8,128)(2,1)}, u32[]{:S(2)}, u32[]{:S(2)}) collective-permute-start(bf16[800,384]{1,0:T(8,128)(2,1)S(1)} %collective-permute-done.13), channel_id=1, source_target_pairs={{0,4},{4,0},{8,12},{12,8},{16,20},{20,16},{24,28},{28,24},{1,5},{5... | collective-permute-start | bytes 1843208 | tf_op jit(solution)/shard_map/ppermute | solution.py:291
  136.5 37.4 %collective-permute-start.22 = (bf16[128,768]{1,0:T(8,128)(2,1)S(1)}, bf16[128,768]{1,0:T(8,128)(2,1)S(1)}, u32[]{:S(2)}, u32[]{:S(2)}) collective-permute-start(bf16[128,768]{1,0:T(8,128)(2,1)S(1)} %get-tuple-element.370), channel_id=1, source_target_pairs={{0,4},{4,0},{8,12},{12,8},{16,20},{20,16},{24,28},{28,24},{1,5},{5... | collective-permute-start | bytes 589832 | tf_op jit(solution)/shard_map/ppermute | solution.py:291
  141.9 25.5 %all-to-all-start = ((f32[8,16,384]{2,1,0:T(8,128)}), f32[8,16,384]{2,1,0:T(8,128)S(1)}, u32[]{:S(2)}, u32[]{:S(2)}) async-start(f32[8,16,384]{2,1,0:T(8,128)} %bitcast.35), calls=%async_computation | async-start | bytes 393216 | tf_op jit(solution)/shard_map/all_to_all | solution.py:1328
  172.8 17.0 %collective-permute-start.28 = (bf16[128,768]{1,0:T(8,128)(2,1)S(1)}, bf16[128,768]{1,0:T(8,128)(2,1)S(1)}, u32[]{:S(2)}, u32[]{:S(2)}) collective-permute-start(bf16[128,768]{1,0:T(8,128)(2,1)S(1)} %get-tuple-element.369), channel_id=1, source_target_pairs={{0,4},{4,0},{8,12},{12,8},{16,20},{20,16},{24,28},{28,24},{1,5},{5... | collective-permute-start | bytes 589832 | tf_op jit(solution)/shard_map/ppermute | solution.py:291
  173.9 46.5 %collective-permute-start.23 = (bf16[800,384]{1,0:T(8,128)(2,1)}, bf16[800,384]{1,0:T(8,128)(2,1)S(1)}, u32[]{:S(2)}, u32[]{:S(2)}) collective-permute-start(bf16[800,384]{1,0:T(8,128)(2,1)} %collective-permute-done.18), channel_id=1, source_target_pairs={{0,8},{4,12},{8,16},{12,20},{16,24},{20,28},{24,0},{28,4},{1,9},{5... | collective-permute-start | bytes 1843208 | tf_op jit(solution)/shard_map/ppermute | solution.py:294
  174.2 46.2 %collective-permute-start.24 = (bf16[800,384]{1,0:T(8,128)(2,1)}, bf16[800,384]{1,0:T(8,128)(2,1)S(1)}, u32[]{:S(2)}, u32[]{:S(2)}) collective-permute-start(bf16[800,384]{1,0:T(8,128)(2,1)} %collective-permute-done.18), channel_id=1, source_target_pairs={{0,4},{4,0},{8,12},{12,8},{16,20},{20,16},{24,28},{28,24},{1,5},{5... | collective-permute-start | bytes 1843208 | tf_op jit(solution)/shard_map/ppermute | solution.py:291
  175.2 45.3 %collective-permute-start.25 = (bf16[576,1024]{1,0:T(8,128)(2,1)}, bf16[576,1024]{1,0:T(8,128)(2,1)S(1)}, u32[]{:S(2)}, u32[]{:S(2)}) collective-permute-start(bf16[576,1024]{1,0:T(8,128)(2,1)} %collective-permute-done.20), channel_id=1, source_target_pairs={{0,8},{4,12},{8,16},{12,20},{16,24},{20,28},{24,0},{28,4},{1,9},{5... | collective-permute-start | bytes 3538952 | tf_op jit(solution)/shard_map/ppermute | solution.py:294
  181.1 39.3 %collective-permute-start.26 = (bf16[576,1024]{1,0:T(8,128)(2,1)}, bf16[576,1024]{1,0:T(8,128)(2,1)S(1)}, u32[]{:S(2)}, u32[]{:S(2)}) collective-permute-start(bf16[576,1024]{1,0:T(8,128)(2,1)} %collective-permute-done.20), channel_id=1, source_target_pairs={{0,4},{4,0},{8,12},{12,8},{16,20},{20,16},{24,28},{28,24},{1,5},{5... | collective-permute-start | bytes 3538952 | tf_op jit(solution)/shard_map/ppermute | solution.py:291
  189.7 29.7 %collective-permute-start.27 = (bf16[128,768]{1,0:T(8,128)(2,1)S(1)}, bf16[128,768]{1,0:T(8,128)(2,1)S(1)}, u32[]{:S(2)}, u32[]{:S(2)}) collective-permute-start(bf16[128,768]{1,0:T(8,128)(2,1)S(1)} %fusion.13), channel_id=1, source_target_pairs={{0,8},{4,12},{8,16},{12,20},{16,24},{20,28},{24,0},{28,4},{1,9},{5... | collective-permute-start | bytes 589832 | tf_op jit(solution)/shard_map/ppermute | solution.py:294
  220.5 47.7 %collective-permute-start.30 = (bf16[576,1024]{1,0:T(8,128)(2,1)S(1)}, bf16[576,1024]{1,0:T(8,128)(2,1)}, u32[]{:S(2)}, u32[]{:S(2)}) collective-permute-start(bf16[576,1024]{1,0:T(8,128)(2,1)S(1)} %collective-permute-done.25), channel_id=1, source_target_pairs={{0,8},{4,12},{8,16},{12,20},{16,24},{20,28},{24,0},{28,4},{1,9},{5... | collective-permute-start | bytes 3538952 | tf_op jit(solution)/shard_map/ppermute | solution.py:294
  224.3 43.9 %collective-permute-start.31 = (bf16[576,1024]{1,0:T(8,128)(2,1)S(1)}, bf16[576,1024]{1,0:T(8,128)(2,1)S(1)}, u32[]{:S(2)}, u32[]{:S(2)}) collective-permute-start(bf16[576,1024]{1,0:T(8,128)(2,1)S(1)} %collective-permute-done.25), channel_id=1, source_target_pairs={{0,4},{4,0},{8,12},{12,8},{16,20},{20,16},{24,28},{28,24},{1,5},{5... | collective-permute-start | bytes 3538952 | tf_op jit(solution)/shard_map/ppermute | solution.py:291
  225.9 42.3 %collective-permute-start.29 = (bf16[800,384]{1,0:T(8,128)(2,1)S(1)}, bf16[800,384]{1,0:T(8,128)(2,1)S(1)}, u32[]{:S(2)}, u32[]{:S(2)}) collective-permute-start(bf16[800,384]{1,0:T(8,128)(2,1)S(1)} %collective-permute-done.23), channel_id=1, source_target_pairs={{0,4},{4,0},{8,12},{12,8},{16,20},{20,16},{24,28},{28,24},{1,5},{5... | collective-permute-start | bytes 1843208 | tf_op jit(solution)/shard_map/ppermute | solution.py:291
  227.3 28.2 %collective-permute-start.32 = (bf16[128,768]{1,0:T(8,128)(2,1)S(1)}, bf16[128,768]{1,0:T(8,128)(2,1)S(1)}, u32[]{:S(2)}, u32[]{:S(2)}) collective-permute-start(bf16[128,768]{1,0:T(8,128)(2,1)S(1)} %fusion.10), channel_id=1, source_target_pairs={{0,8},{4,12},{8,16},{12,20},{16,24},{20,28},{24,0},{28,4},{1,9},{5... | collective-permute-start | bytes 589832 | tf_op jit(solution)/shard_map/ppermute | solution.py:294
  232.5 35.8 %collective-permute-start.35 = (bf16[128,768]{1,0:T(8,128)(2,1)S(1)}, bf16[128,768]{1,0:T(8,128)(2,1)S(1)}, u32[]{:S(2)}, u32[]{:S(2)}) collective-permute-start(bf16[128,768]{1,0:T(8,128)(2,1)S(1)} %get-tuple-element.367), channel_id=1, source_target_pairs={{0,4},{4,0},{8,12},{12,8},{16,20},{20,16},{24,28},{28,24},{1,5},{5... | collective-permute-start | bytes 589832 | tf_op jit(solution)/shard_map/ppermute | solution.py:291
  273.0 27.3 %collective-permute-start.36 = (bf16[576,1024]{1,0:T(8,128)(2,1)}, bf16[576,1024]{1,0:T(8,128)(2,1)}, u32[]{:S(2)}, u32[]{:S(2)}) collective-permute-start(bf16[576,1024]{1,0:T(8,128)(2,1)} %collective-permute-done.30), channel_id=1, source_target_pairs={{0,4},{4,0},{8,12},{12,8},{16,20},{20,16},{24,28},{28,24},{1,5},{5... | collective-permute-start | bytes 3538952 | tf_op jit(solution)/shard_map/ppermute | solution.py:291
  305.2 22.1 %collective-permute-start.40 = (bf16[256,384]{1,0:T(8,128)(2,1)S(1)}, bf16[256,384]{1,0:T(8,128)(2,1)S(1)}, u32[]{:S(2)}, u32[]{:S(2)}) collective-permute-start(bf16[256,384]{1,0:T(8,128)(2,1)S(1)} %pad_maximum_fusion.13), channel_id=1, source_target_pairs={{0,8},{4,12},{8,16},{12,20},{16,24},{20,28},{24,0},{28,4},{1,9},{5... | collective-permute-start | bytes 589832 | tf_op jit(solution)/shard_map/ppermute | solution.py:294
  308.7 18.6 %collective-permute-start.41 = (bf16[256,384]{1,0:T(8,128)(2,1)S(1)}, bf16[256,384]{1,0:T(8,128)(2,1)S(1)}, u32[]{:S(2)}, u32[]{:S(2)}) collective-permute-start(bf16[256,384]{1,0:T(8,128)(2,1)S(1)} %pad_maximum_fusion.13), channel_id=1, source_target_pairs={{0,4},{4,0},{8,12},{12,8},{16,20},{20,16},{24,28},{28,24},{1,5},{5... | collective-permute-start | bytes 589832 | tf_op jit(solution)/shard_map/ppermute | solution.py:291
  327.3 17.9 %collective-permute-start.42 = (bf16[256,384]{1,0:T(8,128)(2,1)S(1)}, bf16[256,384]{1,0:T(8,128)(2,1)S(1)}, u32[]{:S(2)}, u32[]{:S(2)}) collective-permute-start(bf16[256,384]{1,0:T(8,128)(2,1)S(1)} %collective-permute-done.40), channel_id=1, source_target_pairs={{0,8},{4,12},{8,16},{12,20},{16,24},{20,28},{24,0},{28,4},{1,9},{5... | collective-permute-start | bytes 589832 | tf_op jit(solution)/shard_map/ppermute | solution.py:294
  329.8 15.4 %collective-permute-start.44 = (bf16[256,384]{1,0:T(8,128)(2,1)S(1)}, bf16[256,384]{1,0:T(8,128)(2,1)S(1)}, u32[]{:S(2)}, u32[]{:S(2)}) collective-permute-start(bf16[256,384]{1,0:T(8,128)(2,1)S(1)} %collective-permute-done.40), channel_id=1, source_target_pairs={{0,4},{4,0},{8,12},{12,8},{16,20},{20,16},{24,28},{28,24},{1,5},{5... | collective-permute-start | bytes 589832 | tf_op jit(solution)/shard_map/ppermute | solution.py:291
  330.8 14.5 %collective-permute-start.43 = (bf16[2,128,384]{2,1,0:T(8,128)(2,1)S(1)}, bf16[2,128,384]{2,1,0:T(8,128)(2,1)S(1)}, u32[]{:S(2)}, u32[]{:S(2)}) collective-permute-start(bf16[2,128,384]{2,1,0:T(8,128)(2,1)S(1)} %pad_maximum_fusion.14), channel_id=1, source_target_pairs={{0,2},{1,3},{2,0},{3,1},{4,6},{5,7},{6,4},{7,5},{8,10},{9,11},{10,... | collective-permute-start | bytes 589832 | tf_op jit(solution)/shard_map/ppermute | solution.py:369
  345.3 19.5 %collective-permute-start.48 = (bf16[256,384]{1,0:T(8,128)(2,1)S(1)}, bf16[256,384]{1,0:T(8,128)(2,1)S(1)}, u32[]{:S(2)}, u32[]{:S(2)}) collective-permute-start(bf16[256,384]{1,0:T(8,128)(2,1)S(1)} %collective-permute-done.42), channel_id=1, source_target_pairs={{0,8},{4,12},{8,16},{12,20},{16,24},{20,28},{24,0},{28,4},{1,9},{5... | collective-permute-start | bytes 589832 | tf_op jit(solution)/shard_map/ppermute | solution.py:294
  348.3 16.6 %collective-permute-start.50 = (bf16[256,384]{1,0:T(8,128)(2,1)S(1)}, bf16[256,384]{1,0:T(8,128)(2,1)S(1)}, u32[]{:S(2)}, u32[]{:S(2)}) collective-permute-start(bf16[256,384]{1,0:T(8,128)(2,1)S(1)} %collective-permute-done.42), channel_id=1, source_target_pairs={{0,4},{4,0},{8,12},{12,8},{16,20},{20,16},{24,28},{28,24},{1,5},{5... | collective-permute-start | bytes 589832 | tf_op jit(solution)/shard_map/ppermute | solution.py:291
  349.2 15.7 %collective-permute-start.49 = (bf16[2,128,384]{2,1,0:T(8,128)(2,1)S(1)}, bf16[2,128,384]{2,1,0:T(8,128)(2,1)S(1)}, u32[]{:S(2)}, u32[]{:S(2)}) collective-permute-start(bf16[2,128,384]{2,1,0:T(8,128)(2,1)S(1)} %pad_maximum_fusion.15), channel_id=1, source_target_pairs={{0,2},{1,3},{2,0},{3,1},{4,6},{5,7},{6,4},{7,5},{8,10},{9,11},{10,... | collective-permute-start | bytes 589832 | tf_op jit(solution)/shard_map/ppermute | solution.py:369
  366.2 33.2 %collective-permute-start.51 = (bf16[2,128,384]{2,1,0:T(8,128)(2,1)}, bf16[2,128,384]{2,1,0:T(8,128)(2,1)}, u32[]{:S(2)}, u32[]{:S(2)}) collective-permute-start(bf16[2,128,384]{2,1,0:T(8,128)(2,1)} %pad_maximum_fusion.16), channel_id=1, source_target_pairs={{0,2},{1,3},{2,0},{3,1},{4,6},{5,7},{6,4},{7,5},{8,10},{9,11},{10,... | collective-permute-start | bytes 589832 | tf_op jit(solution)/shard_map/ppermute | solution.py:369
  367.7 31.7 %collective-permute-start.52 = (bf16[256,384]{1,0:T(8,128)(2,1)S(1)}, bf16[256,384]{1,0:T(8,128)(2,1)S(1)}, u32[]{:S(2)}, u32[]{:S(2)}) collective-permute-start(bf16[256,384]{1,0:T(8,128)(2,1)S(1)} %collective-permute-done.48), channel_id=1, source_target_pairs={{0,4},{4,0},{8,12},{12,8},{16,20},{20,16},{24,28},{28,24},{1,5},{5... | collective-permute-start | bytes 589832 | tf_op jit(solution)/shard_map/ppermute | solution.py:291
  384.1 29.0 %collective-permute-start.53 = (bf16[576,1024]{1,0:T(8,128)(2,1)S(1)}, bf16[576,1024]{1,0:T(8,128)(2,1)S(1)}, u32[]{:S(2)}, u32[]{:S(2)}) collective-permute-start(bf16[576,1024]{1,0:T(8,128)(2,1)S(1)} %get-tuple-element.360), channel_id=1, source_target_pairs={{0,4},{4,0},{8,12},{12,8},{16,20},{20,16},{24,28},{28,24},{1,5},{5... | collective-permute-start | bytes 3538952 | tf_op jit(solution)/shard_map/ppermute | solution.py:291
  385.1 56.8 %collective-permute-start.58 = (bf16[576,1024]{1,0:T(8,128)(2,1)}, bf16[576,1024]{1,0:T(8,128)(2,1)}, u32[]{:S(2)}, u32[]{:S(2)}) collective-permute-start(bf16[576,1024]{1,0:T(8,128)(2,1)} %get-tuple-element.359), channel_id=1, source_target_pairs={{0,4},{4,0},{8,12},{12,8},{16,20},{20,16},{24,28},{28,24},{1,5},{5... | collective-permute-start | bytes 3538952 | tf_op jit(solution)/shard_map/ppermute | solution.py:291
  413.0 23.3 %collective-permute-start.59 = (bf16[128,384]{1,0:T(8,128)(2,1)S(1)}, bf16[128,384]{1,0:T(8,128)(2,1)S(1)}, u32[]{:S(2)}, u32[]{:S(2)}) collective-permute-start(bf16[128,384]{1,0:T(8,128)(2,1)S(1)} %constant_dynamic-slice_fusion), channel_id=1, source_target_pairs={{0,8},{4,12},{8,16},{12,20},{16,24},{20,28},{24,0},{28,4},{1,9},{5... | collective-permute-start | bytes 294920 | tf_op jit(solution)/shard_map/ppermute | solution.py:294
  413.4 24.7 %collective-permute-start.60 = (bf16[128,384]{1,0:T(8,128)(2,1)S(1)}, bf16[128,384]{1,0:T(8,128)(2,1)S(1)}, u32[]{:S(2)}, u32[]{:S(2)}) collective-permute-start(bf16[128,384]{1,0:T(8,128)(2,1)S(1)} %constant_dynamic-slice_fusion), channel_id=1, source_target_pairs={{0,4},{4,0},{8,12},{12,8},{16,20},{20,16},{24,28},{28,24},{1,5},{5... | collective-permute-start | bytes 294920 | tf_op jit(solution)/shard_map/ppermute | solution.py:291
  417.0 30.7 %collective-permute-start.57 = (bf16[576,1024]{1,0:T(8,128)(2,1)}, bf16[576,1024]{1,0:T(8,128)(2,1)}, u32[]{:S(2)}, u32[]{:S(2)}) collective-permute-start(bf16[576,1024]{1,0:T(8,128)(2,1)} %fusion.1), channel_id=1, source_target_pairs={{0,8},{4,12},{8,16},{12,20},{16,24},{20,28},{24,0},{28,4},{1,9},{5... | collective-permute-start | bytes 3538952 | tf_op jit(solution)/shard_map/ppermute | solution.py:294
  417.1 30.5 %collective-permute-start.64 = (bf16[2,128,384]{2,1,0:T(8,128)(2,1)S(1)}, bf16[2,128,384]{2,1,0:T(8,128)(2,1)S(1)}, u32[]{:S(2)}, u32[]{:S(2)}) collective-permute-start(bf16[2,128,384]{2,1,0:T(8,128)(2,1)S(1)} %pad_maximum_fusion.18), channel_id=1, source_target_pairs={{0,2},{1,3},{2,0},{3,1},{4,6},{5,7},{6,4},{7,5},{8,10},{9,11},{10,... | collective-permute-start | bytes 589832 | tf_op jit(solution)/shard_map/ppermute | solution.py:369
  443.7 40.1 %collective-permute-start.66 = (bf16[576,1024]{1,0:T(8,128)(2,1)S(1)}, bf16[576,1024]{1,0:T(8,128)(2,1)S(1)}, u32[]{:S(2)}, u32[]{:S(2)}) collective-permute-start(bf16[576,1024]{1,0:T(8,128)(2,1)S(1)} %copy-done.49), channel_id=1, source_target_pairs={{0,4},{4,0},{8,12},{12,8},{16,20},{20,16},{24,28},{28,24},{1,5},{5... | collective-permute-start | bytes 3538952 | tf_op jit(solution)/shard_map/ppermute | solution.py:291
  450.2 22.1 %collective-permute-start.71 = (bf16[128,384]{1,0:T(8,128)(2,1)S(1)}, bf16[128,384]{1,0:T(8,128)(2,1)S(1)}, u32[]{:S(2)}, u32[]{:S(2)}) collective-permute-start(bf16[128,384]{1,0:T(8,128)(2,1)S(1)} %collective-permute-done.61), channel_id=1, source_target_pairs={{0,4},{4,0},{8,12},{12,8},{16,20},{20,16},{24,28},{28,24},{1,5},{5... | collective-permute-start | bytes 294920 | tf_op jit(solution)/shard_map/ppermute | solution.py:291
  452.0 21.2 %collective-permute-start.70 = (bf16[2,128,384]{2,1,0:T(8,128)(2,1)S(1)}, bf16[2,128,384]{2,1,0:T(8,128)(2,1)S(1)}, u32[]{:S(2)}, u32[]{:S(2)}) collective-permute-start(bf16[2,128,384]{2,1,0:T(8,128)(2,1)S(1)} %pad_maximum_fusion.19), channel_id=1, source_target_pairs={{0,2},{1,3},{2,0},{3,1},{4,6},{5,7},{6,4},{7,5},{8,10},{9,11},{10,... | collective-permute-start | bytes 589832 | tf_op jit(solution)/shard_map/ppermute | solution.py:369
  452.6 23.3 %collective-permute-start.74 = (bf16[64,1536]{1,0:T(8,128)(2,1)S(1)}, bf16[64,1536]{1,0:T(8,128)(2,1)S(1)}, u32[]{:S(2)}, u32[]{:S(2)}) collective-permute-start(bf16[64,1536]{1,0:T(8,128)(2,1)S(1)} %broadcast_select_fusion.3), channel_id=1, source_target_pairs={{0,1},{1,0},{2,3},{3,2},{4,5},{5,4},{6,7},{7,6},{8,9},{9,8},{10,11... | collective-permute-start | bytes 589832 | tf_op jit(solution)/shard_map/ppermute | solution.py:510
  459.3 31.0 %collective-permute-start.67 = (bf16[640,384]{1,0:T(8,128)(2,1)S(1)}, bf16[640,384]{1,0:T(8,128)(2,1)S(1)}, u32[]{:S(2)}, u32[]{:S(2)}) collective-permute-start(bf16[640,384]{1,0:T(8,128)(2,1)S(1)} %copy-done.62), channel_id=1, source_target_pairs={{0,8},{4,12},{8,16},{12,20},{16,24},{20,28},{24,0},{28,4},{1,9},{5... | collective-permute-start | bytes 1474568 | tf_op jit(solution)/shard_map/ppermute | solution.py:294
  472.2 18.5 %collective-permute-start.68 = (bf16[640,384]{1,0:T(8,128)(2,1)S(1)}, bf16[640,384]{1,0:T(8,128)(2,1)S(1)}, u32[]{:S(2)}, u32[]{:S(2)}) collective-permute-start(bf16[640,384]{1,0:T(8,128)(2,1)S(1)} %copy-done.62), channel_id=1, source_target_pairs={{0,4},{4,0},{8,12},{12,8},{16,20},{20,16},{24,28},{28,24},{1,5},{5... | collective-permute-start | bytes 1474568 | tf_op jit(solution)/shard_map/ppermute | solution.py:291
  473.1 25.1 %collective-permute-start.65 = (bf16[576,1024]{1,0:T(8,128)(2,1)S(1)}, bf16[576,1024]{1,0:T(8,128)(2,1)S(1)}, u32[]{:S(2)}, u32[]{:S(2)}) collective-permute-start(bf16[576,1024]{1,0:T(8,128)(2,1)S(1)} %fusion.3), channel_id=1, source_target_pairs={{0,8},{4,12},{8,16},{12,20},{16,24},{20,28},{24,0},{28,4},{1,9},{5... | collective-permute-start | bytes 3538952 | tf_op jit(solution)/shard_map/ppermute | solution.py:294
  488.6 26.9 %collective-permute-start.78 = (bf16[576,1024]{1,0:T(8,128)(2,1)S(1)}, bf16[576,1024]{1,0:T(8,128)(2,1)S(1)}, u32[]{:S(2)}, u32[]{:S(2)}) collective-permute-start(bf16[576,1024]{1,0:T(8,128)(2,1)S(1)} %get-tuple-element.357), channel_id=1, source_target_pairs={{0,4},{4,0},{8,12},{12,8},{16,20},{20,16},{24,28},{28,24},{1,5},{5... | collective-permute-start | bytes 3538952 | tf_op jit(solution)/shard_map/ppermute | solution.py:291
  490.3 29.1 %collective-permute-start.83 = (bf16[8,128,384]{2,1,0:T(8,128)(2,1)}, bf16[8,128,384]{2,1,0:T(8,128)(2,1)S(1)}, u32[]{:S(2)}, u32[]{:S(2)}) collective-permute-start(bf16[8,128,384]{2,1,0:T(8,128)(2,1)} %slice.284), channel_id=1, source_target_pairs={{0,1},{1,0},{2,3},{3,2},{4,5},{5,4},{6,7},{7,6},{8,9},{9,8},{10,11... | collective-permute-start | bytes 2359304 | tf_op jit(solution)/shard_map/ppermute | solution.py:458
  490.3 31.2 %collective-permute-start.82 = (bf16[8,128,384]{2,1,0:T(8,128)(2,1)S(1)}, bf16[8,128,384]{2,1,0:T(8,128)(2,1)S(1)}, u32[]{:S(2)}, u32[]{:S(2)}) collective-permute-start(bf16[8,128,384]{2,1,0:T(8,128)(2,1)S(1)} %bitcast.324), channel_id=1, source_target_pairs={{0,1},{1,0},{2,3},{3,2},{4,5},{5,4},{6,7},{7,6},{8,9},{9,8},{10,11... | collective-permute-start | bytes 2359304 | tf_op jit(solution)/shard_map/ppermute | solution.py:458
  500.1 36.5 %collective-permute-start.77 = (bf16[576,1024]{1,0:T(8,128)(2,1)S(1)}, bf16[576,1024]{1,0:T(8,128)(2,1)S(1)}, u32[]{:S(2)}, u32[]{:S(2)}) collective-permute-start(bf16[576,1024]{1,0:T(8,128)(2,1)S(1)} %fusion.5), channel_id=1, source_target_pairs={{0,8},{4,12},{8,16},{12,20},{16,24},{20,28},{24,0},{28,4},{1,9},{5... | collective-permute-start | bytes 3538952 | tf_op jit(solution)/shard_map/ppermute | solution.py:294
  500.5 36.2 %collective-permute-start.79 = (bf16[640,384]{1,0:T(8,128)(2,1)S(1)}, bf16[640,384]{1,0:T(8,128)(2,1)}, u32[]{:S(2)}, u32[]{:S(2)}) collective-permute-start(bf16[640,384]{1,0:T(8,128)(2,1)S(1)} %collective-permute-done.67), channel_id=1, source_target_pairs={{0,8},{4,12},{8,16},{12,20},{16,24},{20,28},{24,0},{28,4},{1,9},{5... | collective-permute-start | bytes 1474568 | tf_op jit(solution)/shard_map/ppermute | solution.py:294
  515.5 21.2 %collective-permute-start.80 = (bf16[640,384]{1,0:T(8,128)(2,1)S(1)}, bf16[640,384]{1,0:T(8,128)(2,1)S(1)}, u32[]{:S(2)}, u32[]{:S(2)}) collective-permute-start(bf16[640,384]{1,0:T(8,128)(2,1)S(1)} %collective-permute-done.67), channel_id=1, source_target_pairs={{0,4},{4,0},{8,12},{12,8},{16,20},{20,16},{24,28},{28,24},{1,5},{5... | collective-permute-start | bytes 1474568 | tf_op jit(solution)/shard_map/ppermute | solution.py:291
  521.5 37.7 %collective-permute-start.87 = (bf16[8,128,384]{2,1,0:T(8,128)(2,1)}, bf16[8,128,384]{2,1,0:T(8,128)(2,1)}, u32[]{:S(2)}, u32[]{:S(2)}) collective-permute-start(bf16[8,128,384]{2,1,0:T(8,128)(2,1)} %bitcast.134), channel_id=1, source_target_pairs={{0,1},{1,0},{2,3},{3,2},{4,5},{5,4},{6,7},{7,6},{8,9},{9,8},{10,11... | collective-permute-start | bytes 2359304 | tf_op jit(solution)/shard_map/ppermute | solution.py:458
  536.7 22.5 %collective-permute-start.84 = (bf16[640,384]{1,0:T(8,128)(2,1)}, bf16[640,384]{1,0:T(8,128)(2,1)}, u32[]{:S(2)}, u32[]{:S(2)}) collective-permute-start(bf16[640,384]{1,0:T(8,128)(2,1)} %collective-permute-done.79), channel_id=1, source_target_pairs={{0,8},{4,12},{8,16},{12,20},{16,24},{20,28},{24,0},{28,4},{1,9},{5... | collective-permute-start | bytes 1474568 | tf_op jit(solution)/shard_map/ppermute | solution.py:294
  537.0 22.2 %collective-permute-start.85 = (bf16[640,384]{1,0:T(8,128)(2,1)}, bf16[640,384]{1,0:T(8,128)(2,1)}, u32[]{:S(2)}, u32[]{:S(2)}) collective-permute-start(bf16[640,384]{1,0:T(8,128)(2,1)} %collective-permute-done.79), channel_id=1, source_target_pairs={{0,4},{4,0},{8,12},{12,8},{16,20},{20,16},{24,28},{28,24},{1,5},{5... | collective-permute-start | bytes 1474568 | tf_op jit(solution)/shard_map/ppermute | solution.py:291
  539.2 20.0 %collective-permute-start.86 = (bf16[8,128,384]{2,1,0:T(8,128)(2,1)}, bf16[8,128,384]{2,1,0:T(8,128)(2,1)}, u32[]{:S(2)}, u32[]{:S(2)}) collective-permute-start(bf16[8,128,384]{2,1,0:T(8,128)(2,1)} %bitcast.125), channel_id=1, source_target_pairs={{0,1},{1,0},{2,3},{3,2},{4,5},{5,4},{6,7},{7,6},{8,9},{9,8},{10,11... | collective-permute-start | bytes 2359304 | tf_op jit(solution)/shard_map/ppermute | solution.py:458
  559.2 20.9 %collective-permute-start.91 = (bf16[640,384]{1,0:T(8,128)(2,1)}, bf16[640,384]{1,0:T(8,128)(2,1)S(1)}, u32[]{:S(2)}, u32[]{:S(2)}) collective-permute-start(bf16[640,384]{1,0:T(8,128)(2,1)} %collective-permute-done.84), channel_id=1, source_target_pairs={{0,4},{4,0},{8,12},{12,8},{16,20},{20,16},{24,28},{28,24},{1,5},{5... | collective-permute-start | bytes 1474568 | tf_op jit(solution)/shard_map/ppermute | solution.py:291
  (105 other events, 1493.8 us)

commit v2 on v1

--- a/solution.py
+++ b/solution.py
@@ -927,8 +927,8 @@
     def kernel(
         held_ref, middle_ref, branch_ref, cot_ref, in_ref, gate_ref, up_ref, hidden_ref,
         seg_ref, mod_ref, norm_ref, down_hbm,
-        output_ref, part_ref, gg_ref, gu_ref, gd_ref, dmod_ref, dgain_ref,
-        wg_ref, wu_ref, wd_ref, sems,
+        output_ref, part_ref, grads_ref, dmod_ref, dgain_ref,
+        wg_ref, wu_ref, wd_ref, woven_ref, sems,
     ):
         for_down = pltpu.make_async_copy(down_hbm, wd_ref, sems.at[sum(counts)])
         for_down.start()
@@ -950,17 +950,33 @@
         sigma = jax.nn.sigmoid(gate)
         dup = (dhidden * gate * sigma).astype(BF16)
         dgate = (dhidden * up * (sigma * (1.0 + gate * (1.0 - sigma)))).astype(BF16)
-        for start in range(0, width, cut):
-            hidden_t = hidden_ref[:, start : start + cut].T
-            gd_ref[start : start + cut, :] = dot(hidden_t, dlow).astype(BF16)
+        half = width // 2
+        unit_row = lax.broadcasted_iota(jnp.int32, (width, half), 0)
+        unit_column = lax.broadcasted_iota(jnp.int32, (width, half), 1)
+        chosen = []
+        for parity in range(2):
+            pick = jnp.where(unit_row == 2 * unit_column + parity, 1.0, 0.0).astype(BF16)
+            chosen.append(dot(hidden_ref[...], pick).astype(BF16))
+        for start in range(0, half, cut):
+            pair = [dot(c[:, start : start + cut].T, dlow) for c in chosen]
+            for place in range(3):
+                for j in range(width // LANES):
+                    at = place * width + j * LANES
+                    woven_ref[j, pl.ds(3 * start + place, cut, stride=3), :] = pair[at // depth][
+                        :, at % depth : at % depth + LANES
+                    ]
+        for j in range(width // LANES):
+            grads_ref[2 * depth : 3 * depth, j * LANES : (j + 1) * LANES] = woven_ref[j].astype(
+                BF16
+            )
         for_gate.wait()
         part = dot_t(dgate, wg_ref[...])
         for_up.wait()
         part_ref[...] = (part + dot_t(dup, wu_ref[...])).astype(BF16)
         for start in range(0, depth, cut):
             in_t = in_ref[:, start : start + cut].T
-            gg_ref[start : start + cut, :] = dot(in_t, dgate).astype(BF16)
-            gu_ref[start : start + cut, :] = dot(in_t, dup).astype(BF16)
+            grads_ref[start : start + cut, :] = dot(in_t, dgate).astype(BF16)
+            grads_ref[depth + start : depth + start + cut, :] = dot(in_t, dup).astype(BF16)
 
     def like(rows, columns, kind):
         return jax.ShapeDtypeStruct((rows, columns), kind)
@@ -970,18 +986,17 @@
         out_shape=(
             like(length, depth, BF16),
             like(length, depth, BF16),
-            like(depth, width, BF16),
-            like(depth, width, BF16),
-            like(width, depth, BF16),
+            like(3 * depth, width, BF16),
             like(clips, depth, F32),
             like(1, depth, F32),
         ),
         in_specs=[ANY] + [VMEM] * 10 + [ANY],
-        out_specs=(VMEM,) * 7,
+        out_specs=(VMEM,) * 5,
         scratch_shapes=[
             pltpu.VMEM((depth, width), BF16),
             pltpu.VMEM((depth, width), BF16),
             pltpu.VMEM((width, depth), BF16),
+            pltpu.VMEM((width // LANES, depth, LANES), F32),
             pltpu.SemaphoreType.DMA((sum(counts) + 1,)),
         ],
         compiler_params=params(56),
@@ -1111,7 +1126,8 @@
 
 
 def shard_gradient(layout, index, normed, dattn, text, mixed, acts, ends, cond):
-    groups, packs, length, width = normed.shape
+    groups = len(normed)
+    packs, length, width = normed[0].shape
     key_count, text_cut = text.shape[2:]
     conds = cond.shape[1]
     cut = LANES
@@ -1123,7 +1139,11 @@
     per_cond = cond.shape[2] // cut
     kinds = [3 * per_in, 4 * per_in, 4 * per_in + 2 * per_text, 4 * per_in + 2 * per_text + per_cond]
 
-    def kernel(first_ref, n_ref, d_ref, t_ref, m_ref, a_ref, e_ref, c_ref, out_ref, woven_ref):
+    def kernel(first_ref, t_ref, m_ref, a_ref, e_ref, c_ref, *rest):
+        n_refs, d_refs = rest[:groups], rest[groups : 2 * groups]
+        out_ref, woven_ref = rest[2 * groups :]
+        me = first_ref[1]
+
         @pl.when(pl.program_id(0) == 0)
         def _():
             out_ref[...] = jnp.zeros_like(out_ref)
@@ -1141,8 +1161,12 @@
                 sub = g % per_in
                 lanes = pl.ds(pl.multiple_of(sub % (width // cut) * cut, cut), cut)
                 grads = pl.ds(pl.multiple_of(g // per_in * length, length), length)
-                left = tall(n_ref[sub // (width // cut), :, :, lanes])
-                out_ref[rows, :] += t_dot(left, tall(a_ref[:, grads, :]))
+                right = tall(a_ref[:, grads, :])
+                for key in range(groups):
+
+                    @pl.when(sub // (width // cut) == me ^ key)
+                    def _():
+                        out_ref[rows, :] += t_dot(tall(n_refs[key][:, :, lanes]), right)
 
             @pl.when((g >= kinds[0]) & (g < kinds[1]))
             def _():
@@ -1152,10 +1176,10 @@
                 slab = tall(m_ref[:, length : 2 * length, lanes]).astype(F32)
                 slab = pltpu.roll(slab, (LANES - at % LANES) % LANES, 1)
                 left = slab.T[0:each, :].astype(BF16)
-                for part in range(groups):
-                    value = dot(left, tall(d_ref[part]))
+                for key in range(groups):
+                    value = dot(left, tall(d_refs[key][...]))
                     for j in range(width // LANES):
-                        woven_ref[j, pl.ds(part, each, stride=groups), :] = value[
+                        woven_ref[j, pl.ds(me ^ key, each, stride=groups), :] = value[
                             :, j * LANES : (j + 1) * LANES
                         ]
                 woven = [woven_ref[j] for j in range(width // LANES)]
@@ -1194,7 +1218,8 @@
             pipeline_mode=pl.Buffered(1),
         )
 
-    operands = [(normed, 1), (dattn, 1), (text, 1), (mixed, 0), (acts, 0), (ends, 0), (cond, 0)]
+    operands = [(text, 1), (mixed, 0), (acts, 0), (ends, 0), (cond, 0)]
+    operands += [(array, 0) for array in normed + dattn]
     return pl.pallas_call(
         kernel,
         grid=(packs // step_packs,),
@@ -1203,7 +1228,7 @@
         out_specs=pl.BlockSpec((layout.used, width), lambda s: (0, 0)),
         scratch_shapes=[pltpu.VMEM((width // LANES, cut, LANES), F32)],
         compiler_params=params(58),
-    )(first[None], *[o[0] for o in operands])
+    )(jnp.stack([first, lax.axis_index("mp").astype(jnp.int32)]), *[o[0] for o in operands])
 
 
 def input_backward(dnormed, tokens, dmiddle, seg, mods, norms):
@@ -1282,7 +1307,8 @@
     sizes = [model_width] * 4 + [text_width, text_width, 4 * COND, 4]
     starts = [sum(sizes[:i]) for i in range(len(sizes) + 1)]
     attn_rows = to_rows(attn_lay, attn_master, index)
-    ffn_piece = to_rows(ffn_lay, ffn_master, index)
+    attn_rows, ffn_flat, time_steps = join([], attn_rows, ffn_master, time_steps)
+    ffn_piece = to_rows(ffn_lay, ffn_flat, index)
     pieces = Pieces(attn_lay, starts[4], ring)
     digits = jnp.stack([time_steps[0] // 32, time_steps[0] % 32]).astype(BF16)
     near_text = own_cut(text_rows)
@@ -1363,7 +1389,7 @@
     step(early)
     ffn_out = join(early, sum_mp(ffn_part))
     step(early)
-    output, dffn_part, g_gate, g_up, g_down, dmod_gate_ffn, dnorm_four = join(
+    output, dffn_part, ffn_grads, dmod_gate_ffn, dnorm_four = join(
         early,
         *ffn_backward(
             ffn_lay,
@@ -1381,8 +1407,7 @@
             w_down,
         ),
     )
-    ffn_grads = ffn_lay.cut([g_gate, g_up, g_down.reshape(model_width, hidden_width)])
-    ffn_run = Scattering(ring, ffn_grads, index)
+    ffn_run = Scattering(ring, ffn_lay.cut([ffn_grads]), index)
     step(early)
     (
         dmiddle,
@@ -1446,22 +1471,18 @@
         ],
         0,
     ).astype(BF16)
-    normed_four = in_order({0: in_own, 2: in_far, 1: near.got["own"], 3: near.got["far"]})
+    normed_four = [in_own, near.got["own"], in_far, near.got["far"]]
     dattn_own, dattn_far = dattn_run.both()
     near = Once({"own": dattn_own, "far": dattn_far}, 1)
-    ends_all, ffn_shard, normed_four = join(
+    ends_all, ffn_shard = join(
         [acts_run.send(), near],
         gather_small(ends[None], parts),
         to_flat(ffn_lay, ffn_run.result(), index),
-        normed_four,
-    )
-    dattn_four = in_order(
-        {0: dattn_own, 2: dattn_far, 1: near.got["own"], 3: near.got["far"]}
-    )
+    )
+    dattn_four = [dattn_own, near.got["own"], dattn_far, near.got["far"]]
     step_value = step_count[0].astype(F32)
-    dattn_four, *ffn_result = join(
+    ffn_result = join(
         [acts_run.send()],
-        dattn_four,
         *adamw_flat(ffn_lay, ffn_master, ffn_first, ffn_second, ffn_shard, step_value, RATE),
     )
     attn_sum = shard_gradient(

time: 637 us -> 623 us (0.978)
  starting transfers between devices: 115 us -> 145 us
  local copies, waits for them, and re-layouts: 140 us -> 113 us
  waiting for transfers between devices: 212 us -> 201 us
  other arithmetic: 42.3 us -> 35.1 us
    ppermute x24, starting transfers between devices: 34.9 us -> 67.6 us  [onward(): return lax.ppermute(block, 'dp', self.next)]
    ppermute x24, waiting for transfers between devices: 96.2 us -> 76.2 us  [onward(): return lax.ppermute(block, 'dp', self.next)]
    dynamic_update_slice x12 -> x4, local copies, waits for them, and re-layouts: 18.4 us -> 5.96 us  [in_order(): lax.dynamic_update_slice(held, piece[None], (me ^ key,) + (zero,) * piece...]
    ppermute x32, waiting for transfers between devices: 53 us -> 61.1 us  [swap(): return lax.ppermute(block, 'dp', self.pair)]
  transfers between devices with their start and end apart: 93 -> 93, of which waited for: 33 -> 37; matrix products, arithmetic and copies ran while one was open for 24% -> 20% of each run, Pallas kernels for 11% -> 11%
where the time goes in v2:
time: 623 us; the launch traced here: 612 us
  waiting for transfers between devices  201 us (32%)
  starting transfers between devices  145 us (23%)
  local copies, waits for them, and re-layouts  113 us (18%)
  Pallas kernels  108 us (17%)
  other arithmetic  35.1 us (6%)
    ppermute x24, waiting for transfers between devices, onward(): return lax.ppermute(block, 'dp', self.next)  76.2 us
    ppermute x24, starting transfers between devices, onward(): return lax.ppermute(block, 'dp', self.next)  67.6 us
    ppermute x32, waiting for transfers between devices, swap(): return lax.ppermute(block, 'dp', self.pair)  61.1 us
    dynamic_update_slice x46, local copies, waits for them, and re-layouts, put(): lax.dynamic_update_slice(self.held, value[None, None], (slot, side) + (se...  40.2 us
    ppermute x32, starting transfers between devices, swap(): return lax.ppermute(block, 'dp', self.pair)  38.2 us
    ppermute x12, waiting for transfers between devices, send(): self.sent['far'] = lax.ppermute(self.chunk, 'mp', pairs)  28.3 us
    pallas_call x2, Pallas kernels, adamw_flat(): pl.pallas_call(kernel, grid=(steps,), out_shape=(like, like, like, like,...  24 us
    pallas_call x1, Pallas kernels, shard_gradient(): pl.pallas_call(kernel, grid=(packs // step_packs,), out_shape=jax.ShapeDt...  21.4 us
  transfers between devices with their start and end apart: 93, of which 37 were waited for; matrix products, arithmetic and copies ran while one was open for 20% of the time, Pallas kernels for 11%

profile of v2, /device:TPU:8, one launch (start us, length us, event | category | flops | bytes accessed | tf_op | source)
XLA Modules:
  0.0 612.0 jit_solution(221942809558647614)
XLA Ops:
  1.6 3.4 collective-permute-start
  19.6 2.6 collective-permute-start.1
  26.4 23.2 %collective-permute-start.5 = (bf16[144,1024]{1,0:T(8,128)(2,1)S(1)}, bf16[144,1024]{1,0:T(8,128)(2,1)S(1)}, u32[]{:S(2)}, u32[]{:S(2)}) collective-permute-start(bf16[144,1024]{1,0:T(8,128)(2,1)S(1)} %collective-permute-done.3), channel_id=1, source_target_pairs={{0,8},{4,12},{8,16},{12,20},{16,24},{20,28},{24,0},{28,4},{1,9},{5... | collective-permute-start | bytes 884744 | tf_op jit(solution)/shard_map/ppermute | solution.py:294
  56.4 6.4 %collective-permute-done.6 = bf16[2,128,1024]{2,1,0:T(8,128)(2,1)S(1)} collective-permute-done((bf16[2,128,1024]{2,1,0:T(8,128)(2,1)S(1)}, bf16[2,128,1024]{2,1,0:T(8,128)(2,1)S(1)}, u32[]{:S(2)}, u32[]{:S(2)}) %collective-permute-start.6) | collective-permute-done | bytes 524320 | tf_op jit(solution)/shard_map/ppermute | solution.py:369
  69.7 5.1 collective-permute-done.9
  81.8 5.8 collective-permute-done.11
  93.8 6.2 %collective-permute-done.15 = bf16[2,128,1024]{2,1,0:T(8,128)(2,1)S(1)} collective-permute-done((bf16[2,128,1024]{2,1,0:T(8,128)(2,1)S(1)}, bf16[2,128,1024]{2,1,0:T(8,128)(2,1)S(1)}, u32[]{:S(2)}, u32[]{:S(2)}) %collective-permute-start.15) | collective-permute-done | bytes 524320 | tf_op jit(solution)/shard_map/ppermute | solution.py:369
  101.5 4.3 fusion.7
  115.6 10.0 %collective-permute-start.18 = (bf16[800,384]{1,0:T(8,128)(2,1)}, bf16[800,384]{1,0:T(8,128)(2,1)}, u32[]{:S(2)}, u32[]{:S(2)}) collective-permute-start(bf16[800,384]{1,0:T(8,128)(2,1)} %collective-permute-done.13), channel_id=1, source_target_pairs={{0,8},{4,12},{8,16},{12,20},{16,24},{20,28},{24,0},{28,4},{1,9},{5... | collective-permute-start | bytes 1843208 | tf_op jit(solution)/shard_map/ppermute | solution.py:294
  129.5 3.3 copy-done.37
  132.8 6.5 %shard_map.289 = bf16[8,128,768]{2,1,0:T(8,128)(2,1)S(1)} custom-call(s32[2]{0:T(128)S(1)} %pad_add_fusion.place_ref, bf16[2432,384]{1,0:T(8,128)(2,1)S(1)} %shard_map.286.w_ref, bf16[4,8,128,1024]{3,2,1,0:T(8,128)(2,1)} %copy-done.37), custom_call_target="tpu_custom_call" | custom-call | tf_op jit(solution)/shard_map/pallas_call | solution.py:760
  139.4 6.3 %collective-permute-start.22 = (bf16[128,768]{1,0:T(8,128)(2,1)S(1)}, bf16[128,768]{1,0:T(8,128)(2,1)S(1)}, u32[]{:S(2)}, u32[]{:S(2)}) collective-permute-start(bf16[128,768]{1,0:T(8,128)(2,1)S(1)} %get-tuple-element.364), channel_id=1, source_target_pairs={{0,4},{4,0},{8,12},{12,8},{16,20},{20,16},{24,28},{28,24},{1,5},{5... | collective-permute-start | bytes 589832 | tf_op jit(solution)/shard_map/ppermute | solution.py:291
  145.7 5.8 all-to-all-start
  151.5 2.6 broadcast_in_dim.314
  157.0 5.1 all-to-all-done
  162.1 5.3 all_gather.3.mod_ref
  169.1 9.8 %collective-permute-start.23 = (bf16[800,384]{1,0:T(8,128)(2,1)}, bf16[800,384]{1,0:T(8,128)(2,1)S(1)}, u32[]{:S(2)}, u32[]{:S(2)}) collective-permute-start(bf16[800,384]{1,0:T(8,128)(2,1)} %collective-permute-done.18), channel_id=1, source_target_pairs={{0,8},{4,12},{8,16},{12,20},{16,24},{20,28},{24,0},{28,4},{1,9},{5... | collective-permute-start | bytes 1843208 | tf_op jit(solution)/shard_map/ppermute | solution.py:294
  179.2 3.4 collective-permute-start.25
  184.3 4.8 broadcast_in_dim.275
  189.0 2.4 bitcast_dynamic-update-slice_fusion.11
  191.4 2.4 bitcast_dynamic-update-slice_fusion.10
  198.0 24.0 %collective-permute-done.27 = bf16[128,768]{1,0:T(8,128)(2,1)S(1)} collective-permute-done((bf16[128,768]{1,0:T(8,128)(2,1)S(1)}, bf16[128,768]{1,0:T(8,128)(2,1)S(1)}, u32[]{:S(2)}, u32[]{:S(2)}) %collective-permute-start.27) | collective-permute-done | bytes 196640 | tf_op jit(solution)/shard_map/ppermute | solution.py:294
  222.3 3.4 collective-permute-start.30
  227.8 2.5 collective-permute-start.32
  231.5 2.4 bitcast_dynamic-update-slice_fusion.8
  236.5 20.5 %collective-permute-done.32 = bf16[128,768]{1,0:T(8,128)(2,1)S(1)} collective-permute-done((bf16[128,768]{1,0:T(8,128)(2,1)S(1)}, bf16[128,768]{1,0:T(8,128)(2,1)S(1)}, u32[]{:S(2)}, u32[]{:S(2)}) %collective-permute-start.32) | collective-permute-done | bytes 196640 | tf_op jit(solution)/shard_map/ppermute | solution.py:294
  259.1 11.5 %collective-permute-done.35 = bf16[128,768]{1,0:T(8,128)(2,1)S(1)} collective-permute-done((bf16[128,768]{1,0:T(8,128)(2,1)S(1)}, bf16[128,768]{1,0:T(8,128)(2,1)S(1)}, u32[]{:S(2)}, u32[]{:S(2)}) %collective-permute-start.35) | collective-permute-done | bytes 196640 | tf_op jit(solution)/shard_map/ppermute | solution.py:291
  277.5 2.4 reshape.286.w_ref.wo_ref
  281.9 3.7 shard_map.290
  286.4 4.6 shard_map.291
  295.4 4.4 collective-permute-done.38
  302.5 2.4 bitcast_dynamic-update-slice_fusion.5
  304.9 2.4 bitcast_dynamic-update-slice_fusion.4
  307.3 3.0 collective-permute-start.40
  316.7 5.9 reshape.288.down_hbm
  322.6 6.6 %shard_map.292 = (f32[128,1536]{1,0:T(8,128)}, bf16[128,1536]{1,0:T(8,128)(2,1)}, f32[128,1024]{1,0:T(8,128)}, f32[128,1024]{1,0:T(8,128)}, bf16[128,1024]{1,0:T(8,128)(2,1)}, /*index=5*/bf16[128,1536]{1,0:T(8,128)(2,1)}) custom-call(bf16[8,576,1024]{2,1,0:T(8,128)(2,1)} %bitcast.70.held_ref, bf16[128,1536]{1,0:T(8,128)(2,1)} %x_ref.8, ...), custom_call_target="tpu_custom_call" | custom-call | tf_op jit(solution)/shard_map/pallas_call | solution.py:896
  330.2 2.5 collective-permute-start.42
  340.0 5.5 collective-permute-done.46
  347.9 2.9 collective-permute-start.48
  353.6 14.6 %shard_map.293 = (bf16[128,1536]{1,0:T(8,128)(2,1)}, bf16[128,1536]{1,0:T(8,128)(2,1)}, bf16[4608,1024]{1,0:T(8,128)(2,1)}, f32[4,1536]{1,0:T(4,128)}, f32[1,1536]{1,0:T(1,128)}) custom-call(bf16[8,576,1024]{2,1,0:T(8,128)(2,1)} %bitcast.70.held_ref, f32[128,1536]{1,0:T(8,128)} %get-tuple-element.245.middle_ref, ...), custom_call_target="tpu_custom_call" | custom-call | tf_op jit(solution)/shard_map/pallas_call | solution.py:984
  370.9 3.9 dynamic-slice_bitcast_fusion
  378.8 6.4 %collective-permute-done.55 = bf16[64,1536]{1,0:T(8,128)(2,1)S(1)} collective-permute-done((bf16[64,1536]{1,0:T(8,128)(2,1)S(1)}, bf16[64,1536]{1,0:T(8,128)(2,1)S(1)}, u32[]{:S(2)}, u32[]{:S(2)}) %collective-permute-start.55) | collective-permute-done | bytes 196640 | tf_op jit(solution)/shard_map/ppermute | solution.py:515
  387.0 2.8 shard_map.294
  389.8 14.0 %collective-permute-done.53 = bf16[576,1024]{1,0:T(8,128)(2,1)S(1)} collective-permute-done((bf16[576,1024]{1,0:T(8,128)(2,1)S(1)}, bf16[576,1024]{1,0:T(8,128)(2,1)S(1)}, u32[]{:S(2)}, u32[]{:S(2)}) %collective-permute-start.53) | collective-permute-done | bytes 1179680 | tf_op jit(solution)/shard_map/ppermute | solution.py:291
  405.2 2.7 fusion.1
  410.7 12.1 %shard_map.295 = (bf16[128,1536]{1,0:T(8,128)(2,1)}, bf16[640,384]{1,0:T(8,128)(2,1)}, f32[4,384]{1,0:T(4,128)}) custom-call(bf16[8,800,384]{2,1,0:T(8,128)(2,1)} %bitcast.61.held_ref, bf16[128,384]{1,0:T(8,128)(2,1)} %copy-done.35, bf16[128,384]{1,0:T(8,128)(2,1)} %copy-done.25, bf16[128,384]{1,0:T(8,128)(2,1)} %copy-done.26, bf16[128,384]{1,0:T(8,128)(2,1)} %copy-done.27, ...), custom_call_target="tpu_custom_call" | custom-call | tf_op jit(solution)/shard_map/pallas_call | solution.py:1108
  423.0 5.9 collective-permute-done.60
  431.1 3.6 collective-permute-done.61
  442.9 2.8 fusion.3
  448.6 14.3 %collective-permute-done.71 = bf16[128,384]{1,0:T(8,128)(2,1)S(1)} collective-permute-done((bf16[128,384]{1,0:T(8,128)(2,1)S(1)}, bf16[128,384]{1,0:T(8,128)(2,1)S(1)}, u32[]{:S(2)}, u32[]{:S(2)}) %collective-permute-start.71) | collective-permute-done | bytes 98336 | tf_op jit(solution)/shard_map/ppermute | solution.py:291
  466.4 3.8 collective-permute-done.75
  473.4 3.6 collective-permute-done.73
  479.2 9.7 %collective-permute-done.65 = bf16[576,1024]{1,0:T(8,128)(2,1)S(1)} collective-permute-done((bf16[576,1024]{1,0:T(8,128)(2,1)S(1)}, bf16[576,1024]{1,0:T(8,128)(2,1)S(1)}, u32[]{:S(2)}, u32[]{:S(2)}) %collective-permute-start.65) | collective-permute-done | bytes 1179680 | tf_op jit(solution)/shard_map/ppermute | solution.py:294
  496.3 7.5 %collective-permute-done.78 = bf16[576,1024]{1,0:T(8,128)(2,1)S(1)} collective-permute-done((bf16[576,1024]{1,0:T(8,128)(2,1)S(1)}, bf16[576,1024]{1,0:T(8,128)(2,1)S(1)}, u32[]{:S(2)}, u32[]{:S(2)}) %collective-permute-start.78) | collective-permute-done | bytes 1179680 | tf_op jit(solution)/shard_map/ppermute | solution.py:291
  509.3 4.0 collective-permute-done.81
  513.4 14.1 %collective-permute-done.79 = bf16[640,384]{1,0:T(8,128)(2,1)} collective-permute-done((bf16[640,384]{1,0:T(8,128)(2,1)S(1)}, bf16[640,384]{1,0:T(8,128)(2,1)}, u32[]{:S(2)}, u32[]{:S(2)}) %collective-permute-start.79) | collective-permute-done | bytes 491552 | tf_op jit(solution)/shard_map/ppermute | solution.py:294
  531.2 2.7 fusion.x_ref
  533.9 3.5 collective-permute-done.88
  542.6 3.8 collective-permute-start.90
  547.2 2.5 collective-permute-done.90
  552.3 9.5 %shard_map.298 = (f32[1,589824]{1,0:T(1,128)}, f32[1,589824]{1,0:T(1,128)}, f32[1,589824]{1,0:T(1,128)}, f32[1,589824]{1,0:T(1,128)}, bf16[1,589824]{1,0:T(2,128)(2,1)}) custom-call(f32[2]{0:T(128)S(1)} %pad_maximum_fusion.23.fix_ref, f32[1,589824]{1,0:T(1,128)S(1)} %copy-done.8, f32[1,589824]{1,0:T(1,128)S(1)} %copy-done.18, f32[1,589824]{1,0:T(1,128)} %v_ref.2, ...), custom_call_target="tpu_custom_call" | custom-call | tf_op jit(solution)/shard_map/pallas_call | solution.py:271
  569.0 21.4 %shard_map.299.x_ref = f32[2432,384]{1,0:T(8,128)} custom-call(s32[2]{0:T(128)} %pad_add_fusion.1.first_ref, bf16[4,8,128,1024]{3,2,1,0:T(8,128)(2,1)} %copy-done.37, bf16[8,256,384]{2,1,0:T(8,128)(2,1)} %bitcast.298, bf16[8,640,384]{2,1,0:T(8,128)(2,1)} %bitcast.147.a_ref, bf16[8,48,384]{2,1,0:T(8,128)(2,1)} %copy-done.46, bf16[8,16,4096]{2,1,0:T(8,128)(2,1)} %copy-done.6, ...), custom_call_target="tpu_custom_call" | custom-call | tf_op jit(solution)/shard_map/pallas_call | solution.py:1223
  590.3 4.8 shard_map.300.g_ref
  597.0 14.5 %shard_map.301 = (f32[1,884928]{1,0:T(1,128)}, f32[1,884928]{1,0:T(1,128)}, f32[1,884928]{1,0:T(1,128)}, f32[1,884928]{1,0:T(1,128)}, bf16[1,884928]{1,0:T(2,128)(2,1)}) custom-call(f32[2]{0:T(128)S(1)} %pad_maximum_fusion.23.fix_ref, f32[1,884928]{1,0:T(1,128)S(1)} %copy-done.4, f32[1,884928]{1,0:T(1,128)} %m_ref.3, f32[1,884928]{1,0:T(1,128)} %v_ref.3, ...), custom_call_target="tpu_custom_call" | custom-call | tf_op jit(solution)/shard_map/pallas_call | solution.py:271
  (510 shorter events, 184.1 us)
Async XLA Ops:
  1.6 10.7 %collective-permute-start = (bf16[16,128]{1,0:T(8,128)(2,1)S(1)}, bf16[16,128]{1,0:T(8,128)(2,1)S(1)}, u32[]{:S(2)}, u32[]{:S(2)}) collective-permute-start(bf16[16,128]{1,0:T(8,128)(2,1)S(1)} %bitcast.315), channel_id=1, source_target_pairs={{0,4},{4,8},{8,12},{12,16},{16,20},{20,24},{24,28},{1,5},{5,9},{9,... | collective-permute-start | bytes 12296 | tf_op jit(solution)/shard_map/ppermute | solution.py:145
  19.6 60.6 %collective-permute-start.1 = (bf16[768,384]{1,0:T(8,128)(2,1)S(1)}, bf16[768,384]{1,0:T(8,128)(2,1)S(1)}, u32[]{:S(2)}, u32[]{:S(2)}) collective-permute-start(bf16[768,384]{1,0:T(8,128)(2,1)S(1)} %get-tuple-element.360), channel_id=1, source_target_pairs={{0,24},{4,28},{8,12},{1,25},{5,29},{9,13},{2,26},{6,30},{10,14},{3... | collective-permute-start | bytes 1769480 | tf_op jit(solution)/shard_map/ppermute | solution.py:105
  22.2 58.0 %collective-permute-start.2 = (bf16[768,384]{1,0:T(8,128)(2,1)S(1)}, bf16[768,384]{1,0:T(8,128)(2,1)S(1)}, u32[]{:S(2)}, u32[]{:S(2)}) collective-permute-start(bf16[768,384]{1,0:T(8,128)(2,1)S(1)} %get-tuple-element.359), channel_id=1, source_target_pairs={{0,16},{4,20},{1,17},{5,21},{2,18},{6,22},{3,19},{7,23}} | collective-permute-start | bytes 1769480 | tf_op jit(solution)/shard_map/ppermute | solution.py:105
  26.4 29.6 %collective-permute-start.5 = (bf16[144,1024]{1,0:T(8,128)(2,1)S(1)}, bf16[144,1024]{1,0:T(8,128)(2,1)S(1)}, u32[]{:S(2)}, u32[]{:S(2)}) collective-permute-start(bf16[144,1024]{1,0:T(8,128)(2,1)S(1)} %collective-permute-done.3), channel_id=1, source_target_pairs={{0,8},{4,12},{8,16},{12,20},{16,24},{20,28},{24,0},{28,4},{1,9},{5... | collective-permute-start | bytes 884744 | tf_op jit(solution)/shard_map/ppermute | solution.py:294
  51.7 11.1 %collective-permute-start.6 = (bf16[2,128,1024]{2,1,0:T(8,128)(2,1)S(1)}, bf16[2,128,1024]{2,1,0:T(8,128)(2,1)S(1)}, u32[]{:S(2)}, u32[]{:S(2)}) collective-permute-start(bf16[2,128,1024]{2,1,0:T(8,128)(2,1)S(1)} %pad_maximum_fusion.3), channel_id=1, source_target_pairs={{0,2},{1,3},{2,0},{3,1},{4,6},{5,7},{6,4},{7,5},{8,10},{9,11},{10,... | collective-permute-start | bytes 1572872 | tf_op jit(solution)/shard_map/ppermute | solution.py:369
  62.9 11.9 %collective-permute-start.9 = (bf16[2,128,1024]{2,1,0:T(8,128)(2,1)S(1)}, bf16[2,128,1024]{2,1,0:T(8,128)(2,1)S(1)}, u32[]{:S(2)}, u32[]{:S(2)}) collective-permute-start(bf16[2,128,1024]{2,1,0:T(8,128)(2,1)S(1)} %pad_maximum_fusion.4), channel_id=1, source_target_pairs={{0,2},{1,3},{2,0},{3,1},{4,6},{5,7},{6,4},{7,5},{8,10},{9,11},{10,... | collective-permute-start | bytes 1572872 | tf_op jit(solution)/shard_map/ppermute | solution.py:369
  88.7 24.8 %collective-permute-start.13 = (bf16[800,384]{1,0:T(8,128)(2,1)}, bf16[800,384]{1,0:T(8,128)(2,1)}, u32[]{:S(2)}, u32[]{:S(2)}) collective-permute-start(bf16[800,384]{1,0:T(8,128)(2,1)} %pad_maximum_fusion.2), channel_id=1, source_target_pairs={{0,8},{4,12},{8,16},{12,20},{16,24},{20,28},{24,0},{28,4},{1,9},{5... | collective-permute-start | bytes 1843208 | tf_op jit(solution)/shard_map/ppermute | solution.py:294
  88.7 26.9 %collective-permute-start.14 = (bf16[800,384]{1,0:T(8,128)(2,1)}, bf16[800,384]{1,0:T(8,128)(2,1)}, u32[]{:S(2)}, u32[]{:S(2)}) collective-permute-start(bf16[800,384]{1,0:T(8,128)(2,1)} %pad_maximum_fusion.2), channel_id=1, source_target_pairs={{0,4},{4,0},{8,12},{12,8},{16,20},{20,16},{24,28},{28,24},{1,5},{5... | collective-permute-start | bytes 1843208 | tf_op jit(solution)/shard_map/ppermute | solution.py:291
  92.4 23.3 %collective-permute-start.17 = (bf16[8,128,1024]{2,1,0:T(8,128)(2,1)}, bf16[8,128,1024]{2,1,0:T(8,128)(2,1)}, u32[]{:S(2)}, u32[]{:S(2)}) collective-permute-start(bf16[8,128,1024]{2,1,0:T(8,128)(2,1)} %slice.272), channel_id=1, source_target_pairs={{0,1},{1,0},{2,3},{3,2},{4,5},{5,4},{6,7},{7,6},{8,9},{9,8},{10,11... | collective-permute-start | bytes 6291464 | tf_op jit(solution)/shard_map/ppermute | solution.py:458
  101.5 14.1 %collective-permute-start.16 = (bf16[8,128,1024]{2,1,0:T(8,128)(2,1)}, bf16[8,128,1024]{2,1,0:T(8,128)(2,1)}, u32[]{:S(2)}, u32[]{:S(2)}) collective-permute-start(bf16[8,128,1024]{2,1,0:T(8,128)(2,1)} %bitcast.23), channel_id=1, source_target_pairs={{0,1},{1,0},{2,3},{3,2},{4,5},{5,4},{6,7},{7,6},{8,9},{9,8},{10,11... | collective-permute-start | bytes 6291464 | tf_op jit(solution)/shard_map/ppermute | solution.py:458
  107.4 60.1 %collective-permute-start.20 = (bf16[576,1024]{1,0:T(8,128)(2,1)}, bf16[576,1024]{1,0:T(8,128)(2,1)}, u32[]{:S(2)}, u32[]{:S(2)}) collective-permute-start(bf16[576,1024]{1,0:T(8,128)(2,1)} %shard_map.287), channel_id=1, source_target_pairs={{0,8},{4,12},{8,16},{12,20},{16,24},{20,28},{24,0},{28,4},{1,9},{5... | collective-permute-start | bytes 3538952 | tf_op jit(solution)/shard_map/ppermute | solution.py:294
  113.5 55.6 %collective-permute-start.21 = (bf16[576,1024]{1,0:T(8,128)(2,1)}, bf16[576,1024]{1,0:T(8,128)(2,1)}, u32[]{:S(2)}, u32[]{:S(2)}) collective-permute-start(bf16[576,1024]{1,0:T(8,128)(2,1)} %shard_map.287), channel_id=1, source_target_pairs={{0,4},{4,0},{8,12},{12,8},{16,20},{20,16},{24,28},{28,24},{1,5},{5... | collective-permute-start | bytes 3538952 | tf_op jit(solution)/shard_map/ppermute | solution.py:291
  115.6 53.5 %collective-permute-start.18 = (bf16[800,384]{1,0:T(8,128)(2,1)}, bf16[800,384]{1,0:T(8,128)(2,1)}, u32[]{:S(2)}, u32[]{:S(2)}) collective-permute-start(bf16[800,384]{1,0:T(8,128)(2,1)} %collective-permute-done.13), channel_id=1, source_target_pairs={{0,8},{4,12},{8,16},{12,20},{16,24},{20,28},{24,0},{28,4},{1,9},{5... | collective-permute-start | bytes 1843208 | tf_op jit(solution)/shard_map/ppermute | solution.py:294
  125.7 43.4 %collective-permute-start.19 = (bf16[800,384]{1,0:T(8,128)(2,1)}, bf16[800,384]{1,0:T(8,128)(2,1)}, u32[]{:S(2)}, u32[]{:S(2)}) collective-permute-start(bf16[800,384]{1,0:T(8,128)(2,1)} %collective-permute-done.13), channel_id=1, source_target_pairs={{0,4},{4,0},{8,12},{12,8},{16,20},{20,16},{24,28},{28,24},{1,5},{5... | collective-permute-start | bytes 1843208 | tf_op jit(solution)/shard_map/ppermute | solution.py:291
  139.4 29.7 %collective-permute-start.22 = (bf16[128,768]{1,0:T(8,128)(2,1)S(1)}, bf16[128,768]{1,0:T(8,128)(2,1)S(1)}, u32[]{:S(2)}, u32[]{:S(2)}) collective-permute-start(bf16[128,768]{1,0:T(8,128)(2,1)S(1)} %get-tuple-element.364), channel_id=1, source_target_pairs={{0,4},{4,0},{8,12},{12,8},{16,20},{20,16},{24,28},{28,24},{1,5},{5... | collective-permute-start | bytes 589832 | tf_op jit(solution)/shard_map/ppermute | solution.py:291
  145.7 16.4 %all-to-all-start = ((f32[8,16,384]{2,1,0:T(8,128)}), f32[8,16,384]{2,1,0:T(8,128)S(1)}, u32[]{:S(2)}, u32[]{:S(2)}) async-start(f32[8,16,384]{2,1,0:T(8,128)} %bitcast.290), calls=%async_computation | async-start | bytes 393216 | tf_op jit(solution)/shard_map/all_to_all | solution.py:1354
  167.5 28.4 %collective-permute-start.28 = (bf16[128,768]{1,0:T(8,128)(2,1)S(1)}, bf16[128,768]{1,0:T(8,128)(2,1)S(1)}, u32[]{:S(2)}, u32[]{:S(2)}) collective-permute-start(bf16[128,768]{1,0:T(8,128)(2,1)S(1)} %get-tuple-element.363), channel_id=1, source_target_pairs={{0,4},{4,0},{8,12},{12,8},{16,20},{20,16},{24,28},{28,24},{1,5},{5... | collective-permute-start | bytes 589832 | tf_op jit(solution)/shard_map/ppermute | solution.py:291
  169.1 53.1 %collective-permute-start.23 = (bf16[800,384]{1,0:T(8,128)(2,1)}, bf16[800,384]{1,0:T(8,128)(2,1)S(1)}, u32[]{:S(2)}, u32[]{:S(2)}) collective-permute-start(bf16[800,384]{1,0:T(8,128)(2,1)} %collective-permute-done.18), channel_id=1, source_target_pairs={{0,8},{4,12},{8,16},{12,20},{16,24},{20,28},{24,0},{28,4},{1,9},{5... | collective-permute-start | bytes 1843208 | tf_op jit(solution)/shard_map/ppermute | solution.py:294
  178.9 43.4 %collective-permute-start.24 = (bf16[800,384]{1,0:T(8,128)(2,1)}, bf16[800,384]{1,0:T(8,128)(2,1)S(1)}, u32[]{:S(2)}, u32[]{:S(2)}) collective-permute-start(bf16[800,384]{1,0:T(8,128)(2,1)} %collective-permute-done.18), channel_id=1, source_target_pairs={{0,4},{4,0},{8,12},{12,8},{16,20},{20,16},{24,28},{28,24},{1,5},{5... | collective-permute-start | bytes 1843208 | tf_op jit(solution)/shard_map/ppermute | solution.py:291
  179.2 43.1 %collective-permute-start.25 = (bf16[576,1024]{1,0:T(8,128)(2,1)}, bf16[576,1024]{1,0:T(8,128)(2,1)S(1)}, u32[]{:S(2)}, u32[]{:S(2)}) collective-permute-start(bf16[576,1024]{1,0:T(8,128)(2,1)} %collective-permute-done.20), channel_id=1, source_target_pairs={{0,8},{4,12},{8,16},{12,20},{16,24},{20,28},{24,0},{28,4},{1,9},{5... | collective-permute-start | bytes 3538952 | tf_op jit(solution)/shard_map/ppermute | solution.py:294
  182.5 39.7 %collective-permute-start.26 = (bf16[576,1024]{1,0:T(8,128)(2,1)}, bf16[576,1024]{1,0:T(8,128)(2,1)S(1)}, u32[]{:S(2)}, u32[]{:S(2)}) collective-permute-start(bf16[576,1024]{1,0:T(8,128)(2,1)} %collective-permute-done.20), channel_id=1, source_target_pairs={{0,4},{4,0},{8,12},{12,8},{16,20},{20,16},{24,28},{28,24},{1,5},{5... | collective-permute-start | bytes 3538952 | tf_op jit(solution)/shard_map/ppermute | solution.py:291
  195.8 26.1 %collective-permute-start.27 = (bf16[128,768]{1,0:T(8,128)(2,1)S(1)}, bf16[128,768]{1,0:T(8,128)(2,1)S(1)}, u32[]{:S(2)}, u32[]{:S(2)}) collective-permute-start(bf16[128,768]{1,0:T(8,128)(2,1)S(1)} %fusion.13), channel_id=1, source_target_pairs={{0,8},{4,12},{8,16},{12,20},{16,24},{20,28},{24,0},{28,4},{1,9},{5... | collective-permute-start | bytes 589832 | tf_op jit(solution)/shard_map/ppermute | solution.py:294
  221.9 12.9 %collective-permute-start.33 = (bf16[128,768]{1,0:T(8,128)(2,1)S(1)}, bf16[128,768]{1,0:T(8,128)(2,1)S(1)}, u32[]{:S(2)}, u32[]{:S(2)}) collective-permute-start(bf16[128,768]{1,0:T(8,128)(2,1)S(1)} %get-tuple-element.362), channel_id=1, source_target_pairs={{0,4},{4,0},{8,12},{12,8},{16,20},{20,16},{24,28},{28,24},{1,5},{5... | collective-permute-start | bytes 589832 | tf_op jit(solution)/shard_map/ppermute | solution.py:291
  222.3 48.4 %collective-permute-start.30 = (bf16[576,1024]{1,0:T(8,128)(2,1)S(1)}, bf16[576,1024]{1,0:T(8,128)(2,1)}, u32[]{:S(2)}, u32[]{:S(2)}) collective-permute-start(bf16[576,1024]{1,0:T(8,128)(2,1)S(1)} %collective-permute-done.25), channel_id=1, source_target_pairs={{0,8},{4,12},{8,16},{12,20},{16,24},{20,28},{24,0},{28,4},{1,9},{5... | collective-permute-start | bytes 3538952 | tf_op jit(solution)/shard_map/ppermute | solution.py:294
  225.7 44.9 %collective-permute-start.31 = (bf16[576,1024]{1,0:T(8,128)(2,1)S(1)}, bf16[576,1024]{1,0:T(8,128)(2,1)S(1)}, u32[]{:S(2)}, u32[]{:S(2)}) collective-permute-start(bf16[576,1024]{1,0:T(8,128)(2,1)S(1)} %collective-permute-done.25), channel_id=1, source_target_pairs={{0,4},{4,0},{8,12},{12,8},{16,20},{20,16},{24,28},{28,24},{1,5},{5... | collective-permute-start | bytes 3538952 | tf_op jit(solution)/shard_map/ppermute | solution.py:291
  227.4 43.2 %collective-permute-start.29 = (bf16[800,384]{1,0:T(8,128)(2,1)S(1)}, bf16[800,384]{1,0:T(8,128)(2,1)S(1)}, u32[]{:S(2)}, u32[]{:S(2)}) collective-permute-start(bf16[800,384]{1,0:T(8,128)(2,1)S(1)} %collective-permute-done.23), channel_id=1, source_target_pairs={{0,4},{4,0},{8,12},{12,8},{16,20},{20,16},{24,28},{28,24},{1,5},{5... | collective-permute-start | bytes 1843208 | tf_op jit(solution)/shard_map/ppermute | solution.py:291
  227.8 29.2 %collective-permute-start.32 = (bf16[128,768]{1,0:T(8,128)(2,1)S(1)}, bf16[128,768]{1,0:T(8,128)(2,1)S(1)}, u32[]{:S(2)}, u32[]{:S(2)}) collective-permute-start(bf16[128,768]{1,0:T(8,128)(2,1)S(1)} %fusion.10), channel_id=1, source_target_pairs={{0,8},{4,12},{8,16},{12,20},{16,24},{20,28},{24,0},{28,4},{1,9},{5... | collective-permute-start | bytes 589832 | tf_op jit(solution)/shard_map/ppermute | solution.py:294
  234.8 35.8 %collective-permute-start.35 = (bf16[128,768]{1,0:T(8,128)(2,1)S(1)}, bf16[128,768]{1,0:T(8,128)(2,1)S(1)}, u32[]{:S(2)}, u32[]{:S(2)}) collective-permute-start(bf16[128,768]{1,0:T(8,128)(2,1)S(1)} %get-tuple-element.361), channel_id=1, source_target_pairs={{0,4},{4,0},{8,12},{12,8},{16,20},{20,16},{24,28},{28,24},{1,5},{5... | collective-permute-start | bytes 589832 | tf_op jit(solution)/shard_map/ppermute | solution.py:291
  257.1 13.6 %collective-permute-start.34 = (bf16[128,768]{1,0:T(8,128)(2,1)S(1)}, bf16[128,768]{1,0:T(8,128)(2,1)S(1)}, u32[]{:S(2)}, u32[]{:S(2)}) collective-permute-start(bf16[128,768]{1,0:T(8,128)(2,1)S(1)} %fusion.12), channel_id=1, source_target_pairs={{0,8},{4,12},{8,16},{12,20},{16,24},{20,28},{24,0},{28,4},{1,9},{5... | collective-permute-start | bytes 589832 | tf_op jit(solution)/shard_map/ppermute | solution.py:294
  275.5 27.0 %collective-permute-start.36 = (bf16[576,1024]{1,0:T(8,128)(2,1)}, bf16[576,1024]{1,0:T(8,128)(2,1)}, u32[]{:S(2)}, u32[]{:S(2)}) collective-permute-start(bf16[576,1024]{1,0:T(8,128)(2,1)} %collective-permute-done.30), channel_id=1, source_target_pairs={{0,4},{4,0},{8,12},{12,8},{16,20},{20,16},{24,28},{28,24},{1,5},{5... | collective-permute-start | bytes 3538952 | tf_op jit(solution)/shard_map/ppermute | solution.py:291
  307.3 22.9 %collective-permute-start.40 = (bf16[256,384]{1,0:T(8,128)(2,1)}, bf16[256,384]{1,0:T(8,128)(2,1)}, u32[]{:S(2)}, u32[]{:S(2)}) collective-permute-start(bf16[256,384]{1,0:T(8,128)(2,1)} %pad_maximum_fusion.12), channel_id=1, source_target_pairs={{0,8},{4,12},{8,16},{12,20},{16,24},{20,28},{24,0},{28,4},{1,9},{5... | collective-permute-start | bytes 589832 | tf_op jit(solution)/shard_map/ppermute | solution.py:294
  310.3 19.9 %collective-permute-start.41 = (bf16[256,384]{1,0:T(8,128)(2,1)}, bf16[256,384]{1,0:T(8,128)(2,1)}, u32[]{:S(2)}, u32[]{:S(2)}) collective-permute-start(bf16[256,384]{1,0:T(8,128)(2,1)} %pad_maximum_fusion.12), channel_id=1, source_target_pairs={{0,4},{4,0},{8,12},{12,8},{16,20},{20,16},{24,28},{28,24},{1,5},{5... | collective-permute-start | bytes 589832 | tf_op jit(solution)/shard_map/ppermute | solution.py:291
  330.2 17.8 %collective-permute-start.42 = (bf16[256,384]{1,0:T(8,128)(2,1)}, bf16[256,384]{1,0:T(8,128)(2,1)S(1)}, u32[]{:S(2)}, u32[]{:S(2)}) collective-permute-start(bf16[256,384]{1,0:T(8,128)(2,1)} %collective-permute-done.40), channel_id=1, source_target_pairs={{0,8},{4,12},{8,16},{12,20},{16,24},{20,28},{24,0},{28,4},{1,9},{5... | collective-permute-start | bytes 589832 | tf_op jit(solution)/shard_map/ppermute | solution.py:294
  332.7 15.2 %collective-permute-start.44 = (bf16[256,384]{1,0:T(8,128)(2,1)}, bf16[256,384]{1,0:T(8,128)(2,1)S(1)}, u32[]{:S(2)}, u32[]{:S(2)}) collective-permute-start(bf16[256,384]{1,0:T(8,128)(2,1)} %collective-permute-done.40), channel_id=1, source_target_pairs={{0,4},{4,0},{8,12},{12,8},{16,20},{20,16},{24,28},{28,24},{1,5},{5... | collective-permute-start | bytes 589832 | tf_op jit(solution)/shard_map/ppermute | solution.py:291
  334.3 13.7 %collective-permute-start.43 = (bf16[2,128,384]{2,1,0:T(8,128)(2,1)S(1)}, bf16[2,128,384]{2,1,0:T(8,128)(2,1)S(1)}, u32[]{:S(2)}, u32[]{:S(2)}) collective-permute-start(bf16[2,128,384]{2,1,0:T(8,128)(2,1)S(1)} %pad_maximum_fusion.13), channel_id=1, source_target_pairs={{0,2},{1,3},{2,0},{3,1},{4,6},{5,7},{6,4},{7,5},{8,10},{9,11},{10,... | collective-permute-start | bytes 589832 | tf_op jit(solution)/shard_map/ppermute | solution.py:369
  347.9 20.4 %collective-permute-start.48 = (bf16[256,384]{1,0:T(8,128)(2,1)S(1)}, bf16[256,384]{1,0:T(8,128)(2,1)}, u32[]{:S(2)}, u32[]{:S(2)}) collective-permute-start(bf16[256,384]{1,0:T(8,128)(2,1)S(1)} %collective-permute-done.42), channel_id=1, source_target_pairs={{0,8},{4,12},{8,16},{12,20},{16,24},{20,28},{24,0},{28,4},{1,9},{5... | collective-permute-start | bytes 589832 | tf_op jit(solution)/shard_map/ppermute | solution.py:294
  350.8 17.5 %collective-permute-start.50 = (bf16[256,384]{1,0:T(8,128)(2,1)S(1)}, bf16[256,384]{1,0:T(8,128)(2,1)S(1)}, u32[]{:S(2)}, u32[]{:S(2)}) collective-permute-start(bf16[256,384]{1,0:T(8,128)(2,1)S(1)} %collective-permute-done.42), channel_id=1, source_target_pairs={{0,4},{4,0},{8,12},{12,8},{16,20},{20,16},{24,28},{28,24},{1,5},{5... | collective-permute-start | bytes 589832 | tf_op jit(solution)/shard_map/ppermute | solution.py:291
  351.9 16.4 %collective-permute-start.49 = (bf16[2,128,384]{2,1,0:T(8,128)(2,1)S(1)}, bf16[2,128,384]{2,1,0:T(8,128)(2,1)S(1)}, u32[]{:S(2)}, u32[]{:S(2)}) collective-permute-start(bf16[2,128,384]{2,1,0:T(8,128)(2,1)S(1)} %pad_maximum_fusion.14), channel_id=1, source_target_pairs={{0,2},{1,3},{2,0},{3,1},{4,6},{5,7},{6,4},{7,5},{8,10},{9,11},{10,... | collective-permute-start | bytes 589832 | tf_op jit(solution)/shard_map/ppermute | solution.py:369
  368.4 21.4 %collective-permute-start.51 = (bf16[2,128,384]{2,1,0:T(8,128)(2,1)S(1)}, bf16[2,128,384]{2,1,0:T(8,128)(2,1)S(1)}, u32[]{:S(2)}, u32[]{:S(2)}) collective-permute-start(bf16[2,128,384]{2,1,0:T(8,128)(2,1)S(1)} %pad_maximum_fusion.15), channel_id=1, source_target_pairs={{0,2},{1,3},{2,0},{3,1},{4,6},{5,7},{6,4},{7,5},{8,10},{9,11},{10,... | collective-permute-start | bytes 589832 | tf_op jit(solution)/shard_map/ppermute | solution.py:369
  369.9 19.9 %collective-permute-start.52 = (bf16[256,384]{1,0:T(8,128)(2,1)}, bf16[256,384]{1,0:T(8,128)(2,1)S(1)}, u32[]{:S(2)}, u32[]{:S(2)}) collective-permute-start(bf16[256,384]{1,0:T(8,128)(2,1)} %collective-permute-done.48), channel_id=1, source_target_pairs={{0,4},{4,0},{8,12},{12,8},{16,20},{20,16},{24,28},{28,24},{1,5},{5... | collective-permute-start | bytes 589832 | tf_op jit(solution)/shard_map/ppermute | solution.py:291
  374.8 29.0 %collective-permute-start.53 = (bf16[576,1024]{1,0:T(8,128)(2,1)S(1)}, bf16[576,1024]{1,0:T(8,128)(2,1)S(1)}, u32[]{:S(2)}, u32[]{:S(2)}) collective-permute-start(bf16[576,1024]{1,0:T(8,128)(2,1)S(1)} %get-tuple-element.354), channel_id=1, source_target_pairs={{0,4},{4,0},{8,12},{12,8},{16,20},{20,16},{24,28},{28,24},{1,5},{5... | collective-permute-start | bytes 3538952 | tf_op jit(solution)/shard_map/ppermute | solution.py:291
  376.1 53.9 %collective-permute-start.58 = (bf16[576,1024]{1,0:T(8,128)(2,1)}, bf16[576,1024]{1,0:T(8,128)(2,1)}, u32[]{:S(2)}, u32[]{:S(2)}) collective-permute-start(bf16[576,1024]{1,0:T(8,128)(2,1)} %get-tuple-element.353), channel_id=1, source_target_pairs={{0,4},{4,0},{8,12},{12,8},{16,20},{20,16},{24,28},{28,24},{1,5},{5... | collective-permute-start | bytes 3538952 | tf_op jit(solution)/shard_map/ppermute | solution.py:291
  403.8 19.1 %collective-permute-start.59 = (bf16[128,384]{1,0:T(8,128)(2,1)S(1)}, bf16[128,384]{1,0:T(8,128)(2,1)S(1)}, u32[]{:S(2)}, u32[]{:S(2)}) collective-permute-start(bf16[128,384]{1,0:T(8,128)(2,1)S(1)} %constant_dynamic-slice_fusion), channel_id=1, source_target_pairs={{0,8},{4,12},{8,16},{12,20},{16,24},{20,28},{24,0},{28,4},{1,9},{5... | collective-permute-start | bytes 294920 | tf_op jit(solution)/shard_map/ppermute | solution.py:294
  404.2 24.7 %collective-permute-start.60 = (bf16[128,384]{1,0:T(8,128)(2,1)S(1)}, bf16[128,384]{1,0:T(8,128)(2,1)S(1)}, u32[]{:S(2)}, u32[]{:S(2)}) collective-permute-start(bf16[128,384]{1,0:T(8,128)(2,1)S(1)} %constant_dynamic-slice_fusion), channel_id=1, source_target_pairs={{0,4},{4,0},{8,12},{12,8},{16,20},{20,16},{24,28},{28,24},{1,5},{5... | collective-permute-start | bytes 294920 | tf_op jit(solution)/shard_map/ppermute | solution.py:291
  408.0 27.8 %collective-permute-start.57 = (bf16[576,1024]{1,0:T(8,128)(2,1)}, bf16[576,1024]{1,0:T(8,128)(2,1)}, u32[]{:S(2)}, u32[]{:S(2)}) collective-permute-start(bf16[576,1024]{1,0:T(8,128)(2,1)} %fusion.1), channel_id=1, source_target_pairs={{0,8},{4,12},{8,16},{12,20},{16,24},{20,28},{24,0},{28,4},{1,9},{5... | collective-permute-start | bytes 3538952 | tf_op jit(solution)/shard_map/ppermute | solution.py:294
  408.8 27.0 %collective-permute-start.64 = (bf16[2,128,384]{2,1,0:T(8,128)(2,1)}, bf16[2,128,384]{2,1,0:T(8,128)(2,1)}, u32[]{:S(2)}, u32[]{:S(2)}) collective-permute-start(bf16[2,128,384]{2,1,0:T(8,128)(2,1)} %pad_maximum_fusion.17), channel_id=1, source_target_pairs={{0,2},{1,3},{2,0},{3,1},{4,6},{5,7},{6,4},{7,5},{8,10},{9,11},{10,... | collective-permute-start | bytes 589832 | tf_op jit(solution)/shard_map/ppermute | solution.py:369
  434.7 37.5 %collective-permute-start.66 = (bf16[576,1024]{1,0:T(8,128)(2,1)S(1)}, bf16[576,1024]{1,0:T(8,128)(2,1)S(1)}, u32[]{:S(2)}, u32[]{:S(2)}) collective-permute-start(bf16[576,1024]{1,0:T(8,128)(2,1)S(1)} %get-tuple-element.352), channel_id=1, source_target_pairs={{0,4},{4,0},{8,12},{12,8},{16,20},{20,16},{24,28},{28,24},{1,5},{5... | collective-permute-start | bytes 3538952 | tf_op jit(solution)/shard_map/ppermute | solution.py:291
  436.2 26.8 %collective-permute-start.71 = (bf16[128,384]{1,0:T(8,128)(2,1)S(1)}, bf16[128,384]{1,0:T(8,128)(2,1)S(1)}, u32[]{:S(2)}, u32[]{:S(2)}) collective-permute-start(bf16[128,384]{1,0:T(8,128)(2,1)S(1)} %collective-permute-done.61), channel_id=1, source_target_pairs={{0,4},{4,0},{8,12},{12,8},{16,20},{20,16},{24,28},{28,24},{1,5},{5... | collective-permute-start | bytes 294920 | tf_op jit(solution)/shard_map/ppermute | solution.py:291
  437.2 26.7 %collective-permute-start.70 = (bf16[2,128,384]{2,1,0:T(8,128)(2,1)S(1)}, bf16[2,128,384]{2,1,0:T(8,128)(2,1)S(1)}, u32[]{:S(2)}, u32[]{:S(2)}) collective-permute-start(bf16[2,128,384]{2,1,0:T(8,128)(2,1)S(1)} %pad_maximum_fusion.18), channel_id=1, source_target_pairs={{0,2},{1,3},{2,0},{3,1},{4,6},{5,7},{6,4},{7,5},{8,10},{9,11},{10,... | collective-permute-start | bytes 589832 | tf_op jit(solution)/shard_map/ppermute | solution.py:369
  438.5 25.8 %collective-permute-start.74 = (bf16[64,1536]{1,0:T(8,128)(2,1)S(1)}, bf16[64,1536]{1,0:T(8,128)(2,1)S(1)}, u32[]{:S(2)}, u32[]{:S(2)}) collective-permute-start(bf16[64,1536]{1,0:T(8,128)(2,1)S(1)} %broadcast_select_fusion.3), channel_id=1, source_target_pairs={{0,1},{1,0},{2,3},{3,2},{4,5},{5,4},{6,7},{7,6},{8,9},{9,8},{10,11... | collective-permute-start | bytes 589832 | tf_op jit(solution)/shard_map/ppermute | solution.py:510
  446.3 32.3 %collective-permute-start.67 = (bf16[640,384]{1,0:T(8,128)(2,1)S(1)}, bf16[640,384]{1,0:T(8,128)(2,1)S(1)}, u32[]{:S(2)}, u32[]{:S(2)}) collective-permute-start(bf16[640,384]{1,0:T(8,128)(2,1)S(1)} %copy-done.59), channel_id=1, source_target_pairs={{0,8},{4,12},{8,16},{12,20},{16,24},{20,28},{24,0},{28,4},{1,9},{5... | collective-permute-start | bytes 1474568 | tf_op jit(solution)/shard_map/ppermute | solution.py:294
  463.0 16.3 %collective-permute-start.68 = (bf16[640,384]{1,0:T(8,128)(2,1)S(1)}, bf16[640,384]{1,0:T(8,128)(2,1)S(1)}, u32[]{:S(2)}, u32[]{:S(2)}) collective-permute-start(bf16[640,384]{1,0:T(8,128)(2,1)S(1)} %copy-done.59), channel_id=1, source_target_pairs={{0,4},{4,0},{8,12},{12,8},{16,20},{20,16},{24,28},{28,24},{1,5},{5... | collective-permute-start | bytes 1474568 | tf_op jit(solution)/shard_map/ppermute | solution.py:291
  464.0 24.9 %collective-permute-start.65 = (bf16[576,1024]{1,0:T(8,128)(2,1)S(1)}, bf16[576,1024]{1,0:T(8,128)(2,1)S(1)}, u32[]{:S(2)}, u32[]{:S(2)}) collective-permute-start(bf16[576,1024]{1,0:T(8,128)(2,1)S(1)} %fusion.3), channel_id=1, source_target_pairs={{0,8},{4,12},{8,16},{12,20},{16,24},{20,28},{24,0},{28,4},{1,9},{5... | collective-permute-start | bytes 3538952 | tf_op jit(solution)/shard_map/ppermute | solution.py:294
  477.0 26.9 %collective-permute-start.78 = (bf16[576,1024]{1,0:T(8,128)(2,1)S(1)}, bf16[576,1024]{1,0:T(8,128)(2,1)S(1)}, u32[]{:S(2)}, u32[]{:S(2)}) collective-permute-start(bf16[576,1024]{1,0:T(8,128)(2,1)S(1)} %get-tuple-element.351), channel_id=1, source_target_pairs={{0,4},{4,0},{8,12},{12,8},{16,20},{20,16},{24,28},{28,24},{1,5},{5... | collective-permute-start | bytes 3538952 | tf_op jit(solution)/shard_map/ppermute | solution.py:291
  478.7 29.0 %collective-permute-start.83 = (bf16[8,128,384]{2,1,0:T(8,128)(2,1)S(1)}, bf16[8,128,384]{2,1,0:T(8,128)(2,1)S(1)}, u32[]{:S(2)}, u32[]{:S(2)}) collective-permute-start(bf16[8,128,384]{2,1,0:T(8,128)(2,1)S(1)} %slice.280.rest_0_), channel_id=1, source_target_pairs={{0,1},{1,0},{2,3},{3,2},{4,5},{5,4},{6,7},{7,6},{8,9},{9,8},{10,11... | collective-permute-start | bytes 2359304 | tf_op jit(solution)/shard_map/ppermute | solution.py:458
  478.7 30.6 %collective-permute-start.82 = (bf16[8,128,384]{2,1,0:T(8,128)(2,1)S(1)}, bf16[8,128,384]{2,1,0:T(8,128)(2,1)S(1)}, u32[]{:S(2)}, u32[]{:S(2)}) collective-permute-start(bf16[8,128,384]{2,1,0:T(8,128)(2,1)S(1)} %bitcast.306), channel_id=1, source_target_pairs={{0,1},{1,0},{2,3},{3,2},{4,5},{5,4},{6,7},{7,6},{8,9},{9,8},{10,11... | collective-permute-start | bytes 2359304 | tf_op jit(solution)/shard_map/ppermute | solution.py:458
  490.9 36.5 %collective-permute-start.77 = (bf16[576,1024]{1,0:T(8,128)(2,1)S(1)}, bf16[576,1024]{1,0:T(8,128)(2,1)S(1)}, u32[]{:S(2)}, u32[]{:S(2)}) collective-permute-start(bf16[576,1024]{1,0:T(8,128)(2,1)S(1)} %fusion.5), channel_id=1, source_target_pairs={{0,8},{4,12},{8,16},{12,20},{16,24},{20,28},{24,0},{28,4},{1,9},{5... | collective-permute-start | bytes 3538952 | tf_op jit(solution)/shard_map/ppermute | solution.py:294
  491.0 36.5 %collective-permute-start.79 = (bf16[640,384]{1,0:T(8,128)(2,1)S(1)}, bf16[640,384]{1,0:T(8,128)(2,1)}, u32[]{:S(2)}, u32[]{:S(2)}) collective-permute-start(bf16[640,384]{1,0:T(8,128)(2,1)S(1)} %collective-permute-done.67), channel_id=1, source_target_pairs={{0,8},{4,12},{8,16},{12,20},{16,24},{20,28},{24,0},{28,4},{1,9},{5... | collective-permute-start | bytes 1474568 | tf_op jit(solution)/shard_map/ppermute | solution.py:294
  503.9 23.6 %collective-permute-start.80 = (bf16[640,384]{1,0:T(8,128)(2,1)S(1)}, bf16[640,384]{1,0:T(8,128)(2,1)S(1)}, u32[]{:S(2)}, u32[]{:S(2)}) collective-permute-start(bf16[640,384]{1,0:T(8,128)(2,1)S(1)} %collective-permute-done.67), channel_id=1, source_target_pairs={{0,4},{4,0},{8,12},{12,8},{16,20},{20,16},{24,28},{28,24},{1,5},{5... | collective-permute-start | bytes 1474568 | tf_op jit(solution)/shard_map/ppermute | solution.py:291
  509.3 40.6 %collective-permute-start.87 = (bf16[8,128,384]{2,1,0:T(8,128)(2,1)S(1)}, bf16[8,128,384]{2,1,0:T(8,128)(2,1)}, u32[]{:S(2)}, u32[]{:S(2)}) collective-permute-start(bf16[8,128,384]{2,1,0:T(8,128)(2,1)S(1)} %bitcast.304), channel_id=1, source_target_pairs={{0,1},{1,0},{2,3},{3,2},{4,5},{5,4},{6,7},{7,6},{8,9},{9,8},{10,11... | collective-permute-start | bytes 2359304 | tf_op jit(solution)/shard_map/ppermute | solution.py:458
  527.5 22.4 %collective-permute-start.84 = (bf16[640,384]{1,0:T(8,128)(2,1)}, bf16[640,384]{1,0:T(8,128)(2,1)}, u32[]{:S(2)}, u32[]{:S(2)}) collective-permute-start(bf16[640,384]{1,0:T(8,128)(2,1)} %collective-permute-done.79), channel_id=1, source_target_pairs={{0,8},{4,12},{8,16},{12,20},{16,24},{20,28},{24,0},{28,4},{1,9},{5... | collective-permute-start | bytes 1474568 | tf_op jit(solution)/shard_map/ppermute | solution.py:294
  527.6 22.3 %collective-permute-start.85 = (bf16[640,384]{1,0:T(8,128)(2,1)}, bf16[640,384]{1,0:T(8,128)(2,1)}, u32[]{:S(2)}, u32[]{:S(2)}) collective-permute-start(bf16[640,384]{1,0:T(8,128)(2,1)} %collective-permute-done.79), channel_id=1, source_target_pairs={{0,4},{4,0},{8,12},{12,8},{16,20},{20,16},{24,28},{28,24},{1,5},{5... | collective-permute-start | bytes 1474568 | tf_op jit(solution)/shard_map/ppermute | solution.py:291
  529.3 20.6 %collective-permute-start.86 = (bf16[8,128,384]{2,1,0:T(8,128)(2,1)}, bf16[8,128,384]{2,1,0:T(8,128)(2,1)}, u32[]{:S(2)}, u32[]{:S(2)}) collective-permute-start(bf16[8,128,384]{2,1,0:T(8,128)(2,1)} %bitcast.130.rest_6_), channel_id=1, source_target_pairs={{0,1},{1,0},{2,3},{3,2},{4,5},{5,4},{6,7},{7,6},{8,9},{9,8},{10,11... | collective-permute-start | bytes 2359304 | tf_op jit(solution)/shard_map/ppermute | solution.py:458
  549.9 16.3 %collective-permute-start.91 = (bf16[640,384]{1,0:T(8,128)(2,1)}, bf16[640,384]{1,0:T(8,128)(2,1)S(1)}, u32[]{:S(2)}, u32[]{:S(2)}) collective-permute-start(bf16[640,384]{1,0:T(8,128)(2,1)} %collective-permute-done.84), channel_id=1, source_target_pairs={{0,4},{4,0},{8,12},{12,8},{16,20},{20,16},{24,28},{28,24},{1,5},{5... | collective-permute-start | bytes 1474568 | tf_op jit(solution)/shard_map/ppermute | solution.py:291
  (105 other events, 1553.2 us)

commit v3 on v2

--- a/solution.py
+++ b/solution.py
@@ -856,20 +856,19 @@
     )(query, key, value, text_lin, seg, seg_row, gains, w_out)
 
 
-def ffn_forward(layout, held, tokens, attn_out, seg, mods, norms, w_down):
+def ffn_forward(layout, held, tokens, attn_out, seg, mods, norms):
     length, depth = tokens.shape
     width = layout.width
-    counts = [len(layout.spans(i * depth, (i + 1) * depth)) for i in range(2)]
+    counts = [len(layout.spans(i * depth, (i + 1) * depth)) for i in range(3)]
 
     def kernel(
-        held_ref, x_ref, branch_ref, seg_ref, mod_ref, norm_ref, down_hbm,
-        middle_ref, ffn_in_ref, gate_ref, up_ref, hidden_ref, part_ref,
-        wg_ref, wu_ref, wd_ref, sems,
+        held_ref, x_ref, branch_ref, seg_ref, mod_ref, norm_ref,
+        middle_ref, ffn_in_ref, gate_ref, up_ref, hidden_ref, part_ref, wd_ref,
+        wg_ref, wu_ref, flat_ref, woven_ref, plain_ref, sems,
     ):
+        for_down = Fetch(held_ref, layout, 2 * depth, 3 * depth, flat_ref, sems, sum(counts[:2]))
         for_gate = Fetch(held_ref, layout, 0, depth, wg_ref, sems, 0)
         for_up = Fetch(held_ref, layout, depth, 2 * depth, wu_ref, sems, counts[0])
-        for_down = pltpu.make_async_copy(down_hbm, wd_ref, sems.at[sum(counts)])
-        for_down.start()
         seg = seg_ref[...]
         branch = branch_ref[...].astype(F32)
         unit = branch * lax.rsqrt(row_mean(branch * branch) + EPS)
@@ -879,6 +878,18 @@
         unit = middle * lax.rsqrt(row_mean(middle * middle) + EPS)
         ffn_in = (unit * norm_ref[2:3, :] * (1.0 + per_token(seg, mod_ref, 2))).astype(BF16)
         ffn_in_ref[...] = ffn_in
+        for_down.wait()
+        for j in range(width // LANES):
+            woven_ref[j] = flat_ref[:, j * LANES : (j + 1) * LANES].astype(F32)
+        half = width // 2
+        for parity in range(2):
+            for i in range(depth // LANES):
+                at = parity * depth + i * LANES
+                plain_ref[i, pl.ds(parity, half, stride=2), :] = woven_ref[
+                    at % width // LANES, pl.ds(at // width, half, stride=3), :
+                ]
+        for i in range(depth // LANES):
+            wd_ref[:, i * LANES : (i + 1) * LANES] = plain_ref[i].astype(BF16)
         for_gate.wait()
         gate = dot(ffn_in, wg_ref[...])
         gate_ref[...] = gate
@@ -887,7 +898,6 @@
         up_ref[...] = up
         hidden = (jax.nn.silu(gate) * up).astype(BF16)
         hidden_ref[...] = hidden
-        for_down.wait()
         part_ref[...] = dot(hidden, wd_ref[...]).astype(BF16)
 
     def like(columns, kind):
@@ -902,17 +912,20 @@
             like(width, F32),
             like(width, BF16),
             like(depth, BF16),
+            jax.ShapeDtypeStruct((width, depth), BF16),
         ),
-        in_specs=[ANY] + [VMEM] * 5 + [ANY],
-        out_specs=(VMEM,) * 6,
+        in_specs=[ANY] + [VMEM] * 5,
+        out_specs=(VMEM,) * 7,
         scratch_shapes=[
             pltpu.VMEM((depth, width), BF16),
             pltpu.VMEM((depth, width), BF16),
-            pltpu.VMEM((width, depth), BF16),
-            pltpu.SemaphoreType.DMA((sum(counts) + 1,)),
+            pltpu.VMEM((depth, width), BF16),
+            pltpu.VMEM((width // LANES, depth, LANES), F32),
+            pltpu.VMEM((depth // LANES, width, LANES), F32),
+            pltpu.SemaphoreType.DMA((sum(counts),)),
         ],
         compiler_params=params(56),
-    )(held, tokens, attn_out, seg, mods, norms, w_down)
+    )(held, tokens, attn_out, seg, mods, norms)
 
 
 def ffn_backward(
@@ -1377,14 +1390,11 @@
     ffn_all = ffn_run.result()
 
     ffn_all, near_in = join([], ffn_all, jnp.concatenate([own_cut(normed), mixed], 0))
-    w_down = ffn_lay.pick(ffn_all, 2 * model_width, 3 * model_width).reshape(
-        hidden_width, model_width
-    )
     in_run = Shared(ring, near_in, index, length)
     early = [in_run.send()]
-    middle, ffn_in, gate, up, hidden, ffn_part = join(
+    middle, ffn_in, gate, up, hidden, ffn_part, w_down = join(
         early,
-        *ffn_forward(ffn_lay, ffn_all, tokens_in, attn_out, seg, mods, norms, w_down),
+        *ffn_forward(ffn_lay, ffn_all, tokens_in, attn_out, seg, mods, norms),
     )
     step(early)
     ffn_out = join(early, sum_mp(ffn_part))

time: 623 us -> 610 us (0.979)
  local copies, waits for them, and re-layouts: 113 us -> 98.8 us
  transfers between devices with their start and end apart: 93 -> 93, of which waited for: 37 -> 37; matrix products, arithmetic and copies ran while one was open for 20% -> 17% of each run, Pallas kernels for 11% -> 11%
where the time goes in v3:
time: 610 us; the launch traced here: 600 us
  waiting for transfers between devices  205 us (34%)
  starting transfers between devices  145 us (24%)
  Pallas kernels  110 us (18%)
  local copies, waits for them, and re-layouts  98.8 us (16%)
  other arithmetic  32.4 us (5%)
    ppermute x24, waiting for transfers between devices, onward(): return lax.ppermute(block, 'dp', self.next)  76.2 us
    ppermute x24, starting transfers between devices, onward(): return lax.ppermute(block, 'dp', self.next)  67.6 us
    ppermute x32, waiting for transfers between devices, swap(): return lax.ppermute(block, 'dp', self.pair)  61.1 us
    ppermute x32, starting transfers between devices, swap(): return lax.ppermute(block, 'dp', self.pair)  38.2 us
    dynamic_update_slice x46, local copies, waits for them, and re-layouts, put(): lax.dynamic_update_slice(self.held, value[None, None], (slot, side) + (se...  37.4 us
    ppermute x12, waiting for transfers between devices, send(): self.sent['far'] = lax.ppermute(self.chunk, 'mp', pairs)  28.4 us
    pallas_call x2, Pallas kernels, adamw_flat(): pl.pallas_call(kernel, grid=(steps,), out_shape=(like, like, like, like,...  24 us
    pallas_call x1, Pallas kernels, shard_gradient(): pl.pallas_call(kernel, grid=(packs // step_packs,), out_shape=jax.ShapeDt...  21.4 us
  transfers between devices with their start and end apart: 93, of which 37 were waited for; matrix products, arithmetic and copies ran while one was open for 17% of the time, Pallas kernels for 11%

profile of v3, /device:TPU:8, one launch (start us, length us, event | category | flops | bytes accessed | tf_op | source)
XLA Modules:
  0.0 600.0 jit_solution(5243250993498811249)
XLA Ops:
  1.6 3.4 collective-permute-start
  19.6 2.6 collective-permute-start.1
  26.4 23.2 %collective-permute-start.5 = (bf16[144,1024]{1,0:T(8,128)(2,1)S(1)}, bf16[144,1024]{1,0:T(8,128)(2,1)S(1)}, u32[]{:S(2)}, u32[]{:S(2)}) collective-permute-start(bf16[144,1024]{1,0:T(8,128)(2,1)S(1)} %collective-permute-done.3), channel_id=1, source_target_pairs={{0,8},{4,12},{8,16},{12,20},{16,24},{20,28},{24,0},{28,4},{1,9},{5... | collective-permute-start | bytes 884744 | tf_op jit(solution)/shard_map/ppermute | solution.py:294
  53.6 2.3 collective-permute-done.5
  56.3 6.4 %collective-permute-done.6 = bf16[2,128,1024]{2,1,0:T(8,128)(2,1)S(1)} collective-permute-done((bf16[2,128,1024]{2,1,0:T(8,128)(2,1)S(1)}, bf16[2,128,1024]{2,1,0:T(8,128)(2,1)S(1)}, u32[]{:S(2)}, u32[]{:S(2)}) %collective-permute-start.6) | collective-permute-done | bytes 524320 | tf_op jit(solution)/shard_map/ppermute | solution.py:369
  69.7 5.1 collective-permute-done.9
  81.8 5.8 collective-permute-done.11
  93.8 6.2 %collective-permute-done.15 = bf16[2,128,1024]{2,1,0:T(8,128)(2,1)S(1)} collective-permute-done((bf16[2,128,1024]{2,1,0:T(8,128)(2,1)S(1)}, bf16[2,128,1024]{2,1,0:T(8,128)(2,1)S(1)}, u32[]{:S(2)}, u32[]{:S(2)}) %collective-permute-start.15) | collective-permute-done | bytes 524320 | tf_op jit(solution)/shard_map/ppermute | solution.py:369
  101.5 4.3 fusion.7
  115.6 10.0 %collective-permute-start.18 = (bf16[800,384]{1,0:T(8,128)(2,1)}, bf16[800,384]{1,0:T(8,128)(2,1)}, u32[]{:S(2)}, u32[]{:S(2)}) collective-permute-start(bf16[800,384]{1,0:T(8,128)(2,1)} %collective-permute-done.13), channel_id=1, source_target_pairs={{0,8},{4,12},{8,16},{12,20},{16,24},{20,28},{24,0},{28,4},{1,9},{5... | collective-permute-start | bytes 1843208 | tf_op jit(solution)/shard_map/ppermute | solution.py:294
  129.5 3.3 copy-done.37
  132.8 6.5 %shard_map.289 = bf16[8,128,768]{2,1,0:T(8,128)(2,1)S(1)} custom-call(s32[2]{0:T(128)S(1)} %pad_add_fusion.place_ref, bf16[2432,384]{1,0:T(8,128)(2,1)S(1)} %shard_map.286.w_ref, bf16[4,8,128,1024]{3,2,1,0:T(8,128)(2,1)} %copy-done.37), custom_call_target="tpu_custom_call" | custom-call | tf_op jit(solution)/shard_map/pallas_call | solution.py:760
  139.4 6.3 %collective-permute-start.22 = (bf16[128,768]{1,0:T(8,128)(2,1)S(1)}, bf16[128,768]{1,0:T(8,128)(2,1)S(1)}, u32[]{:S(2)}, u32[]{:S(2)}) collective-permute-start(bf16[128,768]{1,0:T(8,128)(2,1)S(1)} %get-tuple-element.366), channel_id=1, source_target_pairs={{0,4},{4,0},{8,12},{12,8},{16,20},{20,16},{24,28},{28,24},{1,5},{5... | collective-permute-start | bytes 589832 | tf_op jit(solution)/shard_map/ppermute | solution.py:291
  145.7 5.8 all-to-all-start
  151.5 2.6 broadcast_in_dim.314
  157.0 5.1 all-to-all-done
  162.1 5.3 all_gather.3.mod_ref
  169.1 9.8 %collective-permute-start.23 = (bf16[800,384]{1,0:T(8,128)(2,1)}, bf16[800,384]{1,0:T(8,128)(2,1)S(1)}, u32[]{:S(2)}, u32[]{:S(2)}) collective-permute-start(bf16[800,384]{1,0:T(8,128)(2,1)} %collective-permute-done.18), channel_id=1, source_target_pairs={{0,8},{4,12},{8,16},{12,20},{16,24},{20,28},{24,0},{28,4},{1,9},{5... | collective-permute-start | bytes 1843208 | tf_op jit(solution)/shard_map/ppermute | solution.py:294
  179.2 3.4 collective-permute-start.25
  184.3 4.7 broadcast_in_dim.275
  189.0 2.4 bitcast_dynamic-update-slice_fusion.11
  191.4 2.4 bitcast_dynamic-update-slice_fusion.10
  197.9 24.0 %collective-permute-done.27 = bf16[128,768]{1,0:T(8,128)(2,1)S(1)} collective-permute-done((bf16[128,768]{1,0:T(8,128)(2,1)S(1)}, bf16[128,768]{1,0:T(8,128)(2,1)S(1)}, u32[]{:S(2)}, u32[]{:S(2)}) %collective-permute-start.27) | collective-permute-done | bytes 196640 | tf_op jit(solution)/shard_map/ppermute | solution.py:294
  222.3 3.4 collective-permute-start.30
  227.8 2.5 collective-permute-start.32
  231.4 2.4 bitcast_dynamic-update-slice_fusion.8
  236.5 20.5 %collective-permute-done.32 = bf16[128,768]{1,0:T(8,128)(2,1)S(1)} collective-permute-done((bf16[128,768]{1,0:T(8,128)(2,1)S(1)}, bf16[128,768]{1,0:T(8,128)(2,1)S(1)}, u32[]{:S(2)}, u32[]{:S(2)}) %collective-permute-start.32) | collective-permute-done | bytes 196640 | tf_op jit(solution)/shard_map/ppermute | solution.py:294
  259.1 11.5 %collective-permute-done.35 = bf16[128,768]{1,0:T(8,128)(2,1)S(1)} collective-permute-done((bf16[128,768]{1,0:T(8,128)(2,1)S(1)}, bf16[128,768]{1,0:T(8,128)(2,1)S(1)}, u32[]{:S(2)}, u32[]{:S(2)}) %collective-permute-start.35) | collective-permute-done | bytes 196640 | tf_op jit(solution)/shard_map/ppermute | solution.py:291
  277.5 2.4 reshape.283.w_ref.wo_ref
  281.9 3.7 shard_map.290
  286.4 4.6 shard_map.291
  295.4 4.4 collective-permute-done.38
  302.5 2.4 bitcast_dynamic-update-slice_fusion.5
  304.9 2.4 bitcast_dynamic-update-slice_fusion.4
  307.3 3.0 collective-permute-start.40
  311.6 8.4 %shard_map.292 = (f32[128,1536]{1,0:T(8,128)}, bf16[128,1536]{1,0:T(8,128)(2,1)}, f32[128,1024]{1,0:T(8,128)}, f32[128,1024]{1,0:T(8,128)}, bf16[128,1024]{1,0:T...) custom-call(bf16[8,576,1024]{2,1,0:T(8,128)(2,1)} %bitcast.70.held_ref, bf16[128,1536]{1,0:T(8,128)(2,1)} %x_ref.8, ...), custom_call_target="tpu_custom_call" | custom-call | tf_op jit(solution)/shard_map/pallas_call | solution.py:906
  320.1 2.5 collective-permute-start.42
  328.1 6.4 %collective-permute-done.46 = bf16[64,1536]{1,0:T(8,128)(2,1)S(1)} collective-permute-done((bf16[64,1536]{1,0:T(8,128)(2,1)S(1)}, bf16[64,1536]{1,0:T(8,128)(2,1)S(1)}, u32[]{:S(2)}, u32[]{:S(2)}) %collective-permute-start.46) | collective-permute-done | bytes 196640 | tf_op jit(solution)/shard_map/ppermute | solution.py:515
  336.9 2.9 collective-permute-start.48
  341.6 14.6 %shard_map.293 = (bf16[128,1536]{1,0:T(8,128)(2,1)}, bf16[128,1536]{1,0:T(8,128)(2,1)}, bf16[4608,1024]{1,0:T(8,128)(2,1)}, f32[4,1536]{1,0:T(4,128)}, f32[1,1536]{1,0:T(1,128)}) custom-call(bf16[8,576,1024]{2,1,0:T(8,128)(2,1)} %bitcast.70.held_ref, f32[128,1536]{1,0:T(8,128)} %get-tuple-element.248.middle_ref, ...), custom_call_target="tpu_custom_call" | custom-call | tf_op jit(solution)/shard_map/pallas_call | solution.py:997
  358.9 3.9 dynamic-slice_bitcast_fusion
  366.9 6.4 %collective-permute-done.55 = bf16[64,1536]{1,0:T(8,128)(2,1)S(1)} collective-permute-done((bf16[64,1536]{1,0:T(8,128)(2,1)S(1)}, bf16[64,1536]{1,0:T(8,128)(2,1)S(1)}, u32[]{:S(2)}, u32[]{:S(2)}) %collective-permute-start.55) | collective-permute-done | bytes 196640 | tf_op jit(solution)/shard_map/ppermute | solution.py:515
  375.0 2.8 shard_map.294
  377.8 14.0 %collective-permute-done.53 = bf16[576,1024]{1,0:T(8,128)(2,1)S(1)} collective-permute-done((bf16[576,1024]{1,0:T(8,128)(2,1)S(1)}, bf16[576,1024]{1,0:T(8,128)(2,1)S(1)}, u32[]{:S(2)}, u32[]{:S(2)}) %collective-permute-start.53) | collective-permute-done | bytes 1179680 | tf_op jit(solution)/shard_map/ppermute | solution.py:291
  393.2 2.7 fusion.1
  398.8 12.1 %shard_map.295 = (bf16[128,1536]{1,0:T(8,128)(2,1)}, bf16[640,384]{1,0:T(8,128)(2,1)}, f32[4,384]{1,0:T(4,128)}) custom-call(bf16[8,800,384]{2,1,0:T(8,128)(2,1)} %bitcast.61.held_ref, bf16[128,384]{1,0:T(8,128)(2,1)} %copy-done.35, bf16[128,384]{1,0:T(8,128)(2,1)} %copy-done.25, bf16[128,384]{1,0:T(8,128)(2,1)} %copy-done.26, bf16[128,384]{1,0:T(8,128)(2,1)} %copy-done.27, ...), custom_call_target="tpu_custom_call" | custom-call | tf_op jit(solution)/shard_map/pallas_call | solution.py:1121
  411.0 5.9 collective-permute-done.60
  419.1 3.6 collective-permute-done.61
  430.9 2.8 fusion.3
  436.6 14.4 %collective-permute-done.71 = bf16[128,384]{1,0:T(8,128)(2,1)S(1)} collective-permute-done((bf16[128,384]{1,0:T(8,128)(2,1)S(1)}, bf16[128,384]{1,0:T(8,128)(2,1)S(1)}, u32[]{:S(2)}, u32[]{:S(2)}) %collective-permute-start.71) | collective-permute-done | bytes 98336 | tf_op jit(solution)/shard_map/ppermute | solution.py:291
  454.4 3.8 collective-permute-done.75
  461.3 3.7 collective-permute-done.73
  467.2 9.7 %collective-permute-done.65 = bf16[576,1024]{1,0:T(8,128)(2,1)S(1)} collective-permute-done((bf16[576,1024]{1,0:T(8,128)(2,1)S(1)}, bf16[576,1024]{1,0:T(8,128)(2,1)S(1)}, u32[]{:S(2)}, u32[]{:S(2)}) %collective-permute-start.65) | collective-permute-done | bytes 1179680 | tf_op jit(solution)/shard_map/ppermute | solution.py:294
  484.4 7.4 %collective-permute-done.78 = bf16[576,1024]{1,0:T(8,128)(2,1)S(1)} collective-permute-done((bf16[576,1024]{1,0:T(8,128)(2,1)S(1)}, bf16[576,1024]{1,0:T(8,128)(2,1)S(1)}, u32[]{:S(2)}, u32[]{:S(2)}) %collective-permute-start.78) | collective-permute-done | bytes 1179680 | tf_op jit(solution)/shard_map/ppermute | solution.py:291
  497.4 4.0 collective-permute-done.81
  501.4 14.1 %collective-permute-done.79 = bf16[640,384]{1,0:T(8,128)(2,1)} collective-permute-done((bf16[640,384]{1,0:T(8,128)(2,1)S(1)}, bf16[640,384]{1,0:T(8,128)(2,1)}, u32[]{:S(2)}, u32[]{:S(2)}) %collective-permute-start.79) | collective-permute-done | bytes 491552 | tf_op jit(solution)/shard_map/ppermute | solution.py:294
  519.2 2.7 fusion.x_ref
  521.9 3.6 collective-permute-done.88
  530.6 3.5 collective-permute-start.90
  535.0 2.5 collective-permute-done.90
  540.3 9.5 %shard_map.298 = (f32[1,589824]{1,0:T(1,128)}, f32[1,589824]{1,0:T(1,128)}, f32[1,589824]{1,0:T(1,128)}, f32[1,589824]{1,0:T(1,128)}, bf16[1,589824]{1,0:T(2,128)(2,1)}) custom-call(f32[2]{0:T(128)S(1)} %pad_maximum_fusion.22.fix_ref, f32[1,589824]{1,0:T(1,128)S(1)} %copy-done.8, f32[1,589824]{1,0:T(1,128)S(1)} %copy-done.18, f32[1,589824]{1,0:T(1,128)} %v_ref.2, ...), custom_call_target="tpu_custom_call" | custom-call | tf_op jit(solution)/shard_map/pallas_call | solution.py:271
  557.0 21.4 %shard_map.299.x_ref = f32[2432,384]{1,0:T(8,128)} custom-call(s32[2]{0:T(128)} %pad_add_fusion.1.first_ref, bf16[4,8,128,1024]{3,2,1,0:T(8,128)(2,1)} %copy-done.37, bf16[8,256,384]{2,1,0:T(8,128)(2,1)} %bitcast.292, bf16[8,640,384]{2,1,0:T(8,128)(2,1)} %bitcast.144.a_ref, bf16[8,48,384]{2,1,0:T(8,128)(2,1)} %copy-done.46, bf16[8,16,4096]{2,1,0:T(8,128)(2,1)} %copy-done.6, ...), custom_call_target="tpu_custom_call" | custom-call | tf_op jit(solution)/shard_map/pallas_call | solution.py:1236
  578.3 4.8 shard_map.300.g_ref
  585.0 14.5 %shard_map.301 = (f32[1,884928]{1,0:T(1,128)}, f32[1,884928]{1,0:T(1,128)}, f32[1,884928]{1,0:T(1,128)}, f32[1,884928]{1,0:T(1,128)}, bf16[1,884928]{1,0:T(2,128)(2,1)}) custom-call(f32[2]{0:T(128)S(1)} %pad_maximum_fusion.22.fix_ref, f32[1,884928]{1,0:T(1,128)S(1)} %copy-done.4, f32[1,884928]{1,0:T(1,128)} %m_ref.3, f32[1,884928]{1,0:T(1,128)} %v_ref.3, ...), custom_call_target="tpu_custom_call" | custom-call | tf_op jit(solution)/shard_map/pallas_call | solution.py:271
  (506 shorter events, 173.2 us)
Async XLA Ops:
  1.6 10.7 %collective-permute-start = (bf16[16,128]{1,0:T(8,128)(2,1)S(1)}, bf16[16,128]{1,0:T(8,128)(2,1)S(1)}, u32[]{:S(2)}, u32[]{:S(2)}) collective-permute-start(bf16[16,128]{1,0:T(8,128)(2,1)S(1)} %bitcast.309), channel_id=1, source_target_pairs={{0,4},{4,8},{8,12},{12,16},{16,20},{20,24},{24,28},{1,5},{5,9},{9,... | collective-permute-start | bytes 12296 | tf_op jit(solution)/shard_map/ppermute | solution.py:145
  19.6 60.6 %collective-permute-start.1 = (bf16[768,384]{1,0:T(8,128)(2,1)S(1)}, bf16[768,384]{1,0:T(8,128)(2,1)S(1)}, u32[]{:S(2)}, u32[]{:S(2)}) collective-permute-start(bf16[768,384]{1,0:T(8,128)(2,1)S(1)} %get-tuple-element.362), channel_id=1, source_target_pairs={{0,24},{4,28},{8,12},{1,25},{5,29},{9,13},{2,26},{6,30},{10,14},{3... | collective-permute-start | bytes 1769480 | tf_op jit(solution)/shard_map/ppermute | solution.py:105
  22.2 58.0 %collective-permute-start.2 = (bf16[768,384]{1,0:T(8,128)(2,1)S(1)}, bf16[768,384]{1,0:T(8,128)(2,1)S(1)}, u32[]{:S(2)}, u32[]{:S(2)}) collective-permute-start(bf16[768,384]{1,0:T(8,128)(2,1)S(1)} %get-tuple-element.361), channel_id=1, source_target_pairs={{0,16},{4,20},{1,17},{5,21},{2,18},{6,22},{3,19},{7,23}} | collective-permute-start | bytes 1769480 | tf_op jit(solution)/shard_map/ppermute | solution.py:105
  26.4 29.6 %collective-permute-start.5 = (bf16[144,1024]{1,0:T(8,128)(2,1)S(1)}, bf16[144,1024]{1,0:T(8,128)(2,1)S(1)}, u32[]{:S(2)}, u32[]{:S(2)}) collective-permute-start(bf16[144,1024]{1,0:T(8,128)(2,1)S(1)} %collective-permute-done.3), channel_id=1, source_target_pairs={{0,8},{4,12},{8,16},{12,20},{16,24},{20,28},{24,0},{28,4},{1,9},{5... | collective-permute-start | bytes 884744 | tf_op jit(solution)/shard_map/ppermute | solution.py:294
  51.7 11.1 %collective-permute-start.6 = (bf16[2,128,1024]{2,1,0:T(8,128)(2,1)S(1)}, bf16[2,128,1024]{2,1,0:T(8,128)(2,1)S(1)}, u32[]{:S(2)}, u32[]{:S(2)}) collective-permute-start(bf16[2,128,1024]{2,1,0:T(8,128)(2,1)S(1)} %pad_maximum_fusion.2), channel_id=1, source_target_pairs={{0,2},{1,3},{2,0},{3,1},{4,6},{5,7},{6,4},{7,5},{8,10},{9,11},{10,... | collective-permute-start | bytes 1572872 | tf_op jit(solution)/shard_map/ppermute | solution.py:369
  62.9 11.9 %collective-permute-start.9 = (bf16[2,128,1024]{2,1,0:T(8,128)(2,1)S(1)}, bf16[2,128,1024]{2,1,0:T(8,128)(2,1)S(1)}, u32[]{:S(2)}, u32[]{:S(2)}) collective-permute-start(bf16[2,128,1024]{2,1,0:T(8,128)(2,1)S(1)} %pad_maximum_fusion.3), channel_id=1, source_target_pairs={{0,2},{1,3},{2,0},{3,1},{4,6},{5,7},{6,4},{7,5},{8,10},{9,11},{10,... | collective-permute-start | bytes 1572872 | tf_op jit(solution)/shard_map/ppermute | solution.py:369
  88.7 24.8 %collective-permute-start.13 = (bf16[800,384]{1,0:T(8,128)(2,1)}, bf16[800,384]{1,0:T(8,128)(2,1)}, u32[]{:S(2)}, u32[]{:S(2)}) collective-permute-start(bf16[800,384]{1,0:T(8,128)(2,1)} %pad_maximum_fusion.1), channel_id=1, source_target_pairs={{0,8},{4,12},{8,16},{12,20},{16,24},{20,28},{24,0},{28,4},{1,9},{5... | collective-permute-start | bytes 1843208 | tf_op jit(solution)/shard_map/ppermute | solution.py:294
  88.7 26.9 %collective-permute-start.14 = (bf16[800,384]{1,0:T(8,128)(2,1)}, bf16[800,384]{1,0:T(8,128)(2,1)}, u32[]{:S(2)}, u32[]{:S(2)}) collective-permute-start(bf16[800,384]{1,0:T(8,128)(2,1)} %pad_maximum_fusion.1), channel_id=1, source_target_pairs={{0,4},{4,0},{8,12},{12,8},{16,20},{20,16},{24,28},{28,24},{1,5},{5... | collective-permute-start | bytes 1843208 | tf_op jit(solution)/shard_map/ppermute | solution.py:291
  92.4 23.3 %collective-permute-start.17 = (bf16[8,128,1024]{2,1,0:T(8,128)(2,1)}, bf16[8,128,1024]{2,1,0:T(8,128)(2,1)}, u32[]{:S(2)}, u32[]{:S(2)}) collective-permute-start(bf16[8,128,1024]{2,1,0:T(8,128)(2,1)} %slice.260), channel_id=1, source_target_pairs={{0,1},{1,0},{2,3},{3,2},{4,5},{5,4},{6,7},{7,6},{8,9},{9,8},{10,11... | collective-permute-start | bytes 6291464 | tf_op jit(solution)/shard_map/ppermute | solution.py:458
  101.5 14.1 %collective-permute-start.16 = (bf16[8,128,1024]{2,1,0:T(8,128)(2,1)}, bf16[8,128,1024]{2,1,0:T(8,128)(2,1)}, u32[]{:S(2)}, u32[]{:S(2)}) collective-permute-start(bf16[8,128,1024]{2,1,0:T(8,128)(2,1)} %bitcast.23), channel_id=1, source_target_pairs={{0,1},{1,0},{2,3},{3,2},{4,5},{5,4},{6,7},{7,6},{8,9},{9,8},{10,11... | collective-permute-start | bytes 6291464 | tf_op jit(solution)/shard_map/ppermute | solution.py:458
  107.4 60.1 %collective-permute-start.20 = (bf16[576,1024]{1,0:T(8,128)(2,1)}, bf16[576,1024]{1,0:T(8,128)(2,1)}, u32[]{:S(2)}, u32[]{:S(2)}) collective-permute-start(bf16[576,1024]{1,0:T(8,128)(2,1)} %shard_map.287), channel_id=1, source_target_pairs={{0,8},{4,12},{8,16},{12,20},{16,24},{20,28},{24,0},{28,4},{1,9},{5... | collective-permute-start | bytes 3538952 | tf_op jit(solution)/shard_map/ppermute | solution.py:294
  113.5 55.6 %collective-permute-start.21 = (bf16[576,1024]{1,0:T(8,128)(2,1)}, bf16[576,1024]{1,0:T(8,128)(2,1)}, u32[]{:S(2)}, u32[]{:S(2)}) collective-permute-start(bf16[576,1024]{1,0:T(8,128)(2,1)} %shard_map.287), channel_id=1, source_target_pairs={{0,4},{4,0},{8,12},{12,8},{16,20},{20,16},{24,28},{28,24},{1,5},{5... | collective-permute-start | bytes 3538952 | tf_op jit(solution)/shard_map/ppermute | solution.py:291
  115.6 53.5 %collective-permute-start.18 = (bf16[800,384]{1,0:T(8,128)(2,1)}, bf16[800,384]{1,0:T(8,128)(2,1)}, u32[]{:S(2)}, u32[]{:S(2)}) collective-permute-start(bf16[800,384]{1,0:T(8,128)(2,1)} %collective-permute-done.13), channel_id=1, source_target_pairs={{0,8},{4,12},{8,16},{12,20},{16,24},{20,28},{24,0},{28,4},{1,9},{5... | collective-permute-start | bytes 1843208 | tf_op jit(solution)/shard_map/ppermute | solution.py:294
  125.7 43.4 %collective-permute-start.19 = (bf16[800,384]{1,0:T(8,128)(2,1)}, bf16[800,384]{1,0:T(8,128)(2,1)}, u32[]{:S(2)}, u32[]{:S(2)}) collective-permute-start(bf16[800,384]{1,0:T(8,128)(2,1)} %collective-permute-done.13), channel_id=1, source_target_pairs={{0,4},{4,0},{8,12},{12,8},{16,20},{20,16},{24,28},{28,24},{1,5},{5... | collective-permute-start | bytes 1843208 | tf_op jit(solution)/shard_map/ppermute | solution.py:291
  139.4 29.7 %collective-permute-start.22 = (bf16[128,768]{1,0:T(8,128)(2,1)S(1)}, bf16[128,768]{1,0:T(8,128)(2,1)S(1)}, u32[]{:S(2)}, u32[]{:S(2)}) collective-permute-start(bf16[128,768]{1,0:T(8,128)(2,1)S(1)} %get-tuple-element.366), channel_id=1, source_target_pairs={{0,4},{4,0},{8,12},{12,8},{16,20},{20,16},{24,28},{28,24},{1,5},{5... | collective-permute-start | bytes 589832 | tf_op jit(solution)/shard_map/ppermute | solution.py:291
  145.7 16.4 %all-to-all-start = ((f32[8,16,384]{2,1,0:T(8,128)}), f32[8,16,384]{2,1,0:T(8,128)S(1)}, u32[]{:S(2)}, u32[]{:S(2)}) async-start(f32[8,16,384]{2,1,0:T(8,128)} %bitcast.284), calls=%async_computation | async-start | bytes 393216 | tf_op jit(solution)/shard_map/all_to_all | solution.py:1367
  167.5 28.3 %collective-permute-start.28 = (bf16[128,768]{1,0:T(8,128)(2,1)S(1)}, bf16[128,768]{1,0:T(8,128)(2,1)S(1)}, u32[]{:S(2)}, u32[]{:S(2)}) collective-permute-start(bf16[128,768]{1,0:T(8,128)(2,1)S(1)} %get-tuple-element.365), channel_id=1, source_target_pairs={{0,4},{4,0},{8,12},{12,8},{16,20},{20,16},{24,28},{28,24},{1,5},{5... | collective-permute-start | bytes 589832 | tf_op jit(solution)/shard_map/ppermute | solution.py:291
  169.1 53.1 %collective-permute-start.23 = (bf16[800,384]{1,0:T(8,128)(2,1)}, bf16[800,384]{1,0:T(8,128)(2,1)S(1)}, u32[]{:S(2)}, u32[]{:S(2)}) collective-permute-start(bf16[800,384]{1,0:T(8,128)(2,1)} %collective-permute-done.18), channel_id=1, source_target_pairs={{0,8},{4,12},{8,16},{12,20},{16,24},{20,28},{24,0},{28,4},{1,9},{5... | collective-permute-start | bytes 1843208 | tf_op jit(solution)/shard_map/ppermute | solution.py:294
  178.9 43.4 %collective-permute-start.24 = (bf16[800,384]{1,0:T(8,128)(2,1)}, bf16[800,384]{1,0:T(8,128)(2,1)S(1)}, u32[]{:S(2)}, u32[]{:S(2)}) collective-permute-start(bf16[800,384]{1,0:T(8,128)(2,1)} %collective-permute-done.18), channel_id=1, source_target_pairs={{0,4},{4,0},{8,12},{12,8},{16,20},{20,16},{24,28},{28,24},{1,5},{5... | collective-permute-start | bytes 1843208 | tf_op jit(solution)/shard_map/ppermute | solution.py:291
  179.2 43.1 %collective-permute-start.25 = (bf16[576,1024]{1,0:T(8,128)(2,1)}, bf16[576,1024]{1,0:T(8,128)(2,1)S(1)}, u32[]{:S(2)}, u32[]{:S(2)}) collective-permute-start(bf16[576,1024]{1,0:T(8,128)(2,1)} %collective-permute-done.20), channel_id=1, source_target_pairs={{0,8},{4,12},{8,16},{12,20},{16,24},{20,28},{24,0},{28,4},{1,9},{5... | collective-permute-start | bytes 3538952 | tf_op jit(solution)/shard_map/ppermute | solution.py:294
  182.5 39.7 %collective-permute-start.26 = (bf16[576,1024]{1,0:T(8,128)(2,1)}, bf16[576,1024]{1,0:T(8,128)(2,1)S(1)}, u32[]{:S(2)}, u32[]{:S(2)}) collective-permute-start(bf16[576,1024]{1,0:T(8,128)(2,1)} %collective-permute-done.20), channel_id=1, source_target_pairs={{0,4},{4,0},{8,12},{12,8},{16,20},{20,16},{24,28},{28,24},{1,5},{5... | collective-permute-start | bytes 3538952 | tf_op jit(solution)/shard_map/ppermute | solution.py:291
  195.8 26.1 %collective-permute-start.27 = (bf16[128,768]{1,0:T(8,128)(2,1)S(1)}, bf16[128,768]{1,0:T(8,128)(2,1)S(1)}, u32[]{:S(2)}, u32[]{:S(2)}) collective-permute-start(bf16[128,768]{1,0:T(8,128)(2,1)S(1)} %fusion.13), channel_id=1, source_target_pairs={{0,8},{4,12},{8,16},{12,20},{16,24},{20,28},{24,0},{28,4},{1,9},{5... | collective-permute-start | bytes 589832 | tf_op jit(solution)/shard_map/ppermute | solution.py:294
  221.9 12.9 %collective-permute-start.33 = (bf16[128,768]{1,0:T(8,128)(2,1)S(1)}, bf16[128,768]{1,0:T(8,128)(2,1)S(1)}, u32[]{:S(2)}, u32[]{:S(2)}) collective-permute-start(bf16[128,768]{1,0:T(8,128)(2,1)S(1)} %get-tuple-element.364), channel_id=1, source_target_pairs={{0,4},{4,0},{8,12},{12,8},{16,20},{20,16},{24,28},{28,24},{1,5},{5... | collective-permute-start | bytes 589832 | tf_op jit(solution)/shard_map/ppermute | solution.py:291
  222.3 48.4 %collective-permute-start.30 = (bf16[576,1024]{1,0:T(8,128)(2,1)S(1)}, bf16[576,1024]{1,0:T(8,128)(2,1)}, u32[]{:S(2)}, u32[]{:S(2)}) collective-permute-start(bf16[576,1024]{1,0:T(8,128)(2,1)S(1)} %collective-permute-done.25), channel_id=1, source_target_pairs={{0,8},{4,12},{8,16},{12,20},{16,24},{20,28},{24,0},{28,4},{1,9},{5... | collective-permute-start | bytes 3538952 | tf_op jit(solution)/shard_map/ppermute | solution.py:294
  225.7 44.9 %collective-permute-start.31 = (bf16[576,1024]{1,0:T(8,128)(2,1)S(1)}, bf16[576,1024]{1,0:T(8,128)(2,1)S(1)}, u32[]{:S(2)}, u32[]{:S(2)}) collective-permute-start(bf16[576,1024]{1,0:T(8,128)(2,1)S(1)} %collective-permute-done.25), channel_id=1, source_target_pairs={{0,4},{4,0},{8,12},{12,8},{16,20},{20,16},{24,28},{28,24},{1,5},{5... | collective-permute-start | bytes 3538952 | tf_op jit(solution)/shard_map/ppermute | solution.py:291
  227.4 43.2 %collective-permute-start.29 = (bf16[800,384]{1,0:T(8,128)(2,1)S(1)}, bf16[800,384]{1,0:T(8,128)(2,1)S(1)}, u32[]{:S(2)}, u32[]{:S(2)}) collective-permute-start(bf16[800,384]{1,0:T(8,128)(2,1)S(1)} %collective-permute-done.23), channel_id=1, source_target_pairs={{0,4},{4,0},{8,12},{12,8},{16,20},{20,16},{24,28},{28,24},{1,5},{5... | collective-permute-start | bytes 1843208 | tf_op jit(solution)/shard_map/ppermute | solution.py:291
  227.8 29.2 %collective-permute-start.32 = (bf16[128,768]{1,0:T(8,128)(2,1)S(1)}, bf16[128,768]{1,0:T(8,128)(2,1)S(1)}, u32[]{:S(2)}, u32[]{:S(2)}) collective-permute-start(bf16[128,768]{1,0:T(8,128)(2,1)S(1)} %fusion.10), channel_id=1, source_target_pairs={{0,8},{4,12},{8,16},{12,20},{16,24},{20,28},{24,0},{28,4},{1,9},{5... | collective-permute-start | bytes 589832 | tf_op jit(solution)/shard_map/ppermute | solution.py:294
  234.8 35.8 %collective-permute-start.35 = (bf16[128,768]{1,0:T(8,128)(2,1)S(1)}, bf16[128,768]{1,0:T(8,128)(2,1)S(1)}, u32[]{:S(2)}, u32[]{:S(2)}) collective-permute-start(bf16[128,768]{1,0:T(8,128)(2,1)S(1)} %get-tuple-element.363), channel_id=1, source_target_pairs={{0,4},{4,0},{8,12},{12,8},{16,20},{20,16},{24,28},{28,24},{1,5},{5... | collective-permute-start | bytes 589832 | tf_op jit(solution)/shard_map/ppermute | solution.py:291
  257.1 13.6 %collective-permute-start.34 = (bf16[128,768]{1,0:T(8,128)(2,1)S(1)}, bf16[128,768]{1,0:T(8,128)(2,1)S(1)}, u32[]{:S(2)}, u32[]{:S(2)}) collective-permute-start(bf16[128,768]{1,0:T(8,128)(2,1)S(1)} %fusion.12), channel_id=1, source_target_pairs={{0,8},{4,12},{8,16},{12,20},{16,24},{20,28},{24,0},{28,4},{1,9},{5... | collective-permute-start | bytes 589832 | tf_op jit(solution)/shard_map/ppermute | solution.py:294
  275.5 27.0 %collective-permute-start.36 = (bf16[576,1024]{1,0:T(8,128)(2,1)}, bf16[576,1024]{1,0:T(8,128)(2,1)}, u32[]{:S(2)}, u32[]{:S(2)}) collective-permute-start(bf16[576,1024]{1,0:T(8,128)(2,1)} %collective-permute-done.30), channel_id=1, source_target_pairs={{0,4},{4,0},{8,12},{12,8},{16,20},{20,16},{24,28},{28,24},{1,5},{5... | collective-permute-start | bytes 3538952 | tf_op jit(solution)/shard_map/ppermute | solution.py:291
  307.3 12.8 %collective-permute-start.40 = (bf16[256,384]{1,0:T(8,128)(2,1)S(1)}, bf16[256,384]{1,0:T(8,128)(2,1)S(1)}, u32[]{:S(2)}, u32[]{:S(2)}) collective-permute-start(bf16[256,384]{1,0:T(8,128)(2,1)S(1)} %pad_maximum_fusion.11), channel_id=1, source_target_pairs={{0,8},{4,12},{8,16},{12,20},{16,24},{20,28},{24,0},{28,4},{1,9},{5... | collective-permute-start | bytes 589832 | tf_op jit(solution)/shard_map/ppermute | solution.py:294
  320.1 16.8 %collective-permute-start.42 = (bf16[256,384]{1,0:T(8,128)(2,1)S(1)}, bf16[256,384]{1,0:T(8,128)(2,1)S(1)}, u32[]{:S(2)}, u32[]{:S(2)}) collective-permute-start(bf16[256,384]{1,0:T(8,128)(2,1)S(1)} %collective-permute-done.40), channel_id=1, source_target_pairs={{0,8},{4,12},{8,16},{12,20},{16,24},{20,28},{24,0},{28,4},{1,9},{5... | collective-permute-start | bytes 589832 | tf_op jit(solution)/shard_map/ppermute | solution.py:294
  322.6 14.3 %collective-permute-start.44 = (bf16[256,384]{1,0:T(8,128)(2,1)S(1)}, bf16[256,384]{1,0:T(8,128)(2,1)S(1)}, u32[]{:S(2)}, u32[]{:S(2)}) collective-permute-start(bf16[256,384]{1,0:T(8,128)(2,1)S(1)} %collective-permute-done.40), channel_id=1, source_target_pairs={{0,4},{4,0},{8,12},{12,8},{16,20},{20,16},{24,28},{28,24},{1,5},{5... | collective-permute-start | bytes 589832 | tf_op jit(solution)/shard_map/ppermute | solution.py:291
  323.3 13.6 %collective-permute-start.43 = (bf16[2,128,384]{2,1,0:T(8,128)(2,1)S(1)}, bf16[2,128,384]{2,1,0:T(8,128)(2,1)S(1)}, u32[]{:S(2)}, u32[]{:S(2)}) collective-permute-start(bf16[2,128,384]{2,1,0:T(8,128)(2,1)S(1)} %pad_maximum_fusion.12), channel_id=1, source_target_pairs={{0,2},{1,3},{2,0},{3,1},{4,6},{5,7},{6,4},{7,5},{8,10},{9,11},{10,... | collective-permute-start | bytes 589832 | tf_op jit(solution)/shard_map/ppermute | solution.py:369
  336.9 19.4 %collective-permute-start.48 = (bf16[256,384]{1,0:T(8,128)(2,1)S(1)}, bf16[256,384]{1,0:T(8,128)(2,1)}, u32[]{:S(2)}, u32[]{:S(2)}) collective-permute-start(bf16[256,384]{1,0:T(8,128)(2,1)S(1)} %collective-permute-done.42), channel_id=1, source_target_pairs={{0,8},{4,12},{8,16},{12,20},{16,24},{20,28},{24,0},{28,4},{1,9},{5... | collective-permute-start | bytes 589832 | tf_op jit(solution)/shard_map/ppermute | solution.py:294
  339.7 16.6 %collective-permute-start.50 = (bf16[256,384]{1,0:T(8,128)(2,1)S(1)}, bf16[256,384]{1,0:T(8,128)(2,1)S(1)}, u32[]{:S(2)}, u32[]{:S(2)}) collective-permute-start(bf16[256,384]{1,0:T(8,128)(2,1)S(1)} %collective-permute-done.42), channel_id=1, source_target_pairs={{0,4},{4,0},{8,12},{12,8},{16,20},{20,16},{24,28},{28,24},{1,5},{5... | collective-permute-start | bytes 589832 | tf_op jit(solution)/shard_map/ppermute | solution.py:291
  340.8 15.4 %collective-permute-start.49 = (bf16[2,128,384]{2,1,0:T(8,128)(2,1)S(1)}, bf16[2,128,384]{2,1,0:T(8,128)(2,1)S(1)}, u32[]{:S(2)}, u32[]{:S(2)}) collective-permute-start(bf16[2,128,384]{2,1,0:T(8,128)(2,1)S(1)} %pad_maximum_fusion.13), channel_id=1, source_target_pairs={{0,2},{1,3},{2,0},{3,1},{4,6},{5,7},{6,4},{7,5},{8,10},{9,11},{10,... | collective-permute-start | bytes 589832 | tf_op jit(solution)/shard_map/ppermute | solution.py:369
  356.4 21.5 %collective-permute-start.51 = (bf16[2,128,384]{2,1,0:T(8,128)(2,1)S(1)}, bf16[2,128,384]{2,1,0:T(8,128)(2,1)S(1)}, u32[]{:S(2)}, u32[]{:S(2)}) collective-permute-start(bf16[2,128,384]{2,1,0:T(8,128)(2,1)S(1)} %pad_maximum_fusion.14), channel_id=1, source_target_pairs={{0,2},{1,3},{2,0},{3,1},{4,6},{5,7},{6,4},{7,5},{8,10},{9,11},{10,... | collective-permute-start | bytes 589832 | tf_op jit(solution)/shard_map/ppermute | solution.py:369
  357.9 19.9 %collective-permute-start.52 = (bf16[256,384]{1,0:T(8,128)(2,1)}, bf16[256,384]{1,0:T(8,128)(2,1)S(1)}, u32[]{:S(2)}, u32[]{:S(2)}) collective-permute-start(bf16[256,384]{1,0:T(8,128)(2,1)} %collective-permute-done.48), channel_id=1, source_target_pairs={{0,4},{4,0},{8,12},{12,8},{16,20},{20,16},{24,28},{28,24},{1,5},{5... | collective-permute-start | bytes 589832 | tf_op jit(solution)/shard_map/ppermute | solution.py:291
  362.9 29.0 %collective-permute-start.53 = (bf16[576,1024]{1,0:T(8,128)(2,1)S(1)}, bf16[576,1024]{1,0:T(8,128)(2,1)S(1)}, u32[]{:S(2)}, u32[]{:S(2)}) collective-permute-start(bf16[576,1024]{1,0:T(8,128)(2,1)S(1)} %get-tuple-element.358), channel_id=1, source_target_pairs={{0,4},{4,0},{8,12},{12,8},{16,20},{20,16},{24,28},{28,24},{1,5},{5... | collective-permute-start | bytes 3538952 | tf_op jit(solution)/shard_map/ppermute | solution.py:291
  364.1 54.0 %collective-permute-start.58 = (bf16[576,1024]{1,0:T(8,128)(2,1)}, bf16[576,1024]{1,0:T(8,128)(2,1)}, u32[]{:S(2)}, u32[]{:S(2)}) collective-permute-start(bf16[576,1024]{1,0:T(8,128)(2,1)} %get-tuple-element.357), channel_id=1, source_target_pairs={{0,4},{4,0},{8,12},{12,8},{16,20},{20,16},{24,28},{28,24},{1,5},{5... | collective-permute-start | bytes 3538952 | tf_op jit(solution)/shard_map/ppermute | solution.py:291
  391.8 19.2 %collective-permute-start.59 = (bf16[128,384]{1,0:T(8,128)(2,1)S(1)}, bf16[128,384]{1,0:T(8,128)(2,1)S(1)}, u32[]{:S(2)}, u32[]{:S(2)}) collective-permute-start(bf16[128,384]{1,0:T(8,128)(2,1)S(1)} %constant_dynamic-slice_fusion), channel_id=1, source_target_pairs={{0,8},{4,12},{8,16},{12,20},{16,24},{20,28},{24,0},{28,4},{1,9},{5... | collective-permute-start | bytes 294920 | tf_op jit(solution)/shard_map/ppermute | solution.py:294
  392.2 24.7 %collective-permute-start.60 = (bf16[128,384]{1,0:T(8,128)(2,1)S(1)}, bf16[128,384]{1,0:T(8,128)(2,1)S(1)}, u32[]{:S(2)}, u32[]{:S(2)}) collective-permute-start(bf16[128,384]{1,0:T(8,128)(2,1)S(1)} %constant_dynamic-slice_fusion), channel_id=1, source_target_pairs={{0,4},{4,0},{8,12},{12,8},{16,20},{20,16},{24,28},{28,24},{1,5},{5... | collective-permute-start | bytes 294920 | tf_op jit(solution)/shard_map/ppermute | solution.py:291
  396.0 27.8 %collective-permute-start.57 = (bf16[576,1024]{1,0:T(8,128)(2,1)}, bf16[576,1024]{1,0:T(8,128)(2,1)}, u32[]{:S(2)}, u32[]{:S(2)}) collective-permute-start(bf16[576,1024]{1,0:T(8,128)(2,1)} %fusion.1), channel_id=1, source_target_pairs={{0,8},{4,12},{8,16},{12,20},{16,24},{20,28},{24,0},{28,4},{1,9},{5... | collective-permute-start | bytes 3538952 | tf_op jit(solution)/shard_map/ppermute | solution.py:294
  396.8 27.0 %collective-permute-start.64 = (bf16[2,128,384]{2,1,0:T(8,128)(2,1)}, bf16[2,128,384]{2,1,0:T(8,128)(2,1)}, u32[]{:S(2)}, u32[]{:S(2)}) collective-permute-start(bf16[2,128,384]{2,1,0:T(8,128)(2,1)} %pad_maximum_fusion.16), channel_id=1, source_target_pairs={{0,2},{1,3},{2,0},{3,1},{4,6},{5,7},{6,4},{7,5},{8,10},{9,11},{10,... | collective-permute-start | bytes 589832 | tf_op jit(solution)/shard_map/ppermute | solution.py:369
  422.7 37.5 %collective-permute-start.66 = (bf16[576,1024]{1,0:T(8,128)(2,1)S(1)}, bf16[576,1024]{1,0:T(8,128)(2,1)S(1)}, u32[]{:S(2)}, u32[]{:S(2)}) collective-permute-start(bf16[576,1024]{1,0:T(8,128)(2,1)S(1)} %get-tuple-element.356), channel_id=1, source_target_pairs={{0,4},{4,0},{8,12},{12,8},{16,20},{20,16},{24,28},{28,24},{1,5},{5... | collective-permute-start | bytes 3538952 | tf_op jit(solution)/shard_map/ppermute | solution.py:291
  423.8 10.5 %collective-permute-start.69 = (bf16[128,384]{1,0:T(8,128)(2,1)S(1)}, bf16[128,384]{1,0:T(8,128)(2,1)S(1)}, u32[]{:S(2)}, u32[]{:S(2)}) collective-permute-start(bf16[128,384]{1,0:T(8,128)(2,1)S(1)} %collective-permute-done.61), channel_id=1, source_target_pairs={{0,8},{4,12},{8,16},{12,20},{16,24},{20,28},{24,0},{28,4},{1,9},{5... | collective-permute-start | bytes 294920 | tf_op jit(solution)/shard_map/ppermute | solution.py:294
  424.2 26.8 %collective-permute-start.71 = (bf16[128,384]{1,0:T(8,128)(2,1)S(1)}, bf16[128,384]{1,0:T(8,128)(2,1)S(1)}, u32[]{:S(2)}, u32[]{:S(2)}) collective-permute-start(bf16[128,384]{1,0:T(8,128)(2,1)S(1)} %collective-permute-done.61), channel_id=1, source_target_pairs={{0,4},{4,0},{8,12},{12,8},{16,20},{20,16},{24,28},{28,24},{1,5},{5... | collective-permute-start | bytes 294920 | tf_op jit(solution)/shard_map/ppermute | solution.py:291
  425.2 26.8 %collective-permute-start.70 = (bf16[2,128,384]{2,1,0:T(8,128)(2,1)S(1)}, bf16[2,128,384]{2,1,0:T(8,128)(2,1)S(1)}, u32[]{:S(2)}, u32[]{:S(2)}) collective-permute-start(bf16[2,128,384]{2,1,0:T(8,128)(2,1)S(1)} %pad_maximum_fusion.17), channel_id=1, source_target_pairs={{0,2},{1,3},{2,0},{3,1},{4,6},{5,7},{6,4},{7,5},{8,10},{9,11},{10,... | collective-permute-start | bytes 589832 | tf_op jit(solution)/shard_map/ppermute | solution.py:369
  426.5 25.8 %collective-permute-start.74 = (bf16[64,1536]{1,0:T(8,128)(2,1)S(1)}, bf16[64,1536]{1,0:T(8,128)(2,1)S(1)}, u32[]{:S(2)}, u32[]{:S(2)}) collective-permute-start(bf16[64,1536]{1,0:T(8,128)(2,1)S(1)} %broadcast_select_fusion.3), channel_id=1, source_target_pairs={{0,1},{1,0},{2,3},{3,2},{4,5},{5,4},{6,7},{7,6},{8,9},{9,8},{10,11... | collective-permute-start | bytes 589832 | tf_op jit(solution)/shard_map/ppermute | solution.py:510
  434.3 32.4 %collective-permute-start.67 = (bf16[640,384]{1,0:T(8,128)(2,1)S(1)}, bf16[640,384]{1,0:T(8,128)(2,1)S(1)}, u32[]{:S(2)}, u32[]{:S(2)}) collective-permute-start(bf16[640,384]{1,0:T(8,128)(2,1)S(1)} %copy-done.59), channel_id=1, source_target_pairs={{0,8},{4,12},{8,16},{12,20},{16,24},{20,28},{24,0},{28,4},{1,9},{5... | collective-permute-start | bytes 1474568 | tf_op jit(solution)/shard_map/ppermute | solution.py:294
  451.0 16.3 %collective-permute-start.68 = (bf16[640,384]{1,0:T(8,128)(2,1)S(1)}, bf16[640,384]{1,0:T(8,128)(2,1)S(1)}, u32[]{:S(2)}, u32[]{:S(2)}) collective-permute-start(bf16[640,384]{1,0:T(8,128)(2,1)S(1)} %copy-done.59), channel_id=1, source_target_pairs={{0,4},{4,0},{8,12},{12,8},{16,20},{20,16},{24,28},{28,24},{1,5},{5... | collective-permute-start | bytes 1474568 | tf_op jit(solution)/shard_map/ppermute | solution.py:291
  452.0 24.9 %collective-permute-start.65 = (bf16[576,1024]{1,0:T(8,128)(2,1)S(1)}, bf16[576,1024]{1,0:T(8,128)(2,1)S(1)}, u32[]{:S(2)}, u32[]{:S(2)}) collective-permute-start(bf16[576,1024]{1,0:T(8,128)(2,1)S(1)} %fusion.3), channel_id=1, source_target_pairs={{0,8},{4,12},{8,16},{12,20},{16,24},{20,28},{24,0},{28,4},{1,9},{5... | collective-permute-start | bytes 3538952 | tf_op jit(solution)/shard_map/ppermute | solution.py:294
  465.0 26.9 %collective-permute-start.78 = (bf16[576,1024]{1,0:T(8,128)(2,1)S(1)}, bf16[576,1024]{1,0:T(8,128)(2,1)S(1)}, u32[]{:S(2)}, u32[]{:S(2)}) collective-permute-start(bf16[576,1024]{1,0:T(8,128)(2,1)S(1)} %get-tuple-element.355), channel_id=1, source_target_pairs={{0,4},{4,0},{8,12},{12,8},{16,20},{20,16},{24,28},{28,24},{1,5},{5... | collective-permute-start | bytes 3538952 | tf_op jit(solution)/shard_map/ppermute | solution.py:291
  466.7 29.0 %collective-permute-start.83 = (bf16[8,128,384]{2,1,0:T(8,128)(2,1)S(1)}, bf16[8,128,384]{2,1,0:T(8,128)(2,1)S(1)}, u32[]{:S(2)}, u32[]{:S(2)}) collective-permute-start(bf16[8,128,384]{2,1,0:T(8,128)(2,1)S(1)} %slice.268.rest_0_), channel_id=1, source_target_pairs={{0,1},{1,0},{2,3},{3,2},{4,5},{5,4},{6,7},{7,6},{8,9},{9,8},{10,11... | collective-permute-start | bytes 2359304 | tf_op jit(solution)/shard_map/ppermute | solution.py:458
  466.7 30.6 %collective-permute-start.82 = (bf16[8,128,384]{2,1,0:T(8,128)(2,1)S(1)}, bf16[8,128,384]{2,1,0:T(8,128)(2,1)S(1)}, u32[]{:S(2)}, u32[]{:S(2)}) collective-permute-start(bf16[8,128,384]{2,1,0:T(8,128)(2,1)S(1)} %bitcast.300), channel_id=1, source_target_pairs={{0,1},{1,0},{2,3},{3,2},{4,5},{5,4},{6,7},{7,6},{8,9},{9,8},{10,11... | collective-permute-start | bytes 2359304 | tf_op jit(solution)/shard_map/ppermute | solution.py:458
  479.0 36.5 %collective-permute-start.77 = (bf16[576,1024]{1,0:T(8,128)(2,1)S(1)}, bf16[576,1024]{1,0:T(8,128)(2,1)S(1)}, u32[]{:S(2)}, u32[]{:S(2)}) collective-permute-start(bf16[576,1024]{1,0:T(8,128)(2,1)S(1)} %fusion.5), channel_id=1, source_target_pairs={{0,8},{4,12},{8,16},{12,20},{16,24},{20,28},{24,0},{28,4},{1,9},{5... | collective-permute-start | bytes 3538952 | tf_op jit(solution)/shard_map/ppermute | solution.py:294
  479.0 36.5 %collective-permute-start.79 = (bf16[640,384]{1,0:T(8,128)(2,1)S(1)}, bf16[640,384]{1,0:T(8,128)(2,1)}, u32[]{:S(2)}, u32[]{:S(2)}) collective-permute-start(bf16[640,384]{1,0:T(8,128)(2,1)S(1)} %collective-permute-done.67), channel_id=1, source_target_pairs={{0,8},{4,12},{8,16},{12,20},{16,24},{20,28},{24,0},{28,4},{1,9},{5... | collective-permute-start | bytes 1474568 | tf_op jit(solution)/shard_map/ppermute | solution.py:294
  491.9 23.6 %collective-permute-start.80 = (bf16[640,384]{1,0:T(8,128)(2,1)S(1)}, bf16[640,384]{1,0:T(8,128)(2,1)S(1)}, u32[]{:S(2)}, u32[]{:S(2)}) collective-permute-start(bf16[640,384]{1,0:T(8,128)(2,1)S(1)} %collective-permute-done.67), channel_id=1, source_target_pairs={{0,4},{4,0},{8,12},{12,8},{16,20},{20,16},{24,28},{28,24},{1,5},{5... | collective-permute-start | bytes 1474568 | tf_op jit(solution)/shard_map/ppermute | solution.py:291
  497.3 40.3 %collective-permute-start.87 = (bf16[8,128,384]{2,1,0:T(8,128)(2,1)S(1)}, bf16[8,128,384]{2,1,0:T(8,128)(2,1)}, u32[]{:S(2)}, u32[]{:S(2)}) collective-permute-start(bf16[8,128,384]{2,1,0:T(8,128)(2,1)S(1)} %bitcast.298), channel_id=1, source_target_pairs={{0,1},{1,0},{2,3},{3,2},{4,5},{5,4},{6,7},{7,6},{8,9},{9,8},{10,11... | collective-permute-start | bytes 2359304 | tf_op jit(solution)/shard_map/ppermute | solution.py:458
  515.5 22.1 %collective-permute-start.84 = (bf16[640,384]{1,0:T(8,128)(2,1)}, bf16[640,384]{1,0:T(8,128)(2,1)}, u32[]{:S(2)}, u32[]{:S(2)}) collective-permute-start(bf16[640,384]{1,0:T(8,128)(2,1)} %collective-permute-done.79), channel_id=1, source_target_pairs={{0,8},{4,12},{8,16},{12,20},{16,24},{20,28},{24,0},{28,4},{1,9},{5... | collective-permute-start | bytes 1474568 | tf_op jit(solution)/shard_map/ppermute | solution.py:294
  515.6 22.0 %collective-permute-start.85 = (bf16[640,384]{1,0:T(8,128)(2,1)}, bf16[640,384]{1,0:T(8,128)(2,1)}, u32[]{:S(2)}, u32[]{:S(2)}) collective-permute-start(bf16[640,384]{1,0:T(8,128)(2,1)} %collective-permute-done.79), channel_id=1, source_target_pairs={{0,4},{4,0},{8,12},{12,8},{16,20},{20,16},{24,28},{28,24},{1,5},{5... | collective-permute-start | bytes 1474568 | tf_op jit(solution)/shard_map/ppermute | solution.py:291
  517.3 20.3 %collective-permute-start.86 = (bf16[8,128,384]{2,1,0:T(8,128)(2,1)}, bf16[8,128,384]{2,1,0:T(8,128)(2,1)}, u32[]{:S(2)}, u32[]{:S(2)}) collective-permute-start(bf16[8,128,384]{2,1,0:T(8,128)(2,1)} %bitcast.127.rest_6_), channel_id=1, source_target_pairs={{0,1},{1,0},{2,3},{3,2},{4,5},{5,4},{6,7},{7,6},{8,9},{9,8},{10,11... | collective-permute-start | bytes 2359304 | tf_op jit(solution)/shard_map/ppermute | solution.py:458
  537.6 16.6 %collective-permute-start.91 = (bf16[640,384]{1,0:T(8,128)(2,1)}, bf16[640,384]{1,0:T(8,128)(2,1)S(1)}, u32[]{:S(2)}, u32[]{:S(2)}) collective-permute-start(bf16[640,384]{1,0:T(8,128)(2,1)} %collective-permute-done.84), channel_id=1, source_target_pairs={{0,4},{4,0},{8,12},{12,8},{16,20},{20,16},{24,28},{28,24},{1,5},{5... | collective-permute-start | bytes 1474568 | tf_op jit(solution)/shard_map/ppermute | solution.py:291
  (105 other events, 1550.0 us)
